TPU v7x, 32 devices: a whole 2x2x4 slice. The times are simulated.
32 devices in a mesh: space: 8 (over y, x, core), band: 4 (over z).
Axes of the slice: x: 2, y: 2, z: 4, core: 2. Of those that a mesh axis runs over, the one named last changes fastest.
Arguments:
- psi: float32 [64, 32928], P('band', 'space'), may hold values from -400 to 400
- ham: bfloat16 [96, 512, 512], P('space'), may hold values from -2 to 2, as said below
- conn: int32 [96, 512], P('space'), may hold values from 0 to 4703, as said below
- face_rows: int32 [4704], P('space'), may hold values from 0 to 4115, as said below
Outputs:
- ortho: float32 [64, 32928], P('band', 'space')
Inputs may be any that keep to these rules, and one draw needn't show every extreme that they name: `conn`: rows s * 12 to (s + 1) * 12 - 1 are the elements of domain s. Entries at element-local nodes below 448 name the domain's own rows 0 to 4115; entries at and above 448 name ghost slots 4116 + j, where ghost slot j is the node listed at position j of face_rows of domain (s + 1) mod 8. Every own row and every ghost slot of a domain is named by some element. `face_rows`: entries s * 588 to (s + 1) * 588 - 1 are 588 distinct own rows of domain s: the nodes of its lower face. `ham`: each matrix is symmetric.
All inputs are finite; a program needn't handle non-finite values.
Results may differ from a plain program's by a relative error of at most 0.0037.
Values may be sent and summed in bfloat16 or wider, within the bound.
No kernel may reach another device: no remote copies, remote signals or barrier semaphores. Data moves between devices by JAX's collectives and lax.ppermute only.
A program may use at most 64 MiB of HBM per device.

v0:
```python
import jax
import jax.numpy as jnp
from jax import lax
from jax.sharding import PartitionSpec as P

FACE_EL = 64
IN_EL = 448


CENTER = 6.25
HALF_WIDTH = 7.5


def from_behind(block, axis, distance):
    devices = range(lax.axis_size(axis))
    route = [((i - distance) % len(devices), i) for i in devices]
    return lax.ppermute(block, axis, route)


def per_device(psi, ham, conn, face_rows):
    band_count, node_count = psi.shape
    elem_count = conn.shape[0]
    face_count = face_rows.shape[0]
    conn_inside = conn[:, :IN_EL].reshape(-1)
    conn_upper = conn[:, IN_EL:].reshape(-1) - node_count
    ham_inner = ham[:, :IN_EL, :IN_EL]
    ham_cross = ham[:, :IN_EL, IN_EL:]
    ham_back = ham[:, IN_EL:, :IN_EL]
    ham_face = ham[:, IN_EL:, IN_EL:]

    def apply_operator(field):
        rounded = field.astype(jnp.bfloat16)
        face_values = jnp.take(rounded, face_rows, axis=1)
        ghost = from_behind(face_values, "space", -1)
        inside = jnp.take(rounded, conn_inside, axis=1).reshape(band_count, elem_count, IN_EL)
        interior = jnp.einsum("bem,eml->bel", inside, ham_inner, preferred_element_type=jnp.float32)
        outside = jnp.take(ghost, conn_upper, axis=1).reshape(band_count, elem_count, FACE_EL)
        upper = jnp.einsum("bem,eml->bel", inside, ham_cross, preferred_element_type=jnp.float32)
        upper = upper + jnp.einsum(
            "bem,eml->bel", outside, ham_face, preferred_element_type=jnp.float32
        )
        upper_sums = jnp.zeros((band_count, face_count), jnp.float32)
        upper_sums = upper_sums.at[:, conn_upper].add(
            upper.reshape(band_count, elem_count * FACE_EL)
        )
        remainder = interior + jnp.einsum(
            "bem,eml->bel", outside, ham_back, preferred_element_type=jnp.float32
        )
        owned = jnp.zeros((band_count, node_count), jnp.float32)
        owned = owned.at[:, conn_inside].add(remainder.reshape(band_count, elem_count * IN_EL))
        received = from_behind(upper_sums, "space", 1)
        return owned.at[:, face_rows].add(received)

    current = (apply_operator(psi) - CENTER * psi) / HALF_WIDTH
    scaled = (apply_operator(current) - CENTER * current) / HALF_WIDTH
    following = 2.0 * scaled - psi
    node_rows = lax.all_to_all(following, "band", split_axis=1, concat_axis=0, tiled=True)
    partial_value = lax.dot_general(
        node_rows,
        node_rows,
        (((1,), (1,)), ((), ())),
        precision=lax.Precision.HIGHEST,
        preferred_element_type=jnp.float32,
    )
    correlation = lax.psum(partial_value, ("space", "band"))
    correlation = correlation / (node_count * lax.axis_size("space"))
    factor = jnp.linalg.cholesky(correlation)
    orthonormal = jax.scipy.linalg.solve_triangular(factor, node_rows, lower=True)
    return lax.all_to_all(orthonormal, "band", split_axis=0, concat_axis=1, tiled=True)


def solution(mesh):
    placed = (P("band", "space"), P("space", None, None), P("space", None), P("space"))
    return jax.shard_map(
        per_device, mesh=mesh, in_specs=placed, out_specs=P("band", "space"), check_vma=False
    )
```

profile of v0, /device:TPU:0, one launch (start us, length us, event | category | flops | bytes accessed | tf_op | source)
XLA Modules:
  0.0 238.4 jit_solution(14704558910817277392)
XLA Ops:
  0.0 0.7 compare_and_fusion.2
  0.7 0.7 compare_select_fusion.4
  1.4 1.4 copy.76
  2.8 2.0 gather_fusion.1
  4.9 3.4 %collective-permute-start = (bf16[16,588]{0,1:T(8,128)(2,1)S(1)}, bf16[16,588]{0,1:T(8,128)(2,1)S(1)}, u32[]{:S(2)}, u32[]{:S(2)}) collective-permute-start(bf16[16,588]{0,1:T(8,128)(2,1)S(1)} %select_bitcast_fusion.1), channel_id=1, source_target_pairs={{4,0},{8,4},{12,8},{16,12},{20,16},{24,20},{28,24},{0,28},{5,1},{9... | collective-permute-start | bytes 56456 | tf_op jit(solution)/shard_map/ppermute | solution.py:17
  8.3 0.8 slice_add_fusion
  9.3 0.8 reshape.122
  10.1 0.8 reshape.123
  11.0 10.3 %gather_fusion = bf16[5376,16]{1,0:T(8,128)(2,1)S(1)} fusion(bf16[16,4116]{0,1:T(8,128)(2,1)S(1)} %copy.76, s32[6144]{0:T(1024)S(1)} %pad_clamp_fusion), kind=kCustom, calls=%fused_computation.clone | custom fusion | bytes 365568 | tf_op jit(solution)/shard_map/jit(_take)/gather | solution.py:35
  21.3 2.8 %broadcast_select_fusion = bf16[5376,16]{1,0:T(8,128)(2,1)S(1)} fusion(bf16[5376,16]{1,0:T(8,128)(2,1)S(1)} %gather_fusion, pred[5376]{0:T(1024)(128)(4,1)S(1)} %compare_and_fusion), kind=kLoop, calls=%fused_computation.16 | loop fusion | flops 86016 | bytes 349440 | tf_op jit(solution)/shard_map/jit(_take)/select_n | solution.py:35
  24.1 2.3 fusion.4
  26.3 3.4 %fusion.2 = f32[12,16,448]{2,1,0:T(8,128)S(1)} fusion(bf16[16,12,448]{0,2,1:T(8,128)(2,1)S(1)} %bitcast.63, bf16[12,512,512]{2,1,0:T(8,128)(2,1)} %param.11), kind=kOutput, calls=%fused_computation.14 | convolution fusion | flops 77070336 | bytes 6021120 | tf_op jit(solution)/shard_map/bem,eml->bel/dot_general | solution.py:36
  30.0 1.9 gather_fusion.2
  32.0 1.2 fusion.11
  33.6 6.1 %scatter_custom_fusion.1 = f32[16,588]{0,1:T(8,128)S(1)} fusion(s32[768]{0:T(1024)S(1)} %fusion.31, f32[768,16]{1,0:T(8,128)S(1)} %copy.85, f32[]{:T(128)} %constant.89.clone.1), kind=kCustom, calls=%fused_computation.51 | custom fusion | flops 12288 | bytes 37636 | tf_op jit(solution)/shard_map/scatter-add | solution.py:43
  39.7 1.4 fusion.9
  41.2 0.2 copy.79
  41.6 2.3 copy.80
  43.9 31.4 %scatter_custom_fusion = f32[16,4116]{0,1:T(8,128)S(1)} fusion(s32[5376]{0:T(1024)S(1)} %fusion.30, f32[5376,16]{1,0:T(8,128)} %copy.80, f32[]{:T(128)} %constant.89.clone.1), kind=kCustom, calls=%fused_computation.32 | custom fusion | flops 86016 | bytes 263936 | tf_op jit(solution)/shard_map/scatter-add | solution.py:50
  75.3 7.1 %scatter_custom_fusion.2 = f32[16,4116]{0,1:T(8,128)S(1)} fusion(f32[16,4116]{0,1:T(8,128)S(1)} %scatter_custom_fusion, s32[588]{0:T(1024)S(1)} %compare_select_fusion.4, f32[16,588]{0,1:T(8,128)S(1)} %collective-permute-done.1), kind=kCustom, calls=%fused_computation.38 | custom fusion | flops 9408 | bytes 566528 | tf_op jit(solution)/shard_map/scatter-add | solution.py:52
  82.4 0.6 copy.86
  83.1 0.5 copy.87
  83.6 2.0 gather_fusion.4
  85.6 10.3 %gather_fusion.3 = bf16[5376,16]{1,0:T(8,128)(2,1)S(1)} fusion(bf16[16,4116]{0,1:T(8,128)(2,1)S(1)} %copy.87, s32[6144]{0:T(1024)S(1)} %pad_clamp_fusion), kind=kCustom, calls=%fused_computation.3.clone | custom fusion | bytes 365568 | tf_op jit(solution)/shard_map/jit(_take)/gather | solution.py:35
  96.0 2.7 %collective-permute-start.2 = (bf16[16,588]{0,1:T(8,128)(2,1)S(1)}, bf16[16,588]{0,1:T(8,128)(2,1)S(1)}, u32[]{:S(2)}, u32[]{:S(2)}) collective-permute-start(bf16[16,588]{0,1:T(8,128)(2,1)S(1)} %select_bitcast_fusion), channel_id=1, source_target_pairs={{4,0},{8,4},{12,8},{16,12},{20,16},{24,20},{28,24},{0,28},{5,1},{9... | collective-permute-start | bytes 56456 | tf_op jit(solution)/shard_map/ppermute | solution.py:17
  98.7 2.8 %broadcast_select_fusion.1 = bf16[5376,16]{1,0:T(8,128)(2,1)S(1)} fusion(bf16[5376,16]{1,0:T(8,128)(2,1)S(1)} %gather_fusion.3, pred[5376]{0:T(1024)(128)(4,1)S(1)} %compare_and_fusion), kind=kLoop, calls=%fused_computation.17 | loop fusion | flops 86016 | bytes 349440 | tf_op jit(solution)/shard_map/jit(_take)/select_n | solution.py:35
  101.4 3.4 %fusion = f32[12,16,448]{2,1,0:T(8,128)S(1)} fusion(bf16[16,12,448]{0,2,1:T(8,128)(2,1)S(1)} %bitcast.60, bf16[12,512,512]{2,1,0:T(8,128)(2,1)} %param.11), kind=kOutput, calls=%fused_computation.12 | convolution fusion | flops 77070336 | bytes 6021120 | tf_op jit(solution)/shard_map/bem,eml->bel/dot_general | solution.py:36
  104.9 2.3 fusion.6
  107.1 1.9 gather_fusion.5
  109.2 1.2 fusion.10
  110.7 6.1 %scatter_custom_fusion.4 = f32[16,588]{0,1:T(8,128)S(1)} fusion(s32[768]{0:T(1024)S(1)} %fusion.31, f32[768,16]{1,0:T(8,128)S(1)} %copy.96, f32[]{:T(128)} %constant.89.clone.1), kind=kCustom, calls=%fused_computation.49 | custom fusion | flops 12288 | bytes 37636 | tf_op jit(solution)/shard_map/scatter-add | solution.py:43
  116.8 0.3 collective-permute-start.3
  117.1 1.4 fusion.8
  118.6 0.2 copy.91
  119.0 2.3 copy.92
  121.3 31.4 %scatter_custom_fusion.3 = f32[16,4116]{0,1:T(8,128)S(1)} fusion(s32[5376]{0:T(1024)S(1)} %fusion.30, f32[5376,16]{1,0:T(8,128)} %copy.92, f32[]{:T(128)} %constant.89.clone.1), kind=kCustom, calls=%fused_computation.30 | custom fusion | flops 86016 | bytes 263936 | tf_op jit(solution)/shard_map/scatter-add | solution.py:50
  152.7 6.9 %scatter_custom_fusion.5 = f32[16,4116]{0,1:T(8,128)S(1)} fusion(f32[16,4116]{0,1:T(8,128)S(1)} %scatter_custom_fusion.3, s32[588]{0:T(1024)S(1)} %compare_select_fusion.4, f32[16,588]{0,1:T(8,128)S(1)} %collective-permute-done.3), kind=kCustom, calls=%fused_computation.36 | custom fusion | flops 9408 | bytes 566528 | tf_op jit(solution)/shard_map/scatter-add | solution.py:52
  159.6 0.6 copy.97
  160.6 13.2 %all_to_all.35 = f32[16,4,1029]{2,0,1:T(8,128)S(1)} all-to-all(f32[16,4,1029]{2,0,1:T(8,128)S(1)} %copy.98), channel_id=1, replica_groups=mesh['space'=8,'band'=4] {'band'}, dimensions={1} | all-to-all | bytes 526848 | tf_op jit(solution)/shard_map/all_to_all | solution.py:57
  173.8 0.4 fusion.32
  174.2 38.3 %psum.7 = f32[64,64]{0,1:T(8,128)S(1)} all-reduce(f32[64,64]{0,1:T(8,128)S(1)} %fusion.32), channel_id=1, replica_groups=mesh['space'=8,'band'=4] {'space','band'}, use_global_device_ids=true, to_apply=%region_6.10 | all-reduce | flops 4096 | bytes 32768 | tf_op jit(solution)/shard_map/psum | solution.py:65
  212.7 5.8 %cholesky.16 = f32[64,64]{1,0:T(8,128)S(1)} custom-call(f32[64,64]{1,0:T(8,128)S(1)} %fusion.29), custom_call_target="Cholesky" | custom-call | tf_op jit(solution)/shard_map/jit(cholesky)/cholesky | solution.py:67
  218.6 0.6 compare_reduce_fusion
  219.2 0.7 fusion.28
  219.9 4.9 %custom-call.7 = f32[1,64,64]{1,2,0:T(8,128)S(1)} custom-call(f32[1,64,64]{2,1,0:T(8,128)S(1)} %fusion.28), custom_call_target="InvertDiagBlocksLowerTriangular" | custom-call | tf_op jit(solution)/shard_map/jit(_solve_triangular)/triangular_solve | solution.py:68
  224.9 0.4 fusion.33
  225.3 12.1 %all_to_all.36 = f32[4,16,1029]{2,1,0:T(8,128)S(1)} all-to-all(f32[4,16,1029]{2,1,0:T(8,128)S(1)} %fusion.33), channel_id=1, replica_groups=mesh['space'=8,'band'=4] {'band'}, dimensions={0} | all-to-all | bytes 526848 | tf_op jit(solution)/shard_map/all_to_all | solution.py:69
  237.5 0.9 all_to_all.32
  (41 shorter events, 2.7 us)
Async XLA Ops:
  4.9 25.0 %collective-permute-start = (bf16[16,588]{0,1:T(8,128)(2,1)S(1)}, bf16[16,588]{0,1:T(8,128)(2,1)S(1)}, u32[]{:S(2)}, u32[]{:S(2)}) collective-permute-start(bf16[16,588]{0,1:T(8,128)(2,1)S(1)} %select_bitcast_fusion.1), channel_id=1, source_target_pairs={{4,0},{8,4},{12,8},{16,12},{20,16},{24,20},{28,24},{0,28},{5,1},{9... | collective-permute-start | bytes 56456 | tf_op jit(solution)/shard_map/ppermute | solution.py:17
  39.7 35.7 %collective-permute-start.1 = (f32[16,588]{0,1:T(8,128)S(1)}, f32[16,588]{0,1:T(8,128)S(1)}, u32[]{:S(2)}, u32[]{:S(2)}) collective-permute-start(f32[16,588]{0,1:T(8,128)S(1)} %scatter_custom_fusion.1), channel_id=1, source_target_pairs={{28,0},{0,4},{4,8},{8,12},{12,16},{16,20},{20,24},{24,28},{29,1},{... | collective-permute-start | bytes 112904 | tf_op jit(solution)/shard_map/ppermute | solution.py:17
  75.3 7.7 %copy-start = (f32[16,4116]{1,0:T(8,128)S(1)}, f32[16,4116]{1,0:T(8,128)}, u32[]{:S(2)}) copy-start(f32[16,4116]{1,0:T(8,128)} %param.10) | copy-start | bytes 790276
  96.0 11.2 %collective-permute-start.2 = (bf16[16,588]{0,1:T(8,128)(2,1)S(1)}, bf16[16,588]{0,1:T(8,128)(2,1)S(1)}, u32[]{:S(2)}, u32[]{:S(2)}) collective-permute-start(bf16[16,588]{0,1:T(8,128)(2,1)S(1)} %select_bitcast_fusion), channel_id=1, source_target_pairs={{4,0},{8,4},{12,8},{16,12},{20,16},{24,20},{28,24},{0,28},{5,1},{9... | collective-permute-start | bytes 56456 | tf_op jit(solution)/shard_map/ppermute | solution.py:17
  116.8 35.9 %collective-permute-start.3 = (f32[16,588]{0,1:T(8,128)S(1)}, f32[16,588]{0,1:T(8,128)S(1)}, u32[]{:S(2)}, u32[]{:S(2)}) collective-permute-start(f32[16,588]{0,1:T(8,128)S(1)} %scatter_custom_fusion.4), channel_id=1, source_target_pairs={{28,0},{0,4},{4,8},{8,12},{12,16},{16,20},{20,24},{24,28},{29,1},{... | collective-permute-start | bytes 112904 | tf_op jit(solution)/shard_map/ppermute | solution.py:17
where the time goes:
time: 239 us; the launch traced here: 238 us
  other arithmetic  110 us (46%)
  blocking collectives  63.7 us (27%)
  local copies, waits for them, and re-layouts  40.7 us (17%)
  matrix products  17.6 us (7%)
  starting transfers between devices  6.4 us (3%)
    scatter-add x2, other arithmetic, apply_operator(): owned.at[:, conn_inside]  62.8 us
    psum x1, blocking collectives, per_device(): correlation = lax.psum(partial_value, ('space', 'band'))  38.3 us
    gather x2, local copies, waits for them, and re-layouts, apply_operator(): jnp.take(rounded, conn_inside, axis=1)  20.5 us
    scatter-add x2, other arithmetic, apply_operator(): return owned.at[:, face_rows].add(received)  14 us
    all_to_all x1, blocking collectives, per_device(): lax.all_to_all(following, 'band', split_axis=1, concat_axis=0, tiled=True)  13.2 us
    scatter-add x2, other arithmetic, apply_operator(): upper_sums.at[:, conn_upper]  12.2 us
    all_to_all x1, blocking collectives, per_device(): lax.all_to_all(orthonormal, 'band', split_axis=0, concat_axis=1, tiled=True)  12.1 us
    dot_general x2, matrix products, apply_operator(): jnp.einsum('bem,eml->bel', inside, ham_inner, preferred_element_type=jnp....  6.87 us
  transfers between devices with their start and end apart: 4, of which 0 were waited for; matrix products, arithmetic and copies ran while one was open for 42% of the time, Pallas kernels for 0%

commit v1 on v0

v1 whole, which is shorter than its diff:
```python
import functools

import jax
import jax.numpy as jnp
from jax import lax
from jax.experimental import pallas as pl
from jax.experimental.pallas import tpu as pltpu
from jax.sharding import PartitionSpec as P

FACE_EL = 64
IN_EL = 448
LANES = 256

CENTER = 6.25
HALF_WIDTH = 7.5

F32 = jnp.float32
BF16 = jnp.bfloat16
VMEM = pl.BlockSpec(memory_space=pltpu.VMEM)
ANY = pl.BlockSpec(memory_space=pl.ANY)
LIMIT = 48 * 1024 * 1024


def round_up(count, unit):
    return -(-count // unit) * unit


def one_hot(low):
    rows = lax.broadcasted_iota(jnp.int32, (LANES, low.shape[1]), 0)
    return jnp.where(rows == low, 1.0, 0.0).astype(BF16)


def stacked(field):
    blocks = field.shape[1] // LANES
    return jnp.concatenate([field[:, i * LANES : (i + 1) * LANES] for i in range(blocks)], axis=0)


def unstacked(rows, bands):
    blocks = rows.shape[0] // bands
    return jnp.concatenate([rows[i * bands : (i + 1) * bands] for i in range(blocks)], axis=1)


def pick(rows, high, low_hot, bands, first=0):
    table = jnp.dot(rows, low_hot, preferred_element_type=F32)
    out = jnp.zeros((bands, low_hot.shape[1]), F32)
    for i in range(rows.shape[0] // bands):
        out = jnp.where(high == i + first, table[i * bands : (i + 1) * bands], out)
    return out


def halves(values):
    upper = values.astype(BF16)
    return upper, (values - upper.astype(F32)).astype(BF16)


def spread(values, high, blocks, first=0):
    rows = []
    for part in halves(values):
        wide = part.astype(F32)
        for i in range(blocks):
            rows.append(jnp.where(high == i + first, wide, 0.0).astype(BF16))
    return jnp.concatenate(rows, axis=0)


def gathered_sum(rows, low_hot):
    both = lax.dot_general(rows, low_hot, (((1,), (1,)), ((), ())), preferred_element_type=F32)
    count = both.shape[0] // 2
    return both[:count] + both[count:]


def face_kernel(psi_ref, face_ref, out_ref, pad_ref):
    bands, nodes = psi_ref.shape
    pad_ref[...] = jnp.zeros_like(pad_ref)
    pad_ref[:, :nodes] = psi_ref[...]
    rows = stacked(pad_ref[...]).astype(BF16)
    face = face_ref[...]
    out_ref[...] = pick(rows, face >> 8, one_hot(face & 255), bands).astype(BF16)


def place(conn, nodes, own):
    return jnp.where(conn >= nodes, conn + (own - nodes), conn)


def interior_kernel(psi_ref, conn_ref, ham_ref, out_ref, pad_ref, ham_vmem, sems):
    bands, nodes = psi_ref.shape
    elements, size = conn_ref.shape
    own = pad_ref.shape[1]
    for e in range(elements):
        pltpu.make_async_copy(ham_ref.at[e], ham_vmem.at[e], sems.at[e]).start()
    pad_ref[...] = jnp.zeros_like(pad_ref)
    pad_ref[:, :nodes] = psi_ref[...]
    rows = stacked(pad_ref[...]).astype(BF16)
    for e in range(elements):
        slots = place(conn_ref[e : e + 1, :], nodes, own)
        inside = pick(rows, slots >> 8, one_hot(slots & 255), bands).astype(BF16)
        pltpu.make_async_copy(ham_ref.at[e], ham_vmem.at[e], sems.at[e]).wait()
        out_ref[:, e * size : (e + 1) * size] = jnp.dot(inside, ham_vmem[e], preferred_element_type=F32)


def first_kernel(psi_ref, conn_ref, ham_ref, face_ref, ghost_ref, part_ref, own_ref, upper_ref, low_ref, pad_ref, ham_vmem, sums, hots, sems):
    bands, nodes = psi_ref.shape
    elements, size = conn_ref.shape
    own = pad_ref.shape[1]
    for e in range(elements):
        pltpu.make_async_copy(ham_ref.at[e, pl.ds(IN_EL, FACE_EL)], ham_vmem.at[e], sems.at[e]).start()
    pad_ref[...] = jnp.zeros_like(pad_ref)
    pad_ref[:, :nodes] = psi_ref[...]
    ghost = stacked(ghost_ref[...])
    first = own // LANES
    blocks = first + ghost.shape[0] // bands
    for e in range(elements):
        slots = place(conn_ref[e : e + 1, :], nodes, own)
        high = slots >> 8
        hot = one_hot(slots & 255)
        hots[:, e * size : (e + 1) * size] = hot
        outside = pick(ghost, high[:, IN_EL:], hot[:, IN_EL:], bands, first).astype(BF16)
        pltpu.make_async_copy(ham_ref.at[e, pl.ds(IN_EL, FACE_EL)], ham_vmem.at[e], sems.at[e]).wait()
        product = part_ref[:, e * size : (e + 1) * size] + jnp.dot(outside, ham_vmem[e], preferred_element_type=F32)
        sums[:, e * size : (e + 1) * size] = spread(product, high, blocks)
    total = unstacked(gathered_sum(sums[...], hots[...]), bands)
    current = (total[:, :own] - CENTER * pad_ref[...]) / HALF_WIDTH
    own_ref[...] = current
    upper_ref[...] = total[:, own:] / HALF_WIDTH
    face = face_ref[...]
    face_hot = one_hot(face & 255)
    terms = halves(stacked(current))
    low_ref[...] = pick(terms[0], face >> 8, face_hot, bands) + pick(terms[1], face >> 8, face_hot, bands)


def second_kernel(psi_ref, conn_ref, ham_ref, face_ref, own_in, upper_in, below_in, above_in, own_ref, upper_ref, pad_ref, ham_vmem, sums, hots, sems):
    bands, nodes = psi_ref.shape
    elements, size = conn_ref.shape
    own = pad_ref.shape[1]
    for e in range(elements):
        pltpu.make_async_copy(ham_ref.at[e], ham_vmem.at[e], sems.at[e]).start()
    pad_ref[...] = jnp.zeros_like(pad_ref)
    pad_ref[:, :nodes] = psi_ref[...]
    first = own // LANES
    face = face_ref[...]
    added = gathered_sum(spread(below_in[...], face >> 8, first), one_hot(face & 255))
    current = own_in[...] + unstacked(added, bands)
    ghost = upper_in[...] + above_in[...]
    rows = jnp.concatenate([stacked(current), stacked(ghost)], axis=0).astype(BF16)
    blocks = rows.shape[0] // bands
    for e in range(elements):
        slots = place(conn_ref[e : e + 1, :], nodes, own)
        high = slots >> 8
        hot = one_hot(slots & 255)
        hots[:, e * size : (e + 1) * size] = hot
        inside = pick(rows, high, hot, bands).astype(BF16)
        pltpu.make_async_copy(ham_ref.at[e], ham_vmem.at[e], sems.at[e]).wait()
        product = jnp.dot(inside, ham_vmem[e], preferred_element_type=F32)
        sums[:, e * size : (e + 1) * size] = spread(product, high, blocks)
    total = unstacked(gathered_sum(sums[...], hots[...]), bands)
    own_ref[...] = 2.0 * ((total[:, :own] - CENTER * current) / HALF_WIDTH) - pad_ref[...]
    upper_ref[...] = total[:, own:] * (2.0 / HALF_WIDTH)


def last_kernel(nodes, own_in, face_ref, below_in, out_ref):
    bands, own = own_in.shape
    face = face_ref[...]
    added = gathered_sum(spread(below_in[...], face >> 8, own // LANES), one_hot(face & 255))
    out_ref[...] = (own_in[...] + unstacked(added, bands))[:, :nodes]


def call(kernel, out_shape, inputs, scratch=(), flops=0, moved=0):
    return pl.pallas_call(
        kernel,
        out_shape=out_shape,
        in_specs=[ANY if array.ndim == 3 else VMEM for array in inputs],
        out_specs=jax.tree.map(lambda _: VMEM, out_shape),
        scratch_shapes=list(scratch),
        compiler_params=pltpu.CompilerParams(vmem_limit_bytes=LIMIT),
        cost_estimate=pl.CostEstimate(flops=flops, bytes_accessed=moved, transcendentals=0),
    )(*inputs)


def from_behind(block, axis, distance):
    devices = range(lax.axis_size(axis))
    route = [((i - distance) % len(devices), i) for i in devices]
    return lax.ppermute(block, axis, route)


def filter_field(psi, ham, conn, face_rows):
    bands, nodes = psi.shape
    elements, size = conn.shape
    own = round_up(nodes, LANES)
    slots = round_up(face_rows.shape[0], LANES)
    blocks = (own + slots) // LANES
    face = jnp.pad(face_rows, (0, slots - face_rows.shape[0]), constant_values=-1)[None]
    shape = jax.ShapeDtypeStruct
    pad = pltpu.VMEM((bands, own), F32)
    copies = pltpu.SemaphoreType.DMA((elements,))
    sums = pltpu.VMEM((2 * blocks * bands, elements * size), BF16)
    hots = pltpu.VMEM((LANES, elements * size), BF16)

    with jax.named_scope("face_values"):
        values = call(face_kernel, shape((bands, slots), BF16), (psi, face), (pad,))
    ghost = from_behind(values, "space", -1)
    with jax.named_scope("interior"):
        part = call(
            interior_kernel, shape((bands, elements * size), F32), (psi, conn, ham),
            (pad, pltpu.VMEM((elements, size, size), BF16), copies), flops=4 * 10**9, moved=8 * 10**6,
        )
    with jax.named_scope("first_step"):
        current, upper, low = call(
            first_kernel,
            (shape((bands, own), F32), shape((bands, slots), F32), shape((bands, slots), F32)),
            (psi, conn, ham, face, ghost, part),
            (pad, pltpu.VMEM((elements, FACE_EL, size), BF16), sums, hots, copies), flops=4 * 10**9, moved=10**6,
        )
    below = from_behind(upper, "space", 1)
    above = from_behind(low, "space", -1)
    with jax.named_scope("second_step"):
        following, upper = call(
            second_kernel,
            (shape((bands, own), F32), shape((bands, slots), F32)),
            (psi, conn, ham, face, current, upper, below, above),
            (pad, pltpu.VMEM((elements, size, size), BF16), sums, hots, copies), flops=8 * 10**9, moved=8 * 10**6,
        )
    below = from_behind(upper, "space", 1)
    with jax.named_scope("last_faces"):
        return call(functools.partial(last_kernel, nodes), shape((bands, nodes), F32), (following, face, below))


def per_device(psi, ham, conn, face_rows):
    node_count = psi.shape[1]
    following = filter_field(psi, ham, conn, face_rows)
    node_rows = lax.all_to_all(following, "band", split_axis=1, concat_axis=0, tiled=True)
    partial_value = lax.dot_general(
        node_rows,
        node_rows,
        (((1,), (1,)), ((), ())),
        precision=lax.Precision.HIGHEST,
        preferred_element_type=jnp.float32,
    )
    correlation = lax.psum(partial_value, ("space", "band"))
    correlation = correlation / (node_count * lax.axis_size("space"))
    factor = jnp.linalg.cholesky(correlation)
    orthonormal = jax.scipy.linalg.solve_triangular(factor, node_rows, lower=True)
    return lax.all_to_all(orthonormal, "band", split_axis=0, concat_axis=1, tiled=True)


def solution(mesh):
    placed = (P("band", "space"), P("space", None, None), P("space", None), P("space"))
    return jax.shard_map(
        per_device, mesh=mesh, in_specs=placed, out_specs=P("band", "space"), check_vma=False
    )
```

time: 239 us -> 113 us (0.47)
  other arithmetic: 110 us -> 12.1 us
  local copies, waits for them, and re-layouts: 40.7 us -> 3.83 us
  Pallas kernels: 0 us -> 20.4 us
  matrix products: 17.6 us -> 0.83 us
  waiting for transfers between devices: 0.01 us -> 8.81 us
    scatter-add x6 -> x0, other arithmetic: 88.9 us -> none  [the longest x2 62.8 us: apply_operator(): owned.at[:, conn_inside]]
    gather x6 -> x0, local copies, waits for them, and re-layouts: 28.2 us -> none  [the longest x2 20.5 us: apply_operator(): jnp.take(rounded, conn_inside, axis=1)]
    pallas_call x0 -> x5, Pallas kernels: none -> 20.4 us  [call(): pl.pallas_call(kernel, out_shape=out_shape, in_specs=[ANY if array.ndim =...]
    dot_general x8 -> x0, matrix products: 16.8 us -> none  [the longest x2 6.87 us: apply_operator(): jnp.einsum('bem,eml->bel', inside, ham_inner, preferred_element_type=jnp....]
    ppermute x4, waiting for transfers between devices: 0.01 us -> 8.81 us  [from_behind(): return lax.ppermute(block, axis, route)]
    reshape x10 -> x0, local copies, waits for them, and re-layouts: 7.19 us -> none  [the longest x4 5.01 us: apply_operator(): remainder.reshape(band_count, elem_count * IN_EL)]
    select_n x11 -> x0, other arithmetic: 6.97 us -> none  [the longest x3 5.56 us: apply_operator(): jnp.take(rounded, conn_inside, axis=1)]
  transfers between devices with their start and end apart: 4 -> 4, of which waited for: 0 -> 3; matrix products, arithmetic and copies ran while one was open for 42% -> 0% of each run, Pallas kernels for 0% -> 4%
where the time goes in v1:
time: 113 us
  blocking collectives  62.6 us (55%)
  Pallas kernels  20.4 us (18%)
  other arithmetic  12.1 us (11%)
  waiting for transfers between devices  8.81 us (8%)
  starting transfers between devices  4.17 us (4%)
  local copies, waits for them, and re-layouts  3.83 us (3%)
    psum x1, blocking collectives, per_device(): correlation = lax.psum(partial_value, ('space', 'band'))  38.7 us
    pallas_call x5, Pallas kernels, call(): pl.pallas_call(kernel, out_shape=out_shape, in_specs=[ANY if array.ndim =...  20.4 us
    all_to_all x1, blocking collectives, per_device(): lax.all_to_all(following, 'band', split_axis=1, concat_axis=0, tiled=True)  12.4 us
    all_to_all x1, blocking collectives, per_device(): lax.all_to_all(orthonormal, 'band', split_axis=0, concat_axis=1, tiled=True)  11.5 us
    ppermute x4, waiting for transfers between devices, from_behind(): return lax.ppermute(block, axis, route)  8.81 us
    another operation x3, other arithmetic, per_device(): factor = jnp.linalg.cholesky(correlation)  6.52 us
    another operation x2, other arithmetic, per_device(): jax.scipy.linalg.solve_triangular(factor, node_rows, lower=True)  5.55 us
    ppermute x4, starting transfers between devices, from_behind(): return lax.ppermute(block, axis, route)  4.17 us
  transfers between devices with their start and end apart: 4, of which 3 were waited for; matrix products, arithmetic and copies ran while one was open for 0% of the time, Pallas kernels for 4%

profile of v1, /device:TPU:0, one launch (start us, length us, event | category | flops | bytes accessed | tf_op | source)
XLA Modules:
  0.0 112.9 jit_solution(3623239971905504523)
XLA Ops:
  0.0 0.7 pad.4
  0.7 0.0 copy-start
  0.7 1.0 copy-done
  1.7 0.3 face_values.1
  2.0 3.4 %collective-permute-start = (bf16[16,768]{1,0:T(8,128)(2,1)S(1)}, bf16[16,768]{1,0:T(8,128)(2,1)S(1)}, u32[]{:S(2)}, u32[]{:S(2)}) collective-permute-start(bf16[16,768]{1,0:T(8,128)(2,1)S(1)} %face_values.1), channel_id=1, source_target_pairs={{4,0},{8,4},{12,8},{16,12},{20,16},{24,20},{28,24},{0,28},{5,1},{9... | collective-permute-start | bytes 73736 | tf_op jit(solution)/shard_map/ppermute | solution.py:181
  5.4 0.0 copy-start.1
  5.4 0.8 copy-done.1
  6.1 4.7 %interior.1.part_ref = f32[16,6144]{1,0:T(8,128)S(1)} custom-call(f32[16,4116]{1,0:T(8,128)S(1)} %copy-done, s32[12,512]{1,0:T(8,128)S(1)} %copy-done.1, bf16[12,512,512]{2,1,0:T(8,128)(2,1)} %ham_ref.5), custom_call_target="tpu_custom_call" | custom-call | flops 4000000000 | bytes 8000000 | tf_op jit(solution)/shard_map/interior/pallas_call | solution.py:167
  10.9 0.0 collective-permute-done.ghost_ref
  10.9 6.9 %first_step.1 = (f32[16,4352]{1,0:T(8,128)S(1)}, f32[16,768]{1,0:T(8,128)S(1)}, f32[16,768]{1,0:T(8,128)S(1)}) custom-call(f32[16,4116]{1,0:T(8,128)S(1)} %copy-done, s32[12,512]{1,0:T(8,128)S(1)} %copy-done.1, bf16[12,512,512]{2,1,0:T(8,128)(2,1)} %ham_ref.5, s32[1,768]{1,0:T(1,128)S(1)} %broadcast_in_dim.5.face_ref, ...), custom_call_target="tpu_custom_call" | custom-call | flops 4000000000 | bytes 1000000 | tf_op jit(solution)/shard_map/first_step/pallas_call | solution.py:167
  17.8 0.7 collective-permute-start.2
  18.5 0.0 collective-permute-start.1
  18.5 1.7 %collective-permute-done.2.above_in = f32[16,768]{1,0:T(8,128)S(1)} collective-permute-done((f32[16,768]{1,0:T(8,128)S(1)}, f32[16,768]{1,0:T(8,128)S(1)}, u32[]{:S(2)}, u32[]{:S(2)}) %collective-permute-start.2) | collective-permute-done | bytes 49184 | tf_op jit(solution)/shard_map/ppermute | solution.py:181
  20.2 2.7 %collective-permute-done.1.below_in = f32[16,768]{1,0:T(8,128)S(1)} collective-permute-done((f32[16,768]{1,0:T(8,128)S(1)}, f32[16,768]{1,0:T(8,128)S(1)}, u32[]{:S(2)}, u32[]{:S(2)}) %collective-permute-start.1) | collective-permute-done | bytes 49184 | tf_op jit(solution)/shard_map/ppermute | solution.py:181
  22.9 8.0 %second_step.1 = (f32[16,4352]{1,0:T(8,128)S(1)}, f32[16,768]{1,0:T(8,128)S(1)}) custom-call(f32[16,4116]{1,0:T(8,128)S(1)} %copy-done, s32[12,512]{1,0:T(8,128)S(1)} %copy-done.1, bf16[12,512,512]{2,1,0:T(8,128)(2,1)} %ham_ref.5, s32[1,768]{1,0:T(1,128)S(1)} %broadcast_in_dim.5.face_ref, f32[16,4352]{1,0:T(8,128)S(1)} %get-tuple-element.10.own_in, ...), custom_call_target="tpu_custom_call" | custom-call | flops 8000000000 | bytes 8000000 | tf_op jit(solution)/shard_map/second_step/pallas_call | solution.py:167
  30.9 0.1 collective-permute-start.3
  31.0 4.4 %collective-permute-done.3.below_in = f32[16,768]{1,0:T(8,128)S(1)} collective-permute-done((f32[16,768]{1,0:T(8,128)S(1)}, f32[16,768]{1,0:T(8,128)S(1)}, u32[]{:S(2)}, u32[]{:S(2)}) %collective-permute-start.3) | collective-permute-done | bytes 49184 | tf_op jit(solution)/shard_map/ppermute | solution.py:181
  35.4 0.4 last_faces.1
  35.8 0.2 all_to_all.26
  36.1 12.4 %all_to_all.35 = f32[16,4,1029]{2,0,1:T(8,128)S(1)} all-to-all(f32[16,4,1029]{2,0,1:T(8,128)S(1)} %copy.14), channel_id=1, replica_groups=mesh['space'=8,'band'=4] {'band'}, dimensions={1} | all-to-all | bytes 526848 | tf_op jit(solution)/shard_map/all_to_all | solution.py:229
  48.5 0.4 fusion.2
  49.0 38.7 %psum.7 = f32[64,64]{0,1:T(8,128)S(1)} all-reduce(f32[64,64]{0,1:T(8,128)S(1)} %fusion.2), channel_id=1, replica_groups=mesh['space'=8,'band'=4] {'space','band'}, use_global_device_ids=true, to_apply=%region_0.1 | all-reduce | flops 4096 | bytes 32768 | tf_op jit(solution)/shard_map/psum | solution.py:237
  87.7 0.1 copy.16
  87.8 5.8 %cholesky.16 = f32[64,64]{1,0:T(8,128)S(1)} custom-call(f32[64,64]{1,0:T(8,128)S(1)} %fusion.1), custom_call_target="Cholesky" | custom-call | tf_op jit(solution)/shard_map/jit(cholesky)/cholesky | solution.py:239
  93.6 0.6 compare_reduce_fusion
  94.3 0.7 fusion
  94.9 4.9 %custom-call.7 = f32[1,64,64]{1,2,0:T(8,128)S(1)} custom-call(f32[1,64,64]{2,1,0:T(8,128)S(1)} %fusion), custom_call_target="InvertDiagBlocksLowerTriangular" | custom-call | tf_op jit(solution)/shard_map/jit(_solve_triangular)/triangular_solve | solution.py:240
  99.8 0.1 copy.17
  99.9 0.4 fusion.3
  100.3 11.5 %all_to_all.36 = f32[4,16,1029]{2,1,0:T(8,128)S(1)} all-to-all(f32[4,16,1029]{2,1,0:T(8,128)S(1)} %fusion.3), channel_id=1, replica_groups=mesh['space'=8,'band'=4] {'band'}, dimensions={0} | all-to-all | bytes 526848 | tf_op jit(solution)/shard_map/all_to_all | solution.py:241
  111.9 0.1 copy.18
  112.0 0.9 all_to_all.32
  (5 shorter events, 0.1 us)
Async XLA Ops:
  0.7 1.0 copy-start
  2.0 8.9 %collective-permute-start = (bf16[16,768]{1,0:T(8,128)(2,1)S(1)}, bf16[16,768]{1,0:T(8,128)(2,1)S(1)}, u32[]{:S(2)}, u32[]{:S(2)}) collective-permute-start(bf16[16,768]{1,0:T(8,128)(2,1)S(1)} %face_values.1), channel_id=1, source_target_pairs={{4,0},{8,4},{12,8},{16,12},{20,16},{24,20},{28,24},{0,28},{5,1},{9... | collective-permute-start | bytes 73736 | tf_op jit(solution)/shard_map/ppermute | solution.py:181
  5.4 0.8 copy-start.1
  17.8 2.5 %collective-permute-start.2 = (f32[16,768]{1,0:T(8,128)S(1)}, f32[16,768]{1,0:T(8,128)S(1)}, u32[]{:S(2)}, u32[]{:S(2)}) collective-permute-start(f32[16,768]{1,0:T(8,128)S(1)} %get-tuple-element.12), channel_id=1, source_target_pairs={{4,0},{8,4},{12,8},{16,12},{20,16},{24,20},{28,24},{0,28},{5,1},{9... | collective-permute-start | bytes 147464 | tf_op jit(solution)/shard_map/ppermute | solution.py:181
  18.5 4.4 %collective-permute-start.1 = (f32[16,768]{1,0:T(8,128)S(1)}, f32[16,768]{1,0:T(8,128)S(1)}, u32[]{:S(2)}, u32[]{:S(2)}) collective-permute-start(f32[16,768]{1,0:T(8,128)S(1)} %get-tuple-element.11.upper_in), channel_id=1, source_target_pairs={{28,0},{0,4},{4,8},{8,12},{12,16},{16,20},{20,24},{24,28},{29,1},{... | collective-permute-start | bytes 147464 | tf_op jit(solution)/shard_map/ppermute | solution.py:181
  30.9 4.5 %collective-permute-start.3 = (f32[16,768]{1,0:T(8,128)S(1)}, f32[16,768]{1,0:T(8,128)S(1)}, u32[]{:S(2)}, u32[]{:S(2)}) collective-permute-start(f32[16,768]{1,0:T(8,128)S(1)} %get-tuple-element.14), channel_id=1, source_target_pairs={{28,0},{0,4},{4,8},{8,12},{12,16},{16,20},{20,24},{24,28},{29,1},{... | collective-permute-start | bytes 147464 | tf_op jit(solution)/shard_map/ppermute | solution.py:181

commit v2 on v1

--- a/solution.py
+++ b/solution.py
@@ -223,22 +223,97 @@
         return call(functools.partial(last_kernel, nodes), shape((bands, nodes), F32), (following, face, below))
 
 
+def gram_kernel(*refs):
+    *blocks, terms_ref, gram_ref = refs
+    bands, nodes = blocks[0].shape
+    total = bands * len(blocks)
+    me = lax.axis_index("band")
+    terms_ref[:, nodes - nodes % 128 :] = jnp.zeros_like(terms_ref[:, nodes - nodes % 128 :])
+    for distance, block in enumerate(blocks):
+        source = pl.multiple_of(lax.rem(me - distance + len(blocks), len(blocks)) * bands, bands)
+        upper, lower = halves(block[...])
+        terms_ref[pl.ds(source, bands), :nodes] = upper
+        terms_ref[pl.ds(total + source, bands), :nodes] = lower
+    terms = terms_ref[...]
+    both = lax.dot_general(terms, terms, (((1,), (1,)), ((), ())), preferred_element_type=F32)
+    gram_ref[...] = both[:total, :total] + (both[:total, total:] + both[total:, :total]) + both[total:, total:]
+
+
+def inverse_factor(matrix, block=4):
+    size = matrix.shape[0]
+    width = 2 * size
+    lane = lax.broadcasted_iota(jnp.int32, (8, width), 1)
+    row = lax.broadcasted_iota(jnp.int32, (8, width), 0)
+    zero = jnp.zeros((size, size), F32)
+    wide = jnp.concatenate([matrix, zero], axis=1)
+    groups = [wide[8 * g : 8 * g + 8] + jnp.where(lane == row + (size + 8 * g), 1.0, 0.0) for g in range(size // 8)]
+    for k in range(0, size, block):
+        start = k // 8
+        columns = [
+            [jnp.broadcast_to(groups[g][:, k + q : k + q + 1], (8, width)) for g in range(start, size // 8)]
+            for q in range(block)
+        ]
+        for q in range(block):
+            at = k + q - 8 * start
+            scale = 1.0 / columns[q][0][at : at + 1]
+            column = [jnp.where(row > at, columns[q][0], 0.0)] + columns[q][1:]
+            for p in range(q + 1, block):
+                factor = columns[p][0][at : at + 1] * scale
+                columns[p] = [value - weight * factor for value, weight in zip(columns[p], column)]
+            factor = groups[start][at : at + 1] * scale
+            for g, weight in enumerate(column):
+                groups[start + g] = groups[start + g] - weight * factor
+    out = []
+    for g, rows in enumerate(groups):
+        pivot = jnp.sum(jnp.where(lane == row + 8 * g, rows, 0.0), axis=1, keepdims=True)
+        out.append(rows[:, size:] / jnp.sqrt(pivot))
+    return jnp.concatenate(out, axis=0)
+
+
+def ortho_kernel(nodes, count, gram_ref, terms_ref, out_ref, inverse_ref):
+    bands = out_ref.shape[0]
+    inverse_ref[...] = inverse_factor(gram_ref[...] / count)
+    first = pl.multiple_of(lax.axis_index("band") * bands, bands)
+    upper, lower = halves(inverse_ref[pl.ds(first, bands), :])
+    rows = jnp.concatenate(
+        [jnp.concatenate([upper, upper], axis=1), jnp.concatenate([lower, lower], axis=1)], axis=0
+    )
+    both = jnp.dot(rows, terms_ref[...], preferred_element_type=F32)
+    out_ref[...] = (both[:bands] + both[bands:])[:, :nodes]
+
+
+def space_sum(block):
+    size = lax.axis_size("space")
+    if size & (size - 1):
+        return lax.psum(block, "space")
+    step = 1
+    while step < size:
+        span = 2 if step == 1 or step * 2 == size else 4
+        parts = [
+            lax.ppermute(block, "space", [(i, i ^ (step * k)) for i in range(size)]) for k in range(1, span)
+        ]
+        block = sum(parts, block)
+        step *= span
+    return block
+
+
 def per_device(psi, ham, conn, face_rows):
-    node_count = psi.shape[1]
+    bands, nodes = psi.shape
     following = filter_field(psi, ham, conn, face_rows)
-    node_rows = lax.all_to_all(following, "band", split_axis=1, concat_axis=0, tiled=True)
-    partial_value = lax.dot_general(
-        node_rows,
-        node_rows,
-        (((1,), (1,)), ((), ())),
-        precision=lax.Precision.HIGHEST,
-        preferred_element_type=jnp.float32,
-    )
-    correlation = lax.psum(partial_value, ("space", "band"))
-    correlation = correlation / (node_count * lax.axis_size("space"))
-    factor = jnp.linalg.cholesky(correlation)
-    orthonormal = jax.scipy.linalg.solve_triangular(factor, node_rows, lower=True)
-    return lax.all_to_all(orthonormal, "band", split_axis=0, concat_axis=1, tiled=True)
+    groups = lax.axis_size("band")
+    total = groups * bands
+    own = round_up(nodes, LANES)
+    shape = jax.ShapeDtypeStruct
+    blocks = [following] + [from_behind(following, "band", i) for i in range(1, groups)]
+    with jax.named_scope("gram"):
+        terms, gram = call(gram_kernel, (shape((2 * total, own), BF16), shape((total, total), F32)), blocks)
+    with jax.named_scope("gram_sum"):
+        gram = space_sum(gram)
+    with jax.named_scope("orthonormal"):
+        return call(
+            functools.partial(ortho_kernel, nodes, nodes * lax.axis_size("space")),
+            shape((bands, nodes), F32), (gram, terms), (pltpu.VMEM((total, total), F32),),
+        )
 
 
 def solution(mesh):

time: 113 us -> 72.6 us (0.64)
  blocking collectives: 62.6 us -> 0 us
  waiting for transfers between devices: 8.81 us -> 33 us
  other arithmetic: 12.1 us -> 0.02 us
  starting transfers between devices: 4.17 us -> 12.4 us
  Pallas kernels: 20.4 us -> 24.5 us
  local copies, waits for them, and re-layouts: 3.83 us -> 2.41 us
    psum x1 -> x0, blocking collectives: 38.7 us -> none  [per_device(): correlation = lax.psum(partial_value, ('space', 'band'))]
    all_to_all x2 -> x0, blocking collectives: 24 us -> none  [the longest x1 12.4 us: per_device(): lax.all_to_all(following, 'band', split_axis=1, concat_axis=0, tiled=True)]
    ppermute x4 -> x7, waiting for transfers between devices: 8.81 us -> 28.1 us  [from_behind(): return lax.ppermute(block, axis, route)]
    another operation x5 -> x0, other arithmetic: 12.1 us -> none  [the longest x3 6.52 us: per_device(): factor = jnp.linalg.cholesky(correlation)]
    ppermute x0 -> x4, waiting for transfers between devices: none -> 4.84 us  [space_sum(): lax.ppermute(block, 'space', [(i, i ^ step * k) for i in range(size)])]
    ppermute x4 -> x7, starting transfers between devices: 4.17 us -> 8.81 us  [from_behind(): return lax.ppermute(block, axis, route)]
    pallas_call x5 -> x7, Pallas kernels: 20.4 us -> 24.5 us  [call(): pl.pallas_call(kernel, out_shape=out_shape, in_specs=[ANY if array.ndim =...]
    ppermute x0 -> x4, starting transfers between devices: none -> 3.56 us  [space_sum(): lax.ppermute(block, 'space', [(i, i ^ step * k) for i in range(size)])]
  transfers between devices with their start and end apart: 4 -> 11, of which waited for: 3 -> 9; matrix products, arithmetic and copies ran while one was open for 0% -> 0% of each run, Pallas kernels for 4% -> 7%
where the time goes in v2:
time: 72.6 us; the launch traced here: 72.3 us
  waiting for transfers between devices  33 us (45%)
  Pallas kernels  24.5 us (34%)
  starting transfers between devices  12.4 us (17%)
  local copies, waits for them, and re-layouts  2.41 us (3%)
    ppermute x7, waiting for transfers between devices, from_behind(): return lax.ppermute(block, axis, route)  28.1 us
    pallas_call x7, Pallas kernels, call(): pl.pallas_call(kernel, out_shape=out_shape, in_specs=[ANY if array.ndim =...  24.5 us
    ppermute x7, starting transfers between devices, from_behind(): return lax.ppermute(block, axis, route)  8.81 us
    ppermute x4, waiting for transfers between devices, space_sum(): lax.ppermute(block, 'space', [(i, i ^ step * k) for i in range(size)])  4.84 us
    ppermute x4, starting transfers between devices, space_sum(): lax.ppermute(block, 'space', [(i, i ^ step * k) for i in range(size)])  3.56 us
    unnamed x4, local copies, waits for them, and re-layouts  1.71 us
  transfers between devices with their start and end apart: 11, of which 9 were waited for; matrix products, arithmetic and copies ran while one was open for 0% of the time, Pallas kernels for 7%

profile of v2, /device:TPU:0, one launch (start us, length us, event | category | flops | bytes accessed | tf_op | source)
XLA Modules:
  0.0 72.3 jit_solution(4848987841874255152)
XLA Ops:
  0.0 0.7 pad.4
  0.7 0.0 copy-start
  0.7 1.0 %copy-done = f32[16,4116]{1,0:T(8,128)S(1)} copy-done((f32[16,4116]{1,0:T(8,128)S(1)}, f32[16,4116]{1,0:T(8,128)}, u32[]{:S(2)}) %copy-start) | copy-done | bytes 263448
  1.7 0.3 face_values.1
  2.0 3.4 %collective-permute-start = (bf16[16,768]{1,0:T(8,128)(2,1)S(1)}, bf16[16,768]{1,0:T(8,128)(2,1)S(1)}, u32[]{:S(2)}, u32[]{:S(2)}) collective-permute-start(bf16[16,768]{1,0:T(8,128)(2,1)S(1)} %face_values.1), channel_id=1, source_target_pairs={{4,0},{8,4},{12,8},{16,12},{20,16},{24,20},{28,24},{0,28},{5,1},{9... | collective-permute-start | bytes 73736 | tf_op jit(solution)/shard_map/ppermute | solution.py:181
  5.4 0.0 copy-start.1
  5.4 0.8 %copy-done.1 = s32[12,512]{1,0:T(8,128)S(1)} copy-done((s32[12,512]{1,0:T(8,128)S(1)}, s32[12,512]{1,0:T(8,128)}, u32[]{:S(2)}) %copy-start.1) | copy-done | bytes 24600
  6.1 4.7 %interior.1.part_ref = f32[16,6144]{1,0:T(8,128)S(1)} custom-call(f32[16,4116]{1,0:T(8,128)S(1)} %copy-done, s32[12,512]{1,0:T(8,128)S(1)} %copy-done.1, bf16[12,512,512]{2,1,0:T(8,128)(2,1)} %ham_ref.5), custom_call_target="tpu_custom_call" | custom-call | flops 4000000000 | bytes 8000000 | tf_op jit(solution)/shard_map/interior/pallas_call | solution.py:167
  10.9 0.0 collective-permute-done.ghost_ref
  10.9 6.9 %first_step.1 = (f32[16,4352]{1,0:T(8,128)S(1)}, f32[16,768]{1,0:T(8,128)S(1)}, f32[16,768]{1,0:T(8,128)S(1)}) custom-call(f32[16,4116]{1,0:T(8,128)S(1)} %copy-done, s32[12,512]{1,0:T(8,128)S(1)} %copy-done.1, bf16[12,512,512]{2,1,0:T(8,128)(2,1)} %ham_ref.5, s32[1,768]{1,0:T(1,128)S(1)} %broadcast_in_dim.3.face_ref, ...), custom_call_target="tpu_custom_call" | custom-call | flops 4000000000 | bytes 1000000 | tf_op jit(solution)/shard_map/first_step/pallas_call | solution.py:167
  17.8 0.7 %collective-permute-start.2 = (f32[16,768]{1,0:T(8,128)S(1)}, f32[16,768]{1,0:T(8,128)S(1)}, u32[]{:S(2)}, u32[]{:S(2)}) collective-permute-start(f32[16,768]{1,0:T(8,128)S(1)} %get-tuple-element.14), channel_id=1, source_target_pairs={{4,0},{8,4},{12,8},{16,12},{20,16},{24,20},{28,24},{0,28},{5,1},{9... | collective-permute-start | bytes 147464 | tf_op jit(solution)/shard_map/ppermute | solution.py:181
  18.5 0.0 collective-permute-start.1
  18.5 1.7 %collective-permute-done.2.above_in = f32[16,768]{1,0:T(8,128)S(1)} collective-permute-done((f32[16,768]{1,0:T(8,128)S(1)}, f32[16,768]{1,0:T(8,128)S(1)}, u32[]{:S(2)}, u32[]{:S(2)}) %collective-permute-start.2) | collective-permute-done | bytes 49184 | tf_op jit(solution)/shard_map/ppermute | solution.py:181
  20.3 2.7 %collective-permute-done.1.below_in = f32[16,768]{1,0:T(8,128)S(1)} collective-permute-done((f32[16,768]{1,0:T(8,128)S(1)}, f32[16,768]{1,0:T(8,128)S(1)}, u32[]{:S(2)}, u32[]{:S(2)}) %collective-permute-start.1) | collective-permute-done | bytes 49184 | tf_op jit(solution)/shard_map/ppermute | solution.py:181
  22.9 8.0 %second_step.1 = (f32[16,4352]{1,0:T(8,128)S(1)}, f32[16,768]{1,0:T(8,128)S(1)}) custom-call(f32[16,4116]{1,0:T(8,128)S(1)} %copy-done, s32[12,512]{1,0:T(8,128)S(1)} %copy-done.1, bf16[12,512,512]{2,1,0:T(8,128)(2,1)} %ham_ref.5, s32[1,768]{1,0:T(1,128)S(1)} %broadcast_in_dim.3.face_ref, f32[16,4352]{1,0:T(8,128)S(1)} %get-tuple-element.12.own_in, ...), custom_call_target="tpu_custom_call" | custom-call | flops 8000000000 | bytes 8000000 | tf_op jit(solution)/shard_map/second_step/pallas_call | solution.py:167
  31.0 0.1 collective-permute-start.3
  31.0 4.4 %collective-permute-done.3.below_in = f32[16,768]{1,0:T(8,128)S(1)} collective-permute-done((f32[16,768]{1,0:T(8,128)S(1)}, f32[16,768]{1,0:T(8,128)S(1)}, u32[]{:S(2)}, u32[]{:S(2)}) %collective-permute-start.3) | collective-permute-done | bytes 49184 | tf_op jit(solution)/shard_map/ppermute | solution.py:181
  35.4 0.4 last_faces.1.refs_0_
  35.9 3.6 %collective-permute-start.6 = (f32[16,4116]{1,0:T(8,128)S(1)}, f32[16,4116]{1,0:T(8,128)S(1)}, u32[]{:S(2)}, u32[]{:S(2)}) collective-permute-start(f32[16,4116]{1,0:T(8,128)S(1)} %last_faces.1.refs_0_), channel_id=1, source_target_pairs={{1,0},{2,1},{3,2},{0,3},{5,4},{6,5},{7,6},{4,7},{9,8},{10,9},{11,1... | collective-permute-start | bytes 790280 | tf_op jit(solution)/shard_map/ppermute | solution.py:181
  39.5 0.0 collective-permute-start.5
  39.5 1.0 %collective-permute-start.4 = (f32[16,4116]{1,0:T(8,128)S(1)}, f32[16,4116]{1,0:T(8,128)S(1)}, u32[]{:S(2)}, u32[]{:S(2)}) collective-permute-start(f32[16,4116]{1,0:T(8,128)S(1)} %last_faces.1.refs_0_), channel_id=1, source_target_pairs={{3,0},{0,1},{1,2},{2,3},{7,4},{4,5},{5,6},{6,7},{11,8},{8,9},{9,10... | collective-permute-start | bytes 790280 | tf_op jit(solution)/shard_map/ppermute | solution.py:181
  40.5 5.9 %collective-permute-done.6.refs_3_ = f32[16,4116]{1,0:T(8,128)S(1)} collective-permute-done((f32[16,4116]{1,0:T(8,128)S(1)}, f32[16,4116]{1,0:T(8,128)S(1)}, u32[]{:S(2)}, u32[]{:S(2)}) %collective-permute-start.6) | collective-permute-done | bytes 263456 | tf_op jit(solution)/shard_map/ppermute | solution.py:181
  46.4 13.4 %collective-permute-done.5.refs_2_ = f32[16,4116]{1,0:T(8,128)S(1)} collective-permute-done((f32[16,4116]{1,0:T(8,128)S(1)}, f32[16,4116]{1,0:T(8,128)S(1)}, u32[]{:S(2)}, u32[]{:S(2)}) %collective-permute-start.5) | collective-permute-done | bytes 263456 | tf_op jit(solution)/shard_map/ppermute | solution.py:181
  59.8 0.0 collective-permute-done.4.refs_1_
  59.8 0.8 %gram.1 = (bf16[128,4352]{1,0:T(8,128)(2,1)S(1)}, f32[64,64]{1,0:T(8,128)S(1)}) custom-call(f32[16,4116]{1,0:T(8,128)S(1)} %last_faces.1.refs_0_, f32[16,4116]{1,0:T(8,128)S(1)} %collective-permute-done.4.refs_1_, f32[16,4116]{1,0:T(8,128)S(1)} %collective-permute-done.5.refs_2_, f32[16,4116]{1,0:T(8,128)S(1)} %collective-permute-done.6.refs_3_), custom_call_target="tpu_custom_call" | custom-call | tf_op jit(solution)/shard_map/gram/pallas_call | solution.py:167
  60.6 0.1 collective-permute-start.7
  60.7 1.2 %collective-permute-done.7 = f32[64,64]{1,0:T(8,128)S(1)} collective-permute-done((f32[64,64]{1,0:T(8,128)S(1)}, f32[64,64]{1,0:T(8,128)S(1)}, u32[]{:S(2)}, u32[]{:S(2)}) %collective-permute-start.7) | collective-permute-done | bytes 16416 | tf_op jit(solution)/shard_map/gram_sum/ppermute | solution.py:293
  61.9 2.7 %collective-permute-start.10 = (f32[64,64]{1,0:T(8,128)S(1)}, f32[64,64]{1,0:T(8,128)S(1)}, u32[]{:S(2)}, u32[]{:S(2)}) collective-permute-start(f32[64,64]{1,0:T(8,128)S(1)} %add.14), channel_id=1, source_target_pairs={{0,24},{4,28},{8,16},{12,20},{16,8},{20,12},{24,0},{28,4},{1,25},{... | collective-permute-start | bytes 49160 | tf_op jit(solution)/shard_map/gram_sum/ppermute | solution.py:293
  64.6 0.5 collective-permute-start.9
  65.1 0.3 collective-permute-start.8
  65.4 1.3 %collective-permute-done.10 = f32[64,64]{1,0:T(8,128)S(1)} collective-permute-done((f32[64,64]{1,0:T(8,128)S(1)}, f32[64,64]{1,0:T(8,128)S(1)}, u32[]{:S(2)}, u32[]{:S(2)}) %collective-permute-start.10) | collective-permute-done | bytes 16416 | tf_op jit(solution)/shard_map/gram_sum/ppermute | solution.py:293
  66.7 1.8 %collective-permute-done.9 = f32[64,64]{1,0:T(8,128)S(1)} collective-permute-done((f32[64,64]{1,0:T(8,128)S(1)}, f32[64,64]{1,0:T(8,128)S(1)}, u32[]{:S(2)}, u32[]{:S(2)}) %collective-permute-start.9) | collective-permute-done | bytes 16416 | tf_op jit(solution)/shard_map/gram_sum/ppermute | solution.py:293
  68.5 0.5 collective-permute-done.8
  69.0 3.3 %orthonormal.1 = f32[16,4116]{1,0:T(8,128)} custom-call(f32[64,64]{1,0:T(8,128)S(1)} %add_add_fusion.gram_ref, bf16[128,4352]{1,0:T(8,128)(2,1)S(1)} %get-tuple-element.18.terms_ref), custom_call_target="tpu_custom_call" | custom-call | tf_op jit(solution)/shard_map/orthonormal/pallas_call | solution.py:167
  (3 shorter events, 0.0 us)
Async XLA Ops:
  0.7 1.0 %copy-start = (f32[16,4116]{1,0:T(8,128)S(1)}, f32[16,4116]{1,0:T(8,128)}, u32[]{:S(2)}) copy-start(f32[16,4116]{1,0:T(8,128)} %psi_ref.7) | copy-start | bytes 790276
  2.0 8.9 %collective-permute-start = (bf16[16,768]{1,0:T(8,128)(2,1)S(1)}, bf16[16,768]{1,0:T(8,128)(2,1)S(1)}, u32[]{:S(2)}, u32[]{:S(2)}) collective-permute-start(bf16[16,768]{1,0:T(8,128)(2,1)S(1)} %face_values.1), channel_id=1, source_target_pairs={{4,0},{8,4},{12,8},{16,12},{20,16},{24,20},{28,24},{0,28},{5,1},{9... | collective-permute-start | bytes 73736 | tf_op jit(solution)/shard_map/ppermute | solution.py:181
  5.4 0.8 %copy-start.1 = (s32[12,512]{1,0:T(8,128)S(1)}, s32[12,512]{1,0:T(8,128)}, u32[]{:S(2)}) copy-start(s32[12,512]{1,0:T(8,128)} %conn_ref.5) | copy-start | bytes 73732
  17.8 2.5 %collective-permute-start.2 = (f32[16,768]{1,0:T(8,128)S(1)}, f32[16,768]{1,0:T(8,128)S(1)}, u32[]{:S(2)}, u32[]{:S(2)}) collective-permute-start(f32[16,768]{1,0:T(8,128)S(1)} %get-tuple-element.14), channel_id=1, source_target_pairs={{4,0},{8,4},{12,8},{16,12},{20,16},{24,20},{28,24},{0,28},{5,1},{9... | collective-permute-start | bytes 147464 | tf_op jit(solution)/shard_map/ppermute | solution.py:181
  18.5 4.4 %collective-permute-start.1 = (f32[16,768]{1,0:T(8,128)S(1)}, f32[16,768]{1,0:T(8,128)S(1)}, u32[]{:S(2)}, u32[]{:S(2)}) collective-permute-start(f32[16,768]{1,0:T(8,128)S(1)} %get-tuple-element.13.upper_in), channel_id=1, source_target_pairs={{28,0},{0,4},{4,8},{8,12},{12,16},{16,20},{20,24},{24,28},{29,1},{... | collective-permute-start | bytes 147464 | tf_op jit(solution)/shard_map/ppermute | solution.py:181
  31.0 4.5 %collective-permute-start.3 = (f32[16,768]{1,0:T(8,128)S(1)}, f32[16,768]{1,0:T(8,128)S(1)}, u32[]{:S(2)}, u32[]{:S(2)}) collective-permute-start(f32[16,768]{1,0:T(8,128)S(1)} %get-tuple-element.16), channel_id=1, source_target_pairs={{28,0},{0,4},{4,8},{8,12},{12,16},{16,20},{20,24},{24,28},{29,1},{... | collective-permute-start | bytes 147464 | tf_op jit(solution)/shard_map/ppermute | solution.py:181
  35.9 10.6 %collective-permute-start.6 = (f32[16,4116]{1,0:T(8,128)S(1)}, f32[16,4116]{1,0:T(8,128)S(1)}, u32[]{:S(2)}, u32[]{:S(2)}) collective-permute-start(f32[16,4116]{1,0:T(8,128)S(1)} %last_faces.1.refs_0_), channel_id=1, source_target_pairs={{1,0},{2,1},{3,2},{0,3},{5,4},{6,5},{7,6},{4,7},{9,8},{10,9},{11,1... | collective-permute-start | bytes 790280 | tf_op jit(solution)/shard_map/ppermute | solution.py:181
  39.5 20.3 %collective-permute-start.5 = (f32[16,4116]{1,0:T(8,128)S(1)}, f32[16,4116]{1,0:T(8,128)S(1)}, u32[]{:S(2)}, u32[]{:S(2)}) collective-permute-start(f32[16,4116]{1,0:T(8,128)S(1)} %last_faces.1.refs_0_), channel_id=1, source_target_pairs={{2,0},{3,1},{0,2},{1,3},{6,4},{7,5},{4,6},{5,7},{10,8},{11,9},{8,1... | collective-permute-start | bytes 790280 | tf_op jit(solution)/shard_map/ppermute | solution.py:181
  39.5 20.3 %collective-permute-start.4 = (f32[16,4116]{1,0:T(8,128)S(1)}, f32[16,4116]{1,0:T(8,128)S(1)}, u32[]{:S(2)}, u32[]{:S(2)}) collective-permute-start(f32[16,4116]{1,0:T(8,128)S(1)} %last_faces.1.refs_0_), channel_id=1, source_target_pairs={{3,0},{0,1},{1,2},{2,3},{7,4},{4,5},{5,6},{6,7},{11,8},{8,9},{9,10... | collective-permute-start | bytes 790280 | tf_op jit(solution)/shard_map/ppermute | solution.py:181
  60.6 1.3 %collective-permute-start.7 = (f32[64,64]{1,0:T(8,128)S(1)}, f32[64,64]{1,0:T(8,128)S(1)}, u32[]{:S(2)}, u32[]{:S(2)}) collective-permute-start(f32[64,64]{1,0:T(8,128)S(1)} %get-tuple-element.17), channel_id=1, source_target_pairs={{0,4},{4,0},{8,12},{12,8},{16,20},{20,16},{24,28},{28,24},{1,5},{5... | collective-permute-start | bytes 49160 | tf_op jit(solution)/shard_map/gram_sum/ppermute | solution.py:293
  61.9 4.8 %collective-permute-start.10 = (f32[64,64]{1,0:T(8,128)S(1)}, f32[64,64]{1,0:T(8,128)S(1)}, u32[]{:S(2)}, u32[]{:S(2)}) collective-permute-start(f32[64,64]{1,0:T(8,128)S(1)} %add.14), channel_id=1, source_target_pairs={{0,24},{4,28},{8,16},{12,20},{16,8},{20,12},{24,0},{28,4},{1,25},{... | collective-permute-start | bytes 49160 | tf_op jit(solution)/shard_map/gram_sum/ppermute | solution.py:293
  64.6 3.9 %collective-permute-start.9 = (f32[64,64]{1,0:T(8,128)S(1)}, f32[64,64]{1,0:T(8,128)S(1)}, u32[]{:S(2)}, u32[]{:S(2)}) collective-permute-start(f32[64,64]{1,0:T(8,128)S(1)} %add.14), channel_id=1, source_target_pairs={{0,16},{4,20},{8,24},{12,28},{16,0},{20,4},{24,8},{28,12},{1,17},{... | collective-permute-start | bytes 49160 | tf_op jit(solution)/shard_map/gram_sum/ppermute | solution.py:293
  65.1 3.9 %collective-permute-start.8 = (f32[64,64]{1,0:T(8,128)S(1)}, f32[64,64]{1,0:T(8,128)S(1)}, u32[]{:S(2)}, u32[]{:S(2)}) collective-permute-start(f32[64,64]{1,0:T(8,128)S(1)} %add.14), channel_id=1, source_target_pairs={{0,8},{4,12},{8,0},{12,4},{16,24},{20,28},{24,16},{28,20},{1,9},{5... | collective-permute-start | bytes 49160 | tf_op jit(solution)/shard_map/gram_sum/ppermute | solution.py:293

commit v3 on v2

v3 whole, which is shorter than its diff:
```python
import functools

import jax
import jax.numpy as jnp
from jax import lax
from jax.experimental import pallas as pl
from jax.experimental.pallas import tpu as pltpu
from jax.sharding import PartitionSpec as P

FACE_EL = 64
IN_EL = 448
STRIDE = 4
LANES = 256

CENTER = 6.25
HALF_WIDTH = 7.5

F32 = jnp.float32
BF16 = jnp.bfloat16
VMEM = pl.BlockSpec(memory_space=pltpu.VMEM)
HBM = pl.BlockSpec(memory_space=pltpu.HBM)
LIMIT = 40 * 1024 * 1024


def round_up(count, unit):
    return -(-count // unit) * unit


def one_hot(low):
    rows = lax.broadcasted_iota(jnp.int32, (LANES, low.shape[1]), 0)
    return jnp.where(rows == low, 1.0, 0.0).astype(BF16)


def stacked(field):
    blocks = field.shape[1] // LANES
    return jnp.concatenate([field[:, i * LANES : (i + 1) * LANES] for i in range(blocks)], axis=0)


def unstacked(rows, bands):
    blocks = rows.shape[0] // bands
    return jnp.concatenate([rows[i * bands : (i + 1) * bands] for i in range(blocks)], axis=1)


def pick(rows, high, low_hot, bands, first=0):
    table = jnp.dot(rows, low_hot, preferred_element_type=F32)
    out = jnp.zeros((bands, low_hot.shape[1]), F32)
    for i in range(rows.shape[0] // bands):
        out = jnp.where(high == i + first, table[i * bands : (i + 1) * bands], out)
    return out


def halves(values):
    upper = values.astype(BF16)
    return upper, (values - upper.astype(F32)).astype(BF16)


def spread(values, high, blocks, first=0):
    rows = []
    for part in halves(values):
        wide = part.astype(F32)
        for i in range(blocks):
            rows.append(jnp.where(high == i + first, wide, 0.0).astype(BF16))
    return jnp.concatenate(rows, axis=0)


def gathered_sum(rows, low_hot):
    both = lax.dot_general(rows, low_hot, (((1,), (1,)), ((), ())), preferred_element_type=F32)
    count = both.shape[0] // 2
    return both[:count] + both[count:]


def chunks(elements):
    return [range(e, min(e + STRIDE, elements)) for e in range(0, elements, STRIDE)]


def packed(ref, width, first, last):
    return jnp.concatenate([ref[e : e + 1, first:last] for e in range(width)], axis=1)


def face_kernel(psi_hbm, conn_hbm, face_hbm, values_ref, psi_out, conn_out, face_out, psi_ref, face_ref, sems):
    bands, nodes = psi_hbm.shape
    copies = [
        pltpu.make_async_copy(face_hbm, face_ref, sems.at[0]),
        pltpu.make_async_copy(psi_hbm, psi_ref, sems.at[1]),
        pltpu.make_async_copy(conn_hbm, conn_out, sems.at[2]),
    ]
    for copy in copies:
        copy.start()
    psi_out[...] = jnp.zeros_like(psi_out)
    face_out[...] = jnp.full_like(face_out, -1)
    copies[0].wait()
    face_out[:, : face_ref.shape[1]] = face_ref[...]
    face = face_out[...]
    hot = one_hot(face & 255)
    copies[1].wait()
    psi_out[:, :nodes] = psi_ref[...]
    values_ref[...] = pick(stacked(psi_out[...]).astype(BF16), face >> 8, hot, bands).astype(BF16)
    copies[2].wait()


def interior_kernel(nodes, psi_ref, conn_ref, ham_hbm, part_ref, ham_ref, slots_ref, ghosts_ref, hots_ref, hosts_ref, sems):
    bands = psi_ref.shape[0]
    elements, size = conn_ref.shape
    copies = [pltpu.make_async_copy(ham_hbm.at[e], ham_ref.at[e], sems.at[e]) for e in range(elements)]
    for copy in copies:
        copy.start()
    slots_ref[...] = packed(conn_ref, elements, 0, IN_EL)
    ghosts_ref[...] = packed(conn_ref, elements, IN_EL, size) - nodes
    hosts_ref[...] = one_hot(ghosts_ref[...] & 255)
    rows = stacked(psi_ref[...]).astype(BF16)
    for group in chunks(elements):
        span = slice(group[0] * IN_EL, (group[-1] + 1) * IN_EL)
        slots = slots_ref[:, span]
        hot = one_hot(slots & 255)
        hots_ref[:, span] = hot
        inside = pick(rows, slots >> 8, hot, bands).astype(BF16)
        for i, e in enumerate(group):
            copies[e].wait()
            part_ref[:, e * size : (e + 1) * size] = jnp.dot(
                inside[:, i * IN_EL : (i + 1) * IN_EL], ham_ref[e, :IN_EL, :], preferred_element_type=F32
            )


def widened(values):
    bands, count = values.shape
    return jnp.concatenate([values, jnp.zeros((bands, round_up(count, LANES) - count), values.dtype)], axis=1)


def first_kernel(
    psi_ref, slots_ref, ghosts_ref, hots_ref, hosts_ref, ham_ref, face_ref, ghost_ref, part_ref,
    own_ref, upper_ref, low_ref, sums,
):
    bands, own = psi_ref.shape
    elements, size = ham_ref.shape[:2]
    face_count = ghost_ref.shape[1]
    ghosts = ghosts_ref[...]
    outside = pick(stacked(widened(ghost_ref[...])), ghosts >> 8, hosts_ref[...], bands).astype(BF16)
    top = []
    for group in chunks(elements):
        inner = []
        for e in group:
            product = part_ref[:, e * size : (e + 1) * size] + jnp.dot(
                outside[:, e * FACE_EL : (e + 1) * FACE_EL], ham_ref[e, IN_EL:, :], preferred_element_type=F32
            )
            inner.append(product[:, :IN_EL])
            top.append(product[:, IN_EL:])
        span = slice(group[0] * IN_EL, (group[-1] + 1) * IN_EL)
        sums[:, span] = spread(jnp.concatenate(inner, axis=1), slots_ref[:, span] >> 8, own // LANES)
    rows = spread(jnp.concatenate(top, axis=1), ghosts >> 8, round_up(face_count, LANES) // LANES)
    upper_ref[...] = unstacked(gathered_sum(rows, hosts_ref[...]), bands)[:, :face_count] / HALF_WIDTH
    total = unstacked(gathered_sum(sums[...], hots_ref[...]), bands)
    current = (total - CENTER * psi_ref[...]) / HALF_WIDTH
    own_ref[...] = current
    face = face_ref[...]
    face_hot = one_hot(face & 255)
    terms = halves(stacked(current))
    low_ref[...] = pick(terms[0], face >> 8, face_hot, bands) + pick(terms[1], face >> 8, face_hot, bands)


def second_kernel(
    slots_ref, ghosts_ref, hots_ref, hosts_ref, ham_ref, face_ref, own_in, upper_in, below_in, above_in,
    own_ref, field_ref, upper_ref,
):
    bands, own = own_in.shape
    elements, size = ham_ref.shape[:2]
    face_count = upper_in.shape[1]
    face = face_ref[...]
    added = gathered_sum(spread(below_in[...], face >> 8, own // LANES), one_hot(face & 255))
    current = own_in[...] + unstacked(added, bands)
    own_ref[...] = current
    rows = stacked(current).astype(BF16)
    ghost = stacked(widened(upper_in[...] + above_in[...])).astype(BF16)
    ghosts = ghosts_ref[...]
    outside = pick(ghost, ghosts >> 8, hosts_ref[...], bands).astype(BF16)
    top = []
    for group in chunks(elements):
        span = slice(group[0] * IN_EL, (group[-1] + 1) * IN_EL)
        inside = pick(rows, slots_ref[:, span] >> 8, hots_ref[:, span], bands).astype(BF16)
        for i, e in enumerate(group):
            values = jnp.concatenate(
                [inside[:, i * IN_EL : (i + 1) * IN_EL], outside[:, e * FACE_EL : (e + 1) * FACE_EL]], axis=1
            )
            field_ref[:, e * size : (e + 1) * size] = values
            product = jnp.dot(values, ham_ref[e, :, size - 128 :], preferred_element_type=F32)
            top.append(product[:, 128 - FACE_EL :])
    sums = spread(jnp.concatenate(top, axis=1), ghosts >> 8, round_up(face_count, LANES) // LANES)
    upper_ref[...] = unstacked(gathered_sum(sums, hosts_ref[...]), bands)[:, :face_count] * (2.0 / HALF_WIDTH)


def third_kernel(psi_ref, slots_ref, hots_ref, ham_ref, own_in, field_ref, own_ref, sums):
    bands, own = own_in.shape
    elements, size = ham_ref.shape[:2]
    for group in chunks(elements):
        inner = []
        for e in group:
            product = jnp.dot(field_ref[:, e * size : (e + 1) * size], ham_ref[e], preferred_element_type=F32)
            inner.append(product[:, :IN_EL])
        span = slice(group[0] * IN_EL, (group[-1] + 1) * IN_EL)
        sums[:, span] = spread(jnp.concatenate(inner, axis=1), slots_ref[:, span] >> 8, own // LANES)
    total = unstacked(gathered_sum(sums[...], hots_ref[...]), bands)
    own_ref[...] = 2.0 * ((total - CENTER * own_in[...]) / HALF_WIDTH) - psi_ref[...]


def last_kernel(own_in, face_ref, below_in, out_ref, short_ref):
    bands, own = own_in.shape
    face = face_ref[...]
    added = gathered_sum(spread(below_in[...], face >> 8, own // LANES), one_hot(face & 255))
    total = own_in[...] + unstacked(added, bands)
    out_ref[...] = total
    short_ref[...] = total.astype(BF16)


def call(kernel, out_shape, inputs, scratch=(), flops=0, moved=0, far=()):
    return pl.pallas_call(
        kernel,
        out_shape=out_shape,
        in_specs=[HBM if i in far else VMEM for i in range(len(inputs))],
        out_specs=jax.tree.map(lambda _: VMEM, out_shape),
        scratch_shapes=list(scratch),
        compiler_params=pltpu.CompilerParams(vmem_limit_bytes=LIMIT),
        cost_estimate=pl.CostEstimate(flops=flops, bytes_accessed=moved, transcendentals=0),
    )(*inputs)


def from_behind(block, axis, distance):
    devices = range(lax.axis_size(axis))
    route = [((i - distance) % len(devices), i) for i in devices]
    return lax.ppermute(block, axis, route)


def filter_field(psi, ham, conn, face_rows):
    bands, nodes = psi.shape
    elements, size = conn.shape
    own = round_up(nodes, LANES)
    faces = round_up(face_rows.shape[0], 128)
    face_count = elements * (size - IN_EL)
    inner_count = elements * IN_EL
    shape = jax.ShapeDtypeStruct
    face_field = shape((bands, faces), F32)
    own_field = shape((bands, own), F32)
    sums = pltpu.VMEM((2 * own // LANES * bands, inner_count), BF16)

    with jax.named_scope("face_values"):
        values, wide, conn, face = call(
            face_kernel,
            (shape((bands, faces), BF16), own_field, shape(conn.shape, jnp.int32), shape((1, faces), jnp.int32)),
            (psi, conn, face_rows[None]),
            (pltpu.VMEM(psi.shape, F32), pltpu.VMEM((1, face_rows.shape[0]), jnp.int32), pltpu.SemaphoreType.DMA((3,))),
            far=(0, 1, 2),
        )
    ghost = from_behind(values, "space", -1)
    with jax.named_scope("interior"):
        part, near, slots, ghosts, hots, hosts = call(
            functools.partial(interior_kernel, nodes),
            (
                shape((bands, elements * size), F32), shape(ham.shape, BF16),
                shape((1, inner_count), jnp.int32), shape((1, face_count), jnp.int32),
                shape((LANES, inner_count), BF16), shape((LANES, face_count), BF16),
            ),
            (wide, conn, ham), (pltpu.SemaphoreType.DMA((elements,)),), flops=4 * 10**9, moved=8 * 10**6, far=(2,),
        )
    with jax.named_scope("first_step"):
        current, upper, low = call(
            first_kernel, (own_field, face_field, face_field),
            (wide, slots, ghosts, hots, hosts, near, face, ghost, part), (sums,), flops=4 * 10**9, moved=10**6,
        )
    below = from_behind(upper, "space", 1)
    above = from_behind(low, "space", -1)
    with jax.named_scope("second_step"):
        current, field, upper = call(
            second_kernel, (own_field, shape((bands, elements * size), BF16), face_field),
            (slots, ghosts, hots, hosts, near, face, current, upper, below, above), flops=4 * 10**9, moved=10**6,
        )
    below = from_behind(upper, "space", 1)
    with jax.named_scope("second_sums"):
        following = call(
            third_kernel, own_field, (wide, slots, hots, near, current, field), (sums,), flops=4 * 10**9, moved=8 * 10**6
        )
    with jax.named_scope("last_faces"):
        return call(last_kernel, (own_field, shape(own_field.shape, BF16)), (following, face, below))


def gram_kernel(*refs):
    *blocks, terms_ref, gram_ref = refs
    bands = blocks[0].shape[0]
    total = bands * len(blocks)
    me = lax.axis_index("band")
    for distance, block in enumerate(blocks):
        source = pl.multiple_of(lax.rem(me - distance + len(blocks), len(blocks)) * bands, bands)
        upper, lower = halves(block[...].astype(F32))
        terms_ref[pl.ds(source, bands), :] = upper
        terms_ref[pl.ds(total + source, bands), :] = lower
    terms = terms_ref[...]
    both = lax.dot_general(terms, terms, (((1,), (1,)), ((), ())), preferred_element_type=F32)
    gram_ref[...] = both[:total, :total] + (both[:total, total:] + both[total:, :total]) + both[total:, total:]


def inverse_factor(matrix, block=8):
    size = matrix.shape[0]
    width = 2 * size
    lane = lax.broadcasted_iota(jnp.int32, (8, width), 1)
    row = lax.broadcasted_iota(jnp.int32, (8, width), 0)
    zero = jnp.zeros((size, size), F32)
    wide = jnp.concatenate([matrix, zero], axis=1)
    groups = [wide[8 * g : 8 * g + 8] + jnp.where(lane == row + (size + 8 * g), 1.0, 0.0) for g in range(size // 8)]
    for k in range(0, size, block):
        start = k // 8
        columns = [
            [jnp.broadcast_to(groups[g][:, k + q : k + q + 1], (8, width)) for g in range(start, size // 8)]
            for q in range(block)
        ]
        for q in range(block):
            at = k + q - 8 * start
            scale = 1.0 / columns[q][0][at : at + 1]
            column = [jnp.where(row > at, columns[q][0], 0.0)] + columns[q][1:]
            for p in range(q + 1, block):
                factor = columns[p][0][at : at + 1] * scale
                columns[p] = [value - weight * factor for value, weight in zip(columns[p], column)]
            factor = groups[start][at : at + 1] * scale
            for g, weight in enumerate(column):
                groups[start + g] = groups[start + g] - weight * factor
    out = []
    for g, rows in enumerate(groups):
        pivot = jnp.sum(jnp.where(lane == row + 8 * g, rows, 0.0), axis=1, keepdims=True)
        out.append(rows[:, size:] / jnp.sqrt(pivot))
    return jnp.concatenate(out, axis=0)


def ortho_kernel(nodes, count, gram_ref, terms_ref, out_ref, inverse_ref):
    bands = out_ref.shape[0]
    inverse_ref[...] = inverse_factor(gram_ref[...] / count)
    first = pl.multiple_of(lax.axis_index("band") * bands, bands)
    upper, lower = halves(inverse_ref[pl.ds(first, bands), :])
    rows = jnp.concatenate(
        [jnp.concatenate([upper, upper], axis=1), jnp.concatenate([lower, lower], axis=1)], axis=0
    )
    both = jnp.dot(rows, terms_ref[...], preferred_element_type=F32)
    out_ref[...] = (both[:bands] + both[bands:])[:, :nodes]


def space_sum(block):
    size = lax.axis_size("space")
    if size & (size - 1):
        return lax.psum(block, "space")
    step = 1
    while step < size:
        span = 2 if step == 1 or step * 2 == size else 4
        parts = [
            lax.ppermute(block, "space", [(i, i ^ (step * k)) for i in range(size)]) for k in range(1, span)
        ]
        block = sum(parts, block)
        step *= span
    return block


def per_device(psi, ham, conn, face_rows):
    bands, nodes = psi.shape
    following, short = filter_field(psi, ham, conn, face_rows)
    groups = lax.axis_size("band")
    total = groups * bands
    own = round_up(nodes, LANES)
    shape = jax.ShapeDtypeStruct
    blocks = [following] + [from_behind(short, "band", i) for i in range(1, groups)]
    with jax.named_scope("gram"):
        terms, gram = call(gram_kernel, (shape((2 * total, own), BF16), shape((total, total), F32)), blocks)
    with jax.named_scope("gram_sum"):
        gram = space_sum(gram)
    with jax.named_scope("orthonormal"):
        return call(
            functools.partial(ortho_kernel, nodes, nodes * lax.axis_size("space")),
            shape((bands, nodes), F32), (gram, terms), (pltpu.VMEM((total, total), F32),),
        )


def solution(mesh):
    placed = (P("band", "space"), P("space", None, None), P("space", None), P("space"))
    return jax.shard_map(
        per_device, mesh=mesh, in_specs=placed, out_specs=P("band", "space"), check_vma=False
    )
```

time: 72.6 us -> 51 us (0.70)
  waiting for transfers between devices: 33 us -> 18.8 us
  Pallas kernels: 24.5 us -> 17 us
    ppermute x7, waiting for transfers between devices: 28.1 us -> 15.2 us  [from_behind(): return lax.ppermute(block, axis, route)]
    pallas_call x7 -> x8, Pallas kernels: 24.5 us -> 17 us  [call(): pl.pallas_call(kernel, out_shape=out_shape, in_specs=[HBM if i in far els...]
    ppermute x4, waiting for transfers between devices: 4.84 us -> 3.6 us  [space_sum(): lax.ppermute(block, 'space', [(i, i ^ step * k) for i in range(size)])]
  transfers between devices with their start and end apart: 11 -> 11, of which waited for: 9 -> 9; matrix products, arithmetic and copies ran while one was open for 0% -> 0% of each run, Pallas kernels for 7% -> 14%
where the time goes in v3:
time: 51 us; the launch traced here: 50.8 us
  waiting for transfers between devices  18.8 us (37%)
  Pallas kernels  17 us (33%)
  starting transfers between devices  12.4 us (24%)
  local copies, waits for them, and re-layouts  2.4 us (5%)
    pallas_call x8, Pallas kernels, call(): pl.pallas_call(kernel, out_shape=out_shape, in_specs=[HBM if i in far els...  17 us
    ppermute x7, waiting for transfers between devices, from_behind(): return lax.ppermute(block, axis, route)  15.2 us
    ppermute x7, starting transfers between devices, from_behind(): return lax.ppermute(block, axis, route)  8.87 us
    ppermute x4, waiting for transfers between devices, space_sum(): lax.ppermute(block, 'space', [(i, i ^ step * k) for i in range(size)])  3.6 us
    ppermute x4, starting transfers between devices, space_sum(): lax.ppermute(block, 'space', [(i, i ^ step * k) for i in range(size)])  3.56 us
    unnamed x4, local copies, waits for them, and re-layouts  1.71 us
  transfers between devices with their start and end apart: 11, of which 9 were waited for; matrix products, arithmetic and copies ran while one was open for 0% of the time, Pallas kernels for 14%

profile of v3, /device:TPU:0, one launch (start us, length us, event | category | flops | bytes accessed | tf_op | source)
XLA Modules:
  0.0 50.8 jit_solution(14734600956961794153)
XLA Ops:
  0.0 0.7 %broadcast_in_dim.3.face_hbm = s32[1,588]{1,0:T(1,128)S(1)} reshape(s32[588]{0:T(1024)} %param.7) | data formatting | bytes 4704 | tf_op jit(solution)/shard_map/face_values/broadcast_in_dim | solution.py:247
  0.7 0.0 copy-start
  0.7 1.0 %copy-done = f32[16,4116]{1,0:T(8,128)S(1)} copy-done((f32[16,4116]{1,0:T(8,128)S(1)}, f32[16,4116]{1,0:T(8,128)}, u32[]{:S(2)}) %copy-start) | copy-done | bytes 263448
  1.6 0.0 copy-start.1
  1.6 0.8 %copy-done.1 = s32[12,512]{1,0:T(8,128)S(1)} copy-done((s32[12,512]{1,0:T(8,128)S(1)}, s32[12,512]{1,0:T(8,128)}, u32[]{:S(2)}) %copy-start.1) | copy-done | bytes 24600
  2.4 0.5 face_values.1
  2.9 3.4 %collective-permute-start = (bf16[16,640]{1,0:T(8,128)(2,1)S(1)}, bf16[16,640]{1,0:T(8,128)(2,1)S(1)}, u32[]{:S(2)}, u32[]{:S(2)}) collective-permute-start(bf16[16,640]{1,0:T(8,128)(2,1)S(1)} %get-tuple-element.33), channel_id=1, source_target_pairs={{4,0},{8,4},{12,8},{16,12},{20,16},{24,20},{28,24},{0,28},{5,1},{9... | collective-permute-start | bytes 61448 | tf_op jit(solution)/shard_map/ppermute | solution.py:228
  6.3 4.7 %interior.1 = (f32[16,6144]{1,0:T(8,128)S(1)}, bf16[12,512,512]{2,1,0:T(8,128)(2,1)S(1)}, s32[1,5376]{1,0:T(1,128)S(1)}, s32[1,768]{1,0:T(1,128)S(1)}, bf16[256,...) custom-call(f32[16,4352]{1,0:T(8,128)S(1)} %get-tuple-element.25.psi_ref, s32[12,512]{1,0:T(8,128)S(1)} %get-tuple-element.26.conn_ref, ...), custom_call_target="tpu_custom_call" | custom-call | flops 4000000000 | bytes 8000000 | tf_op jit(solution)/shard_map/interior/pallas_call | solution.py:214
  11.0 0.0 collective-permute-done.ghost_ref
  11.0 2.9 %first_step.1 = (f32[16,4352]{1,0:T(8,128)S(1)}, f32[16,640]{1,0:T(8,128)S(1)}, f32[16,640]{1,0:T(8,128)S(1)}) custom-call(f32[16,4352]{1,0:T(8,128)S(1)} %get-tuple-element.25.psi_ref, s32[1,5376]{1,0:T(1,128)S(1)} %get-tuple-element.27.slots_ref, s32[1,768]{1,0:T(1,128)S(1)} %get-tuple-element.30.ghosts_ref, ...), custom_call_target="tpu_custom_call" | custom-call | flops 4000000000 | bytes 1000000 | tf_op jit(solution)/shard_map/first_step/pallas_call | solution.py:214
  13.9 0.7 %collective-permute-start.2 = (f32[16,640]{1,0:T(8,128)S(1)}, f32[16,640]{1,0:T(8,128)S(1)}, u32[]{:S(2)}, u32[]{:S(2)}) collective-permute-start(f32[16,640]{1,0:T(8,128)S(1)} %get-tuple-element.37), channel_id=1, source_target_pairs={{4,0},{8,4},{12,8},{16,12},{20,16},{24,20},{28,24},{0,28},{5,1},{9... | collective-permute-start | bytes 122888 | tf_op jit(solution)/shard_map/ppermute | solution.py:228
  14.6 0.0 collective-permute-start.1
  14.6 1.7 %collective-permute-done.2.above_in = f32[16,640]{1,0:T(8,128)S(1)} collective-permute-done((f32[16,640]{1,0:T(8,128)S(1)}, f32[16,640]{1,0:T(8,128)S(1)}, u32[]{:S(2)}, u32[]{:S(2)}) %collective-permute-start.2) | collective-permute-done | bytes 40992 | tf_op jit(solution)/shard_map/ppermute | solution.py:228
  16.3 2.7 %collective-permute-done.1.below_in = f32[16,640]{1,0:T(8,128)S(1)} collective-permute-done((f32[16,640]{1,0:T(8,128)S(1)}, f32[16,640]{1,0:T(8,128)S(1)}, u32[]{:S(2)}, u32[]{:S(2)}) %collective-permute-start.1) | collective-permute-done | bytes 40992 | tf_op jit(solution)/shard_map/ppermute | solution.py:228
  19.0 2.5 %second_step.1 = (f32[16,4352]{1,0:T(8,128)S(1)}, bf16[16,6144]{1,0:T(8,128)(2,1)S(1)}, f32[16,640]{1,0:T(8,128)S(1)}) custom-call(s32[1,5376]{1,0:T(1,128)S(1)} %get-tuple-element.27.slots_ref, s32[1,768]{1,0:T(1,128)S(1)} %get-tuple-element.30.ghosts_ref, bf16[256,5376]{1,0:T(8,128)(2,1)S(1)} %get-tuple-element.28.hots_ref, ...), custom_call_target="tpu_custom_call" | custom-call | flops 4000000000 | bytes 1000000 | tf_op jit(solution)/shard_map/second_step/pallas_call | solution.py:214
  21.4 0.1 collective-permute-start.3
  21.5 2.5 %second_sums.1.own_in = f32[16,4352]{1,0:T(8,128)S(1)} custom-call(f32[16,4352]{1,0:T(8,128)S(1)} %get-tuple-element.25.psi_ref, s32[1,5376]{1,0:T(1,128)S(1)} %get-tuple-element.27.slots_ref, bf16[256,5376]{1,0:T(8,128)(2,1)S(1)} %get-tuple-element.28.hots_ref, bf16[12,512,512]{2,1,0:T(8,128)(2,1)S(1)} %get-tuple-element.29.ham_ref, ...), custom_call_target="tpu_custom_call" | custom-call | flops 4000000000 | bytes 8000000 | tf_op jit(solution)/shard_map/second_sums/pallas_call | solution.py:214
  24.1 1.8 %collective-permute-done.3.below_in = f32[16,640]{1,0:T(8,128)S(1)} collective-permute-done((f32[16,640]{1,0:T(8,128)S(1)}, f32[16,640]{1,0:T(8,128)S(1)}, u32[]{:S(2)}, u32[]{:S(2)}) %collective-permute-start.3) | collective-permute-done | bytes 40992 | tf_op jit(solution)/shard_map/ppermute | solution.py:228
  25.8 0.4 last_faces.1
  26.3 3.7 %collective-permute-start.6 = (bf16[16,4352]{1,0:T(8,128)(2,1)S(1)}, bf16[16,4352]{1,0:T(8,128)(2,1)S(1)}, u32[]{:S(2)}, u32[]{:S(2)}) collective-permute-start(bf16[16,4352]{1,0:T(8,128)(2,1)S(1)} %get-tuple-element.42), channel_id=1, source_target_pairs={{1,0},{2,1},{3,2},{0,3},{5,4},{6,5},{7,6},{4,7},{9,8},{10,9},{11,1... | collective-permute-start | bytes 417800 | tf_op jit(solution)/shard_map/ppermute | solution.py:228
  29.9 0.0 collective-permute-start.5
  29.9 1.0 %collective-permute-start.4 = (bf16[16,4352]{1,0:T(8,128)(2,1)S(1)}, bf16[16,4352]{1,0:T(8,128)(2,1)S(1)}, u32[]{:S(2)}, u32[]{:S(2)}) collective-permute-start(bf16[16,4352]{1,0:T(8,128)(2,1)S(1)} %get-tuple-element.42), channel_id=1, source_target_pairs={{3,0},{0,1},{1,2},{2,3},{7,4},{4,5},{5,6},{6,7},{11,8},{8,9},{9,10... | collective-permute-start | bytes 417800 | tf_op jit(solution)/shard_map/ppermute | solution.py:228
  31.0 2.3 %collective-permute-done.6.refs_3_ = bf16[16,4352]{1,0:T(8,128)(2,1)S(1)} collective-permute-done((bf16[16,4352]{1,0:T(8,128)(2,1)S(1)}, bf16[16,4352]{1,0:T(8,128)(2,1)S(1)}, u32[]{:S(2)}, u32[]{:S(2)}) %collective-permute-start.6) | collective-permute-done | bytes 139296 | tf_op jit(solution)/shard_map/ppermute | solution.py:228
  33.2 6.8 %collective-permute-done.5.refs_2_ = bf16[16,4352]{1,0:T(8,128)(2,1)S(1)} collective-permute-done((bf16[16,4352]{1,0:T(8,128)(2,1)S(1)}, bf16[16,4352]{1,0:T(8,128)(2,1)S(1)}, u32[]{:S(2)}, u32[]{:S(2)}) %collective-permute-start.5) | collective-permute-done | bytes 139296 | tf_op jit(solution)/shard_map/ppermute | solution.py:228
  40.1 0.0 collective-permute-done.4.refs_1_
  40.1 0.8 %gram.1 = (bf16[128,4352]{1,0:T(8,128)(2,1)S(1)}, f32[64,64]{1,0:T(8,128)S(1)}) custom-call(f32[16,4352]{1,0:T(8,128)S(1)} %get-tuple-element.41.refs_0_, bf16[16,4352]{1,0:T(8,128)(2,1)S(1)} %collective-permute-done.4.refs_1_, bf16[16,4352]{1,0:T(8,128)(2,1)S(1)} %collective-permute-done.5.refs_2_, bf16[16,4352]{1,0:T(8,128)(2,1)S(1)} %collective-permute-done.6.refs_3_), custom_call_target="tpu_custom_call" | custom-call | tf_op jit(solution)/shard_map/gram/pallas_call | solution.py:214
  40.9 0.1 collective-permute-start.7
  41.0 1.2 %collective-permute-done.7 = f32[64,64]{1,0:T(8,128)S(1)} collective-permute-done((f32[64,64]{1,0:T(8,128)S(1)}, f32[64,64]{1,0:T(8,128)S(1)}, u32[]{:S(2)}, u32[]{:S(2)}) %collective-permute-start.7) | collective-permute-done | bytes 16416 | tf_op jit(solution)/shard_map/gram_sum/ppermute | solution.py:349
  42.2 1.7 %collective-permute-start.10 = (f32[64,64]{1,0:T(8,128)S(1)}, f32[64,64]{1,0:T(8,128)S(1)}, u32[]{:S(2)}, u32[]{:S(2)}) collective-permute-start(f32[64,64]{1,0:T(8,128)S(1)} %add.12), channel_id=1, source_target_pairs={{0,24},{4,28},{8,16},{12,20},{16,8},{20,12},{24,0},{28,4},{1,25},{... | collective-permute-start | bytes 49160 | tf_op jit(solution)/shard_map/gram_sum/ppermute | solution.py:349
  43.8 0.3 collective-permute-start.9
  44.1 1.5 %collective-permute-start.8 = (f32[64,64]{1,0:T(8,128)S(1)}, f32[64,64]{1,0:T(8,128)S(1)}, u32[]{:S(2)}, u32[]{:S(2)}) collective-permute-start(f32[64,64]{1,0:T(8,128)S(1)} %add.12), channel_id=1, source_target_pairs={{0,8},{4,12},{8,0},{12,4},{16,24},{20,28},{24,16},{28,20},{1,9},{5... | collective-permute-start | bytes 49160 | tf_op jit(solution)/shard_map/gram_sum/ppermute | solution.py:349
  45.7 1.4 %collective-permute-done.10 = f32[64,64]{1,0:T(8,128)S(1)} collective-permute-done((f32[64,64]{1,0:T(8,128)S(1)}, f32[64,64]{1,0:T(8,128)S(1)}, u32[]{:S(2)}, u32[]{:S(2)}) %collective-permute-start.10) | collective-permute-done | bytes 16416 | tf_op jit(solution)/shard_map/gram_sum/ppermute | solution.py:349
  47.1 0.7 %collective-permute-done.9 = f32[64,64]{1,0:T(8,128)S(1)} collective-permute-done((f32[64,64]{1,0:T(8,128)S(1)}, f32[64,64]{1,0:T(8,128)S(1)}, u32[]{:S(2)}, u32[]{:S(2)}) %collective-permute-start.9) | collective-permute-done | bytes 16416 | tf_op jit(solution)/shard_map/gram_sum/ppermute | solution.py:349
  47.8 0.3 collective-permute-done.8
  48.1 2.7 %orthonormal.1 = f32[16,4116]{1,0:T(8,128)} custom-call(f32[64,64]{1,0:T(8,128)S(1)} %add_add_fusion.gram_ref, bf16[128,4352]{1,0:T(8,128)(2,1)S(1)} %get-tuple-element.44.terms_ref), custom_call_target="tpu_custom_call" | custom-call | tf_op jit(solution)/shard_map/orthonormal/pallas_call | solution.py:214
  (2 shorter events, 0.0 us)
Async XLA Ops:
  0.7 1.0 %copy-start = (f32[16,4116]{1,0:T(8,128)S(1)}, f32[16,4116]{1,0:T(8,128)}, u32[]{:S(2)}) copy-start(f32[16,4116]{1,0:T(8,128)} %psi_hbm.1) | copy-start | bytes 790276
  1.6 0.8 %copy-start.1 = (s32[12,512]{1,0:T(8,128)S(1)}, s32[12,512]{1,0:T(8,128)}, u32[]{:S(2)}) copy-start(s32[12,512]{1,0:T(8,128)} %conn_hbm.1) | copy-start | bytes 73732
  2.9 8.1 %collective-permute-start = (bf16[16,640]{1,0:T(8,128)(2,1)S(1)}, bf16[16,640]{1,0:T(8,128)(2,1)S(1)}, u32[]{:S(2)}, u32[]{:S(2)}) collective-permute-start(bf16[16,640]{1,0:T(8,128)(2,1)S(1)} %get-tuple-element.33), channel_id=1, source_target_pairs={{4,0},{8,4},{12,8},{16,12},{20,16},{24,20},{28,24},{0,28},{5,1},{9... | collective-permute-start | bytes 61448 | tf_op jit(solution)/shard_map/ppermute | solution.py:228
  13.9 2.4 %collective-permute-start.2 = (f32[16,640]{1,0:T(8,128)S(1)}, f32[16,640]{1,0:T(8,128)S(1)}, u32[]{:S(2)}, u32[]{:S(2)}) collective-permute-start(f32[16,640]{1,0:T(8,128)S(1)} %get-tuple-element.37), channel_id=1, source_target_pairs={{4,0},{8,4},{12,8},{16,12},{20,16},{24,20},{28,24},{0,28},{5,1},{9... | collective-permute-start | bytes 122888 | tf_op jit(solution)/shard_map/ppermute | solution.py:228
  14.6 4.3 %collective-permute-start.1 = (f32[16,640]{1,0:T(8,128)S(1)}, f32[16,640]{1,0:T(8,128)S(1)}, u32[]{:S(2)}, u32[]{:S(2)}) collective-permute-start(f32[16,640]{1,0:T(8,128)S(1)} %get-tuple-element.36.upper_in), channel_id=1, source_target_pairs={{28,0},{0,4},{4,8},{8,12},{12,16},{16,20},{20,24},{24,28},{29,1},{... | collective-permute-start | bytes 122888 | tf_op jit(solution)/shard_map/ppermute | solution.py:228
  21.4 4.4 %collective-permute-start.3 = (f32[16,640]{1,0:T(8,128)S(1)}, f32[16,640]{1,0:T(8,128)S(1)}, u32[]{:S(2)}, u32[]{:S(2)}) collective-permute-start(f32[16,640]{1,0:T(8,128)S(1)} %get-tuple-element.40), channel_id=1, source_target_pairs={{28,0},{0,4},{4,8},{8,12},{12,16},{16,20},{20,24},{24,28},{29,1},{... | collective-permute-start | bytes 122888 | tf_op jit(solution)/shard_map/ppermute | solution.py:228
  26.3 7.0 %collective-permute-start.6 = (bf16[16,4352]{1,0:T(8,128)(2,1)S(1)}, bf16[16,4352]{1,0:T(8,128)(2,1)S(1)}, u32[]{:S(2)}, u32[]{:S(2)}) collective-permute-start(bf16[16,4352]{1,0:T(8,128)(2,1)S(1)} %get-tuple-element.42), channel_id=1, source_target_pairs={{1,0},{2,1},{3,2},{0,3},{5,4},{6,5},{7,6},{4,7},{9,8},{10,9},{11,1... | collective-permute-start | bytes 417800 | tf_op jit(solution)/shard_map/ppermute | solution.py:228
  29.9 10.1 %collective-permute-start.5 = (bf16[16,4352]{1,0:T(8,128)(2,1)S(1)}, bf16[16,4352]{1,0:T(8,128)(2,1)S(1)}, u32[]{:S(2)}, u32[]{:S(2)}) collective-permute-start(bf16[16,4352]{1,0:T(8,128)(2,1)S(1)} %get-tuple-element.42), channel_id=1, source_target_pairs={{2,0},{3,1},{0,2},{1,3},{6,4},{7,5},{4,6},{5,7},{10,8},{11,9},{8,1... | collective-permute-start | bytes 417800 | tf_op jit(solution)/shard_map/ppermute | solution.py:228
  29.9 10.1 %collective-permute-start.4 = (bf16[16,4352]{1,0:T(8,128)(2,1)S(1)}, bf16[16,4352]{1,0:T(8,128)(2,1)S(1)}, u32[]{:S(2)}, u32[]{:S(2)}) collective-permute-start(bf16[16,4352]{1,0:T(8,128)(2,1)S(1)} %get-tuple-element.42), channel_id=1, source_target_pairs={{3,0},{0,1},{1,2},{2,3},{7,4},{4,5},{5,6},{6,7},{11,8},{8,9},{9,10... | collective-permute-start | bytes 417800 | tf_op jit(solution)/shard_map/ppermute | solution.py:228
  40.9 1.3 %collective-permute-start.7 = (f32[64,64]{1,0:T(8,128)S(1)}, f32[64,64]{1,0:T(8,128)S(1)}, u32[]{:S(2)}, u32[]{:S(2)}) collective-permute-start(f32[64,64]{1,0:T(8,128)S(1)} %get-tuple-element.43), channel_id=1, source_target_pairs={{0,4},{4,0},{8,12},{12,8},{16,20},{20,16},{24,28},{28,24},{1,5},{5... | collective-permute-start | bytes 49160 | tf_op jit(solution)/shard_map/gram_sum/ppermute | solution.py:349
  42.2 4.9 %collective-permute-start.10 = (f32[64,64]{1,0:T(8,128)S(1)}, f32[64,64]{1,0:T(8,128)S(1)}, u32[]{:S(2)}, u32[]{:S(2)}) collective-permute-start(f32[64,64]{1,0:T(8,128)S(1)} %add.12), channel_id=1, source_target_pairs={{0,24},{4,28},{8,16},{12,20},{16,8},{20,12},{24,0},{28,4},{1,25},{... | collective-permute-start | bytes 49160 | tf_op jit(solution)/shard_map/gram_sum/ppermute | solution.py:349
  43.8 3.9 %collective-permute-start.9 = (f32[64,64]{1,0:T(8,128)S(1)}, f32[64,64]{1,0:T(8,128)S(1)}, u32[]{:S(2)}, u32[]{:S(2)}) collective-permute-start(f32[64,64]{1,0:T(8,128)S(1)} %add.12), channel_id=1, source_target_pairs={{0,16},{4,20},{8,24},{12,28},{16,0},{20,4},{24,8},{28,12},{1,17},{... | collective-permute-start | bytes 49160 | tf_op jit(solution)/shard_map/gram_sum/ppermute | solution.py:349
  44.1 3.9 %collective-permute-start.8 = (f32[64,64]{1,0:T(8,128)S(1)}, f32[64,64]{1,0:T(8,128)S(1)}, u32[]{:S(2)}, u32[]{:S(2)}) collective-permute-start(f32[64,64]{1,0:T(8,128)S(1)} %add.12), channel_id=1, source_target_pairs={{0,8},{4,12},{8,0},{12,4},{16,24},{20,28},{24,16},{28,20},{1,9},{5... | collective-permute-start | bytes 49160 | tf_op jit(solution)/shard_map/gram_sum/ppermute | solution.py:349

commit v4 on v3

--- a/solution.py
+++ b/solution.py
@@ -9,7 +9,6 @@
 
 FACE_EL = 64
 IN_EL = 448
-STRIDE = 4
 LANES = 256
 
 CENTER = 6.25
@@ -69,8 +68,42 @@
     return both[:count] + both[count:]
 
 
-def chunks(elements):
-    return [range(e, min(e + STRIDE, elements)) for e in range(0, elements, STRIDE)]
+def tiles(count, width=LANES):
+    return [slice(start, min(start + width, count)) for start in range(0, count, width)]
+
+
+def hot_into(hots_ref, low):
+    for tile in tiles(low.shape[1]):
+        hots_ref[:, tile] = one_hot(low[:, tile])
+
+
+def pick_into(out_ref, rows, high, hots_ref):
+    for tile in tiles(high.shape[1]):
+        out_ref[:, tile] = pick(rows, high[:, tile], hots_ref[:, tile], out_ref.shape[0]).astype(out_ref.dtype)
+
+
+def spread_into(sums_ref, values_ref, high):
+    bands = values_ref.shape[0]
+    blocks = sums_ref.shape[0] // (2 * bands)
+    for tile in tiles(high.shape[1]):
+        at = high[:, tile]
+        upper, lower = (part.astype(F32) for part in halves(values_ref[:, tile]))
+        for i in range(blocks):
+            here = at == i
+            sums_ref[i * bands : (i + 1) * bands, tile] = jnp.where(here, upper, 0.0).astype(BF16)
+            sums_ref[(blocks + i) * bands : (blocks + i + 1) * bands, tile] = jnp.where(here, lower, 0.0).astype(BF16)
+
+
+def split_products(products, inner_ref, top_ref, first):
+    inner = jnp.concatenate([product[:, :IN_EL] for product in products], axis=1)
+    top = jnp.concatenate([product[:, IN_EL:] for product in products], axis=1)
+    inner_ref[:, first * IN_EL : first * IN_EL + inner.shape[1]] = inner
+    if top_ref is not None:
+        top_ref[:, first * FACE_EL : first * FACE_EL + top.shape[1]] = top
+
+
+def pairs(elements):
+    return [range(e, min(e + 2, elements)) for e in range(0, elements, 2)]
 
 
 def packed(ref, width, first, last):
@@ -89,7 +122,7 @@
     psi_out[...] = jnp.zeros_like(psi_out)
     face_out[...] = jnp.full_like(face_out, -1)
     copies[0].wait()
-    face_out[:, : face_ref.shape[1]] = face_ref[...]
+    face_out[:, : face_ref.shape[0]] = face_ref[...].reshape(1, face_ref.shape[0])
     face = face_out[...]
     hot = one_hot(face & 255)
     copies[1].wait()
@@ -98,56 +131,52 @@
     copies[2].wait()
 
 
-def interior_kernel(nodes, psi_ref, conn_ref, ham_hbm, part_ref, ham_ref, slots_ref, ghosts_ref, hots_ref, hosts_ref, sems):
-    bands = psi_ref.shape[0]
+def interior_kernel(
+    nodes, psi_ref, conn_ref, ham_hbm, part_ref, ham_ref, slots_ref, ghosts_ref, hots_ref, hosts_ref, inside_ref, sems
+):
     elements, size = conn_ref.shape
     copies = [pltpu.make_async_copy(ham_hbm.at[e], ham_ref.at[e], sems.at[e]) for e in range(elements)]
     for copy in copies:
         copy.start()
     slots_ref[...] = packed(conn_ref, elements, 0, IN_EL)
     ghosts_ref[...] = packed(conn_ref, elements, IN_EL, size) - nodes
-    hosts_ref[...] = one_hot(ghosts_ref[...] & 255)
-    rows = stacked(psi_ref[...]).astype(BF16)
-    for group in chunks(elements):
-        span = slice(group[0] * IN_EL, (group[-1] + 1) * IN_EL)
-        slots = slots_ref[:, span]
-        hot = one_hot(slots & 255)
-        hots_ref[:, span] = hot
-        inside = pick(rows, slots >> 8, hot, bands).astype(BF16)
-        for i, e in enumerate(group):
-            copies[e].wait()
-            part_ref[:, e * size : (e + 1) * size] = jnp.dot(
-                inside[:, i * IN_EL : (i + 1) * IN_EL], ham_ref[e, :IN_EL, :], preferred_element_type=F32
-            )
+    hot_into(hosts_ref, ghosts_ref[...] & 255)
+    slots = slots_ref[...]
+    hot_into(hots_ref, slots & 255)
+    pick_into(inside_ref, stacked(psi_ref[...]).astype(BF16), slots >> 8, hots_ref)
+    for e in range(elements):
+        copies[e].wait()
+        part_ref[:, e * size : (e + 1) * size] = jnp.dot(
+            inside_ref[:, e * IN_EL : (e + 1) * IN_EL], ham_ref[e, :IN_EL, :], preferred_element_type=F32
+        )
 
 
 def widened(values):
     bands, count = values.shape
+    if count % LANES == 0:
+        return values
     return jnp.concatenate([values, jnp.zeros((bands, round_up(count, LANES) - count), values.dtype)], axis=1)
 
 
 def first_kernel(
     psi_ref, slots_ref, ghosts_ref, hots_ref, hosts_ref, ham_ref, face_ref, ghost_ref, part_ref,
-    own_ref, upper_ref, low_ref, sums,
+    own_ref, upper_ref, low_ref, sums, top_sums, inner, top, outside,
 ):
     bands, own = psi_ref.shape
     elements, size = ham_ref.shape[:2]
     face_count = ghost_ref.shape[1]
     ghosts = ghosts_ref[...]
-    outside = pick(stacked(widened(ghost_ref[...])), ghosts >> 8, hosts_ref[...], bands).astype(BF16)
-    top = []
-    for group in chunks(elements):
-        inner = []
-        for e in group:
-            product = part_ref[:, e * size : (e + 1) * size] + jnp.dot(
-                outside[:, e * FACE_EL : (e + 1) * FACE_EL], ham_ref[e, IN_EL:, :], preferred_element_type=F32
-            )
-            inner.append(product[:, :IN_EL])
-            top.append(product[:, IN_EL:])
-        span = slice(group[0] * IN_EL, (group[-1] + 1) * IN_EL)
-        sums[:, span] = spread(jnp.concatenate(inner, axis=1), slots_ref[:, span] >> 8, own // LANES)
-    rows = spread(jnp.concatenate(top, axis=1), ghosts >> 8, round_up(face_count, LANES) // LANES)
-    upper_ref[...] = unstacked(gathered_sum(rows, hosts_ref[...]), bands)[:, :face_count] / HALF_WIDTH
+    pick_into(outside, stacked(widened(ghost_ref[...])), ghosts >> 8, hosts_ref)
+    for pair in pairs(elements):
+        products = [
+            part_ref[:, e * size : (e + 1) * size]
+            + jnp.dot(outside[:, e * FACE_EL : (e + 1) * FACE_EL], ham_ref[e, IN_EL:, :], preferred_element_type=F32)
+            for e in pair
+        ]
+        split_products(products, inner, top, pair[0])
+    spread_into(sums, inner, slots_ref[...] >> 8)
+    spread_into(top_sums, top, ghosts >> 8)
+    upper_ref[...] = unstacked(gathered_sum(top_sums[...], hosts_ref[...]), bands)[:, :face_count] / HALF_WIDTH
     total = unstacked(gathered_sum(sums[...], hots_ref[...]), bands)
     current = (total - CENTER * psi_ref[...]) / HALF_WIDTH
     own_ref[...] = current
@@ -157,48 +186,71 @@
     low_ref[...] = pick(terms[0], face >> 8, face_hot, bands) + pick(terms[1], face >> 8, face_hot, bands)
 
 
+def far_kernel(own_in, slots_ref, hots_ref, face_ref, inside_ref, high_ref, faces_ref):
+    bands, own = own_in.shape
+    blocks = round_up(own // LANES, 16)
+    face = face_ref[...]
+    number = lax.broadcasted_iota(jnp.int32, (blocks, face.shape[1]), 1)
+    held = lax.broadcasted_iota(jnp.int32, number.shape, 0) == (face >> 8)
+    digits = [jnp.where(held, digit, 0).astype(F32).astype(BF16) for digit in ((number >> 8) + 1, number & 255)]
+    table = lax.dot_general(
+        jnp.concatenate(digits, axis=0), one_hot(face & 255), (((1,), (1,)), ((), ())), preferred_element_type=F32
+    ).astype(BF16)
+    rows = stacked(own_in[...]).astype(BF16)
+    for tile in tiles(slots_ref.shape[1]):
+        high = slots_ref[:, tile] >> 8
+        hot = hots_ref[:, tile]
+        both = jnp.dot(table, hot, preferred_element_type=F32)
+        held = lax.broadcasted_iota(jnp.int32, (blocks, both.shape[1]), 0) == high
+        block = jnp.sum(jnp.where(held, both[:blocks], 0.0), axis=0, keepdims=True).astype(jnp.int32)
+        lane = jnp.sum(jnp.where(held, both[blocks:], 0.0), axis=0, keepdims=True).astype(jnp.int32)
+        high_ref[:, tile] = block - 1
+        faces_ref[:, tile] = one_hot(jnp.where(block > 0, lane, -1))
+        inside_ref[:, tile] = jnp.where(block > 0, 0.0, pick(rows, high, hot, bands)).astype(BF16)
+
+
 def second_kernel(
-    slots_ref, ghosts_ref, hots_ref, hosts_ref, ham_ref, face_ref, own_in, upper_in, below_in, above_in,
-    own_ref, field_ref, upper_ref,
+    inside_ref, high_ref, faces_ref, ghosts_ref, hosts_ref, ham_ref, low_in, upper_in, below_in, above_in,
+    field_ref, upper_ref, top_sums, inside, top, outside,
 ):
-    bands, own = own_in.shape
+    bands, face_count = upper_in.shape
     elements, size = ham_ref.shape[:2]
-    face_count = upper_in.shape[1]
-    face = face_ref[...]
-    added = gathered_sum(spread(below_in[...], face >> 8, own // LANES), one_hot(face & 255))
-    current = own_in[...] + unstacked(added, bands)
-    own_ref[...] = current
-    rows = stacked(current).astype(BF16)
+    faces = stacked(widened(low_in[...] + below_in[...])).astype(BF16)
     ghost = stacked(widened(upper_in[...] + above_in[...])).astype(BF16)
     ghosts = ghosts_ref[...]
-    outside = pick(ghost, ghosts >> 8, hosts_ref[...], bands).astype(BF16)
-    top = []
-    for group in chunks(elements):
-        span = slice(group[0] * IN_EL, (group[-1] + 1) * IN_EL)
-        inside = pick(rows, slots_ref[:, span] >> 8, hots_ref[:, span], bands).astype(BF16)
-        for i, e in enumerate(group):
+    pick_into(outside, ghost, ghosts >> 8, hosts_ref)
+    for tile in tiles(high_ref.shape[1]):
+        extra = pick(faces, high_ref[:, tile], faces_ref[:, tile], bands)
+        inside[:, tile] = inside_ref[:, tile] + extra.astype(BF16)
+    for pair in pairs(elements):
+        products = []
+        for e in pair:
             values = jnp.concatenate(
-                [inside[:, i * IN_EL : (i + 1) * IN_EL], outside[:, e * FACE_EL : (e + 1) * FACE_EL]], axis=1
+                [inside[:, e * IN_EL : (e + 1) * IN_EL], outside[:, e * FACE_EL : (e + 1) * FACE_EL]], axis=1
             )
             field_ref[:, e * size : (e + 1) * size] = values
             product = jnp.dot(values, ham_ref[e, :, size - 128 :], preferred_element_type=F32)
-            top.append(product[:, 128 - FACE_EL :])
-    sums = spread(jnp.concatenate(top, axis=1), ghosts >> 8, round_up(face_count, LANES) // LANES)
-    upper_ref[...] = unstacked(gathered_sum(sums, hosts_ref[...]), bands)[:, :face_count] * (2.0 / HALF_WIDTH)
-
-
-def third_kernel(psi_ref, slots_ref, hots_ref, ham_ref, own_in, field_ref, own_ref, sums):
+            products.append(product[:, 128 - FACE_EL :])
+        top[:, pair[0] * FACE_EL : (pair[-1] + 1) * FACE_EL] = jnp.concatenate(products, axis=1)
+    spread_into(top_sums, top, ghosts >> 8)
+    total = unstacked(gathered_sum(top_sums[...], hosts_ref[...]), bands)
+    upper_ref[...] = total[:, :face_count] * (2.0 / HALF_WIDTH)
+
+
+def third_kernel(psi_ref, slots_ref, hots_ref, ham_ref, face_ref, own_in, below_in, field_ref, own_ref, sums, inner):
     bands, own = own_in.shape
     elements, size = ham_ref.shape[:2]
-    for group in chunks(elements):
-        inner = []
-        for e in group:
-            product = jnp.dot(field_ref[:, e * size : (e + 1) * size], ham_ref[e], preferred_element_type=F32)
-            inner.append(product[:, :IN_EL])
-        span = slice(group[0] * IN_EL, (group[-1] + 1) * IN_EL)
-        sums[:, span] = spread(jnp.concatenate(inner, axis=1), slots_ref[:, span] >> 8, own // LANES)
+    face = face_ref[...]
+    added = gathered_sum(spread(below_in[...], face >> 8, own // LANES), one_hot(face & 255))
+    for pair in pairs(elements):
+        products = [
+            jnp.dot(field_ref[:, e * size : (e + 1) * size], ham_ref[e], preferred_element_type=F32) for e in pair
+        ]
+        split_products(products, inner, None, pair[0])
+    spread_into(sums, inner, slots_ref[...] >> 8)
     total = unstacked(gathered_sum(sums[...], hots_ref[...]), bands)
-    own_ref[...] = 2.0 * ((total - CENTER * own_in[...]) / HALF_WIDTH) - psi_ref[...]
+    current = own_in[...] + unstacked(added, bands)
+    own_ref[...] = 2.0 * ((total - CENTER * current) / HALF_WIDTH) - psi_ref[...]
 
 
 def last_kernel(own_in, face_ref, below_in, out_ref, short_ref):
@@ -207,7 +259,7 @@
     added = gathered_sum(spread(below_in[...], face >> 8, own // LANES), one_hot(face & 255))
     total = own_in[...] + unstacked(added, bands)
     out_ref[...] = total
-    short_ref[...] = total.astype(BF16)
+    short_ref[...] = total[:, : short_ref.shape[1]].astype(BF16)
 
 
 def call(kernel, out_shape, inputs, scratch=(), flops=0, moved=0, far=()):
@@ -233,19 +285,25 @@
     elements, size = conn.shape
     own = round_up(nodes, LANES)
     faces = round_up(face_rows.shape[0], 128)
+    trimmed = round_up(nodes, 128)
     face_count = elements * (size - IN_EL)
     inner_count = elements * IN_EL
     shape = jax.ShapeDtypeStruct
     face_field = shape((bands, faces), F32)
     own_field = shape((bands, own), F32)
     sums = pltpu.VMEM((2 * own // LANES * bands, inner_count), BF16)
+    top_sums = pltpu.VMEM((2 * round_up(faces, LANES) // LANES * bands, face_count), BF16)
+    inner = pltpu.VMEM((bands, inner_count), F32)
+    top = pltpu.VMEM((bands, face_count), F32)
+    inside_field = pltpu.VMEM((bands, inner_count), BF16)
+    outside = pltpu.VMEM((bands, face_count), BF16)
 
     with jax.named_scope("face_values"):
         values, wide, conn, face = call(
             face_kernel,
             (shape((bands, faces), BF16), own_field, shape(conn.shape, jnp.int32), shape((1, faces), jnp.int32)),
-            (psi, conn, face_rows[None]),
-            (pltpu.VMEM(psi.shape, F32), pltpu.VMEM((1, face_rows.shape[0]), jnp.int32), pltpu.SemaphoreType.DMA((3,))),
+            [pltpu.with_memory_space_constraint(array, pltpu.HBM) for array in (psi, conn, face_rows)],
+            (pltpu.VMEM(psi.shape, F32), pltpu.VMEM(face_rows.shape, jnp.int32), pltpu.SemaphoreType.DMA((3,))),
             far=(0, 1, 2),
         )
     ghost = from_behind(values, "space", -1)
@@ -257,27 +315,36 @@
                 shape((1, inner_count), jnp.int32), shape((1, face_count), jnp.int32),
                 shape((LANES, inner_count), BF16), shape((LANES, face_count), BF16),
             ),
-            (wide, conn, ham), (pltpu.SemaphoreType.DMA((elements,)),), flops=4 * 10**9, moved=8 * 10**6, far=(2,),
+            (wide, conn, ham), (inside_field, pltpu.SemaphoreType.DMA((elements,))), flops=4 * 10**9, moved=8 * 10**6, far=(2,),
         )
     with jax.named_scope("first_step"):
         current, upper, low = call(
             first_kernel, (own_field, face_field, face_field),
-            (wide, slots, ghosts, hots, hosts, near, face, ghost, part), (sums,), flops=4 * 10**9, moved=10**6,
+            (wide, slots, ghosts, hots, hosts, near, face, ghost, part), (sums, top_sums, inner, top, outside),
+            flops=4 * 10**9, moved=10**6,
         )
     below = from_behind(upper, "space", 1)
     above = from_behind(low, "space", -1)
+    with jax.named_scope("off_face"):
+        inside, high, faces = call(
+            far_kernel,
+            (shape((bands, inner_count), BF16), shape((1, inner_count), jnp.int32), shape((LANES, inner_count), BF16)),
+            (current, slots, hots, face), flops=4 * 10**9, moved=10**6,
+        )
     with jax.named_scope("second_step"):
-        current, field, upper = call(
-            second_kernel, (own_field, shape((bands, elements * size), BF16), face_field),
-            (slots, ghosts, hots, hosts, near, face, current, upper, below, above), flops=4 * 10**9, moved=10**6,
-        )
-    below = from_behind(upper, "space", 1)
+        field, upper = call(
+            second_kernel, (shape((bands, elements * size), BF16), face_field),
+            (inside, high, faces, ghosts, hosts, near, low, upper, below, above), (top_sums, inside_field, top, outside),
+            flops=4 * 10**9, moved=10**6,
+        )
+    from_below = from_behind(upper, "space", 1)
     with jax.named_scope("second_sums"):
         following = call(
-            third_kernel, own_field, (wide, slots, hots, near, current, field), (sums,), flops=4 * 10**9, moved=8 * 10**6
+            third_kernel, own_field, (wide, slots, hots, near, face, current, below, field), (sums, inner),
+            flops=4 * 10**9, moved=8 * 10**6,
         )
     with jax.named_scope("last_faces"):
-        return call(last_kernel, (own_field, shape(own_field.shape, BF16)), (following, face, below))
+        return call(last_kernel, (own_field, shape((bands, trimmed), BF16)), (following, face, from_below))
 
 
 def gram_kernel(*refs):
@@ -287,7 +354,7 @@
     me = lax.axis_index("band")
     for distance, block in enumerate(blocks):
         source = pl.multiple_of(lax.rem(me - distance + len(blocks), len(blocks)) * bands, bands)
-        upper, lower = halves(block[...].astype(F32))
+        upper, lower = halves(widened(block[...].astype(F32)))
         terms_ref[pl.ds(source, bands), :] = upper
         terms_ref[pl.ds(total + source, bands), :] = lower
     terms = terms_ref[...]

time: 51 us -> 49.8 us (0.976)
  waiting for transfers between devices: 18.8 us -> 15.4 us
  starting transfers between devices: 12.4 us -> 15 us
  local copies, waits for them, and re-layouts: 2.4 us -> 0 us
  Pallas kernels: 17 us -> 19.1 us
    ppermute x7, waiting for transfers between devices: 15.2 us -> 10.4 us  [from_behind(): return lax.ppermute(block, axis, route)]
    pallas_call x8 -> x9, Pallas kernels: 17 us -> 19.1 us  [call(): pl.pallas_call(kernel, out_shape=out_shape, in_specs=[HBM if i in far els...]
    ppermute x7, starting transfers between devices: 8.87 us -> 10.8 us  [from_behind(): return lax.ppermute(block, axis, route)]
    unnamed x4 -> x0, local copies, waits for them, and re-layouts: 1.71 us -> none
    ppermute x4, waiting for transfers between devices: 3.6 us -> 5 us  [space_sum(): lax.ppermute(block, 'space', [(i, i ^ step * k) for i in range(size)])]
    broadcast_in_dim x1 -> x0, local copies, waits for them, and re-layouts: 0.69 us -> none  [filter_field(): face_rows[None]]
    ppermute x4, starting transfers between devices: 3.56 us -> 4.22 us  [space_sum(): lax.ppermute(block, 'space', [(i, i ^ step * k) for i in range(size)])]
  transfers between devices with their start and end apart: 11 -> 11, of which waited for: 9 -> 7; matrix products, arithmetic and copies ran while one was open for 0% -> 0% of each run, Pallas kernels for 14% -> 20%
where the time goes in v4:
time: 49.8 us; the launch traced here: 49.6 us
  Pallas kernels  19.1 us (38%)
  waiting for transfers between devices  15.4 us (31%)
  starting transfers between devices  15 us (30%)
    pallas_call x9, Pallas kernels, call(): pl.pallas_call(kernel, out_shape=out_shape, in_specs=[HBM if i in far els...  19.1 us
    ppermute x7, starting transfers between devices, from_behind(): return lax.ppermute(block, axis, route)  10.8 us
    ppermute x7, waiting for transfers between devices, from_behind(): return lax.ppermute(block, axis, route)  10.4 us
    ppermute x4, waiting for transfers between devices, space_sum(): lax.ppermute(block, 'space', [(i, i ^ step * k) for i in range(size)])  5 us
    ppermute x4, starting transfers between devices, space_sum(): lax.ppermute(block, 'space', [(i, i ^ step * k) for i in range(size)])  4.22 us
  transfers between devices with their start and end apart: 11, of which 7 were waited for; matrix products, arithmetic and copies ran while one was open for 0% of the time, Pallas kernels for 20%

profile of v4, /device:TPU:0, one launch (start us, length us, event | category | flops | bytes accessed | tf_op | source)
XLA Modules:
  0.0 49.6 jit_solution(7605231603959597158)
XLA Ops:
  0.0 1.3 %face_values.1 = (bf16[16,640]{1,0:T(8,128)(2,1)S(1)}, f32[16,4352]{1,0:T(8,128)S(1)}, s32[12,512]{1,0:T(8,128)S(1)}, s32[1,640]{1,0:T(1,128)S(1)}) custom-call(f32[16,4116]{1,0:T(8,128)} %psi_hbm.1, s32[12,512]{1,0:T(8,128)} %conn_hbm.1, s32[588]{0:T(1024)} %face_hbm.1), custom_call_target="tpu_custom_call" | custom-call | tf_op jit(solution)/shard_map/face_values/pallas_call | solution.py:266
  1.3 3.4 %collective-permute-start = (bf16[16,640]{1,0:T(8,128)(2,1)S(1)}, bf16[16,640]{1,0:T(8,128)(2,1)S(1)}, u32[]{:S(2)}, u32[]{:S(2)}) collective-permute-start(bf16[16,640]{1,0:T(8,128)(2,1)S(1)} %get-tuple-element.35), channel_id=1, source_target_pairs={{4,0},{8,4},{12,8},{16,12},{20,16},{24,20},{28,24},{0,28},{5,1},{9... | collective-permute-start | bytes 61448 | tf_op jit(solution)/shard_map/ppermute | solution.py:280
  4.7 4.4 %interior.1 = (f32[16,6144]{1,0:T(8,128)S(1)}, bf16[12,512,512]{2,1,0:T(8,128)(2,1)S(1)}, s32[1,5376]{1,0:T(1,128)S(1)}, s32[1,768]{1,0:T(1,128)S(1)}, bf16[256,...) custom-call(f32[16,4352]{1,0:T(8,128)S(1)} %get-tuple-element.27.psi_ref, s32[12,512]{1,0:T(8,128)S(1)} %get-tuple-element.28.conn_ref, ...), custom_call_target="tpu_custom_call" | custom-call | flops 4000000000 | bytes 8000000 | tf_op jit(solution)/shard_map/interior/pallas_call | solution.py:266
  9.0 0.0 collective-permute-done.ghost_ref
  9.0 2.9 %first_step.1 = (f32[16,4352]{1,0:T(8,128)S(1)}, f32[16,640]{1,0:T(8,128)S(1)}, f32[16,640]{1,0:T(8,128)S(1)}) custom-call(f32[16,4352]{1,0:T(8,128)S(1)} %get-tuple-element.27.psi_ref, s32[1,5376]{1,0:T(1,128)S(1)} %get-tuple-element.29.slots_ref, s32[1,768]{1,0:T(1,128)S(1)} %get-tuple-element.33.ghosts_ref, ...), custom_call_target="tpu_custom_call" | custom-call | flops 4000000000 | bytes 1000000 | tf_op jit(solution)/shard_map/first_step/pallas_call | solution.py:266
  12.0 0.1 collective-permute-start.1
  12.0 2.6 %collective-permute-start.2 = (f32[16,640]{1,0:T(8,128)S(1)}, f32[16,640]{1,0:T(8,128)S(1)}, u32[]{:S(2)}, u32[]{:S(2)}) collective-permute-start(f32[16,640]{1,0:T(8,128)S(1)} %get-tuple-element.42.low_in), channel_id=1, source_target_pairs={{4,0},{8,4},{12,8},{16,12},{20,16},{24,20},{28,24},{0,28},{5,1},{9... | collective-permute-start | bytes 122888 | tf_op jit(solution)/shard_map/ppermute | solution.py:280
  14.7 2.7 %off_face.1 = (bf16[16,5376]{1,0:T(8,128)(2,1)S(1)}, s32[1,5376]{1,0:T(1,128)S(1)}, bf16[256,5376]{1,0:T(8,128)(2,1)S(1)}) custom-call(f32[16,4352]{1,0:T(8,128)S(1)} %get-tuple-element.37.own_in, s32[1,5376]{1,0:T(1,128)S(1)} %get-tuple-element.29.slots_ref, bf16[256,5376]{1,0:T(8,128)(2,1)S(1)} %get-tuple-element.30.hots_ref, ...), custom_call_target="tpu_custom_call" | custom-call | flops 4000000000 | bytes 1000000 | tf_op jit(solution)/shard_map/off_face/pallas_call | solution.py:266
  17.3 0.0 collective-permute-done.1.below_in
  17.4 0.0 collective-permute-done.2.above_in
  17.4 1.1 %second_step.1 = (bf16[16,6144]{1,0:T(8,128)(2,1)S(1)}, f32[16,640]{1,0:T(8,128)S(1)}) custom-call(bf16[16,5376]{1,0:T(8,128)(2,1)S(1)} %get-tuple-element.39.inside_ref, s32[1,5376]{1,0:T(1,128)S(1)} %get-tuple-element.40.high_ref, bf16[256,5376]{1,0:T(8,128)(2,1)S(1)} %get-tuple-element.41.faces_ref, s32[1,768]{1,0:T(1,128)S(1)} %get-tuple-element.33.ghosts_ref, ...), custom_call_target="tpu_custom_call" | custom-call | flops 4000000000 | bytes 1000000 | tf_op jit(solution)/shard_map/second_step/pallas_call | solution.py:266
  18.5 0.1 collective-permute-start.3
  18.6 2.8 %second_sums.1.own_in = f32[16,4352]{1,0:T(8,128)S(1)} custom-call(f32[16,4352]{1,0:T(8,128)S(1)} %get-tuple-element.27.psi_ref, s32[1,5376]{1,0:T(1,128)S(1)} %get-tuple-element.29.slots_ref, bf16[256,5376]{1,0:T(8,128)(2,1)S(1)} %get-tuple-element.30.hots_ref, bf16[12,512,512]{2,1,0:T(8,128)(2,1)S(1)} %get-tuple-element.31.ham_ref, ...), custom_call_target="tpu_custom_call" | custom-call | flops 4000000000 | bytes 8000000 | tf_op jit(solution)/shard_map/second_sums/pallas_call | solution.py:266
  21.4 1.5 %collective-permute-done.3.below_in = f32[16,640]{1,0:T(8,128)S(1)} collective-permute-done((f32[16,640]{1,0:T(8,128)S(1)}, f32[16,640]{1,0:T(8,128)S(1)}, u32[]{:S(2)}, u32[]{:S(2)}) %collective-permute-start.3) | collective-permute-done | bytes 40992 | tf_op jit(solution)/shard_map/ppermute | solution.py:280
  22.9 0.4 last_faces.1
  23.3 3.6 %collective-permute-start.6 = (bf16[16,4224]{1,0:T(8,128)(2,1)S(1)}, bf16[16,4224]{1,0:T(8,128)(2,1)S(1)}, u32[]{:S(2)}, u32[]{:S(2)}) collective-permute-start(bf16[16,4224]{1,0:T(8,128)(2,1)S(1)} %get-tuple-element.46), channel_id=1, source_target_pairs={{1,0},{2,1},{3,2},{0,3},{5,4},{6,5},{7,6},{4,7},{9,8},{10,9},{11,1... | collective-permute-start | bytes 405512 | tf_op jit(solution)/shard_map/ppermute | solution.py:280
  27.0 0.0 collective-permute-start.5
  27.0 1.0 %collective-permute-start.4 = (bf16[16,4224]{1,0:T(8,128)(2,1)S(1)}, bf16[16,4224]{1,0:T(8,128)(2,1)S(1)}, u32[]{:S(2)}, u32[]{:S(2)}) collective-permute-start(bf16[16,4224]{1,0:T(8,128)(2,1)S(1)} %get-tuple-element.46), channel_id=1, source_target_pairs={{3,0},{0,1},{1,2},{2,3},{7,4},{4,5},{5,6},{6,7},{11,8},{8,9},{9,10... | collective-permute-start | bytes 405512 | tf_op jit(solution)/shard_map/ppermute | solution.py:280
  28.0 2.2 %collective-permute-done.6.refs_3_ = bf16[16,4224]{1,0:T(8,128)(2,1)S(1)} collective-permute-done((bf16[16,4224]{1,0:T(8,128)(2,1)S(1)}, bf16[16,4224]{1,0:T(8,128)(2,1)S(1)}, u32[]{:S(2)}, u32[]{:S(2)}) %collective-permute-start.6) | collective-permute-done | bytes 135200 | tf_op jit(solution)/shard_map/ppermute | solution.py:280
  30.2 6.6 %collective-permute-done.5.refs_2_ = bf16[16,4224]{1,0:T(8,128)(2,1)S(1)} collective-permute-done((bf16[16,4224]{1,0:T(8,128)(2,1)S(1)}, bf16[16,4224]{1,0:T(8,128)(2,1)S(1)}, u32[]{:S(2)}, u32[]{:S(2)}) %collective-permute-start.5) | collective-permute-done | bytes 135200 | tf_op jit(solution)/shard_map/ppermute | solution.py:280
  36.9 0.0 collective-permute-done.4.refs_1_
  36.9 0.8 %gram.1 = (bf16[128,4352]{1,0:T(8,128)(2,1)S(1)}, f32[64,64]{1,0:T(8,128)S(1)}) custom-call(f32[16,4352]{1,0:T(8,128)S(1)} %get-tuple-element.45.refs_0_, bf16[16,4224]{1,0:T(8,128)(2,1)S(1)} %collective-permute-done.4.refs_1_, bf16[16,4224]{1,0:T(8,128)(2,1)S(1)} %collective-permute-done.5.refs_2_, bf16[16,4224]{1,0:T(8,128)(2,1)S(1)} %collective-permute-done.6.refs_3_), custom_call_target="tpu_custom_call" | custom-call | tf_op jit(solution)/shard_map/gram/pallas_call | solution.py:266
  37.7 0.1 collective-permute-start.7
  37.8 1.2 %collective-permute-done.7 = f32[64,64]{1,0:T(8,128)S(1)} collective-permute-done((f32[64,64]{1,0:T(8,128)S(1)}, f32[64,64]{1,0:T(8,128)S(1)}, u32[]{:S(2)}, u32[]{:S(2)}) %collective-permute-start.7) | collective-permute-done | bytes 16416 | tf_op jit(solution)/shard_map/gram_sum/ppermute | solution.py:416
  39.0 3.5 %collective-permute-start.10 = (f32[64,64]{1,0:T(8,128)S(1)}, f32[64,64]{1,0:T(8,128)S(1)}, u32[]{:S(2)}, u32[]{:S(2)}) collective-permute-start(f32[64,64]{1,0:T(8,128)S(1)} %add.12), channel_id=1, source_target_pairs={{0,24},{4,28},{8,16},{12,20},{16,8},{20,12},{24,0},{28,4},{1,25},{... | collective-permute-start | bytes 49160 | tf_op jit(solution)/shard_map/gram_sum/ppermute | solution.py:416
  42.5 0.5 %collective-permute-start.9 = (f32[64,64]{1,0:T(8,128)S(1)}, f32[64,64]{1,0:T(8,128)S(1)}, u32[]{:S(2)}, u32[]{:S(2)}) collective-permute-start(f32[64,64]{1,0:T(8,128)S(1)} %add.12), channel_id=1, source_target_pairs={{0,16},{4,20},{8,24},{12,28},{16,0},{20,4},{24,8},{28,12},{1,17},{... | collective-permute-start | bytes 49160 | tf_op jit(solution)/shard_map/gram_sum/ppermute | solution.py:416
  43.0 0.1 collective-permute-start.8
  43.1 1.3 %collective-permute-done.10 = f32[64,64]{1,0:T(8,128)S(1)} collective-permute-done((f32[64,64]{1,0:T(8,128)S(1)}, f32[64,64]{1,0:T(8,128)S(1)}, u32[]{:S(2)}, u32[]{:S(2)}) %collective-permute-start.10) | collective-permute-done | bytes 16416 | tf_op jit(solution)/shard_map/gram_sum/ppermute | solution.py:416
  44.4 2.0 %collective-permute-done.9 = f32[64,64]{1,0:T(8,128)S(1)} collective-permute-done((f32[64,64]{1,0:T(8,128)S(1)}, f32[64,64]{1,0:T(8,128)S(1)}, u32[]{:S(2)}, u32[]{:S(2)}) %collective-permute-start.9) | collective-permute-done | bytes 16416 | tf_op jit(solution)/shard_map/gram_sum/ppermute | solution.py:416
  46.4 0.5 %collective-permute-done.8 = f32[64,64]{1,0:T(8,128)S(1)} collective-permute-done((f32[64,64]{1,0:T(8,128)S(1)}, f32[64,64]{1,0:T(8,128)S(1)}, u32[]{:S(2)}, u32[]{:S(2)}) %collective-permute-start.8) | collective-permute-done | bytes 16416 | tf_op jit(solution)/shard_map/gram_sum/ppermute | solution.py:416
  47.0 2.7 %orthonormal.1 = f32[16,4116]{1,0:T(8,128)} custom-call(f32[64,64]{1,0:T(8,128)S(1)} %add_add_fusion.gram_ref, bf16[128,4352]{1,0:T(8,128)(2,1)S(1)} %get-tuple-element.48.terms_ref), custom_call_target="tpu_custom_call" | custom-call | tf_op jit(solution)/shard_map/orthonormal/pallas_call | solution.py:266
  (2 shorter events, 0.0 us)
Async XLA Ops:
  1.3 7.8 %collective-permute-start = (bf16[16,640]{1,0:T(8,128)(2,1)S(1)}, bf16[16,640]{1,0:T(8,128)(2,1)S(1)}, u32[]{:S(2)}, u32[]{:S(2)}) collective-permute-start(bf16[16,640]{1,0:T(8,128)(2,1)S(1)} %get-tuple-element.35), channel_id=1, source_target_pairs={{4,0},{8,4},{12,8},{16,12},{20,16},{24,20},{28,24},{0,28},{5,1},{9... | collective-permute-start | bytes 61448 | tf_op jit(solution)/shard_map/ppermute | solution.py:280
  12.0 5.4 %collective-permute-start.1 = (f32[16,640]{1,0:T(8,128)S(1)}, f32[16,640]{1,0:T(8,128)S(1)}, u32[]{:S(2)}, u32[]{:S(2)}) collective-permute-start(f32[16,640]{1,0:T(8,128)S(1)} %get-tuple-element.38.upper_in), channel_id=1, source_target_pairs={{28,0},{0,4},{4,8},{8,12},{12,16},{16,20},{20,24},{24,28},{29,1},{... | collective-permute-start | bytes 122888 | tf_op jit(solution)/shard_map/ppermute | solution.py:280
  12.0 5.3 %collective-permute-start.2 = (f32[16,640]{1,0:T(8,128)S(1)}, f32[16,640]{1,0:T(8,128)S(1)}, u32[]{:S(2)}, u32[]{:S(2)}) collective-permute-start(f32[16,640]{1,0:T(8,128)S(1)} %get-tuple-element.42.low_in), channel_id=1, source_target_pairs={{4,0},{8,4},{12,8},{16,12},{20,16},{24,20},{28,24},{0,28},{5,1},{9... | collective-permute-start | bytes 122888 | tf_op jit(solution)/shard_map/ppermute | solution.py:280
  18.5 4.4 %collective-permute-start.3 = (f32[16,640]{1,0:T(8,128)S(1)}, f32[16,640]{1,0:T(8,128)S(1)}, u32[]{:S(2)}, u32[]{:S(2)}) collective-permute-start(f32[16,640]{1,0:T(8,128)S(1)} %get-tuple-element.44), channel_id=1, source_target_pairs={{28,0},{0,4},{4,8},{8,12},{12,16},{16,20},{20,24},{24,28},{29,1},{... | collective-permute-start | bytes 122888 | tf_op jit(solution)/shard_map/ppermute | solution.py:280
  23.3 6.9 %collective-permute-start.6 = (bf16[16,4224]{1,0:T(8,128)(2,1)S(1)}, bf16[16,4224]{1,0:T(8,128)(2,1)S(1)}, u32[]{:S(2)}, u32[]{:S(2)}) collective-permute-start(bf16[16,4224]{1,0:T(8,128)(2,1)S(1)} %get-tuple-element.46), channel_id=1, source_target_pairs={{1,0},{2,1},{3,2},{0,3},{5,4},{6,5},{7,6},{4,7},{9,8},{10,9},{11,1... | collective-permute-start | bytes 405512 | tf_op jit(solution)/shard_map/ppermute | solution.py:280
  27.0 9.9 %collective-permute-start.5 = (bf16[16,4224]{1,0:T(8,128)(2,1)S(1)}, bf16[16,4224]{1,0:T(8,128)(2,1)S(1)}, u32[]{:S(2)}, u32[]{:S(2)}) collective-permute-start(bf16[16,4224]{1,0:T(8,128)(2,1)S(1)} %get-tuple-element.46), channel_id=1, source_target_pairs={{2,0},{3,1},{0,2},{1,3},{6,4},{7,5},{4,6},{5,7},{10,8},{11,9},{8,1... | collective-permute-start | bytes 405512 | tf_op jit(solution)/shard_map/ppermute | solution.py:280
  27.0 9.9 %collective-permute-start.4 = (bf16[16,4224]{1,0:T(8,128)(2,1)S(1)}, bf16[16,4224]{1,0:T(8,128)(2,1)S(1)}, u32[]{:S(2)}, u32[]{:S(2)}) collective-permute-start(bf16[16,4224]{1,0:T(8,128)(2,1)S(1)} %get-tuple-element.46), channel_id=1, source_target_pairs={{3,0},{0,1},{1,2},{2,3},{7,4},{4,5},{5,6},{6,7},{11,8},{8,9},{9,10... | collective-permute-start | bytes 405512 | tf_op jit(solution)/shard_map/ppermute | solution.py:280
  37.7 1.3 %collective-permute-start.7 = (f32[64,64]{1,0:T(8,128)S(1)}, f32[64,64]{1,0:T(8,128)S(1)}, u32[]{:S(2)}, u32[]{:S(2)}) collective-permute-start(f32[64,64]{1,0:T(8,128)S(1)} %get-tuple-element.47), channel_id=1, source_target_pairs={{0,4},{4,0},{8,12},{12,8},{16,20},{20,16},{24,28},{28,24},{1,5},{5... | collective-permute-start | bytes 49160 | tf_op jit(solution)/shard_map/gram_sum/ppermute | solution.py:416
  39.0 5.4 %collective-permute-start.10 = (f32[64,64]{1,0:T(8,128)S(1)}, f32[64,64]{1,0:T(8,128)S(1)}, u32[]{:S(2)}, u32[]{:S(2)}) collective-permute-start(f32[64,64]{1,0:T(8,128)S(1)} %add.12), channel_id=1, source_target_pairs={{0,24},{4,28},{8,16},{12,20},{16,8},{20,12},{24,0},{28,4},{1,25},{... | collective-permute-start | bytes 49160 | tf_op jit(solution)/shard_map/gram_sum/ppermute | solution.py:416
  42.5 3.9 %collective-permute-start.9 = (f32[64,64]{1,0:T(8,128)S(1)}, f32[64,64]{1,0:T(8,128)S(1)}, u32[]{:S(2)}, u32[]{:S(2)}) collective-permute-start(f32[64,64]{1,0:T(8,128)S(1)} %add.12), channel_id=1, source_target_pairs={{0,16},{4,20},{8,24},{12,28},{16,0},{20,4},{24,8},{28,12},{1,17},{... | collective-permute-start | bytes 49160 | tf_op jit(solution)/shard_map/gram_sum/ppermute | solution.py:416
  43.0 3.9 %collective-permute-start.8 = (f32[64,64]{1,0:T(8,128)S(1)}, f32[64,64]{1,0:T(8,128)S(1)}, u32[]{:S(2)}, u32[]{:S(2)}) collective-permute-start(f32[64,64]{1,0:T(8,128)S(1)} %add.12), channel_id=1, source_target_pairs={{0,8},{4,12},{8,0},{12,4},{16,24},{20,28},{24,16},{28,20},{1,9},{5... | collective-permute-start | bytes 49160 | tf_op jit(solution)/shard_map/gram_sum/ppermute | solution.py:416

commit v5 on v4

--- a/solution.py
+++ b/solution.py
@@ -132,12 +132,9 @@
 
 
 def interior_kernel(
-    nodes, psi_ref, conn_ref, ham_hbm, part_ref, ham_ref, slots_ref, ghosts_ref, hots_ref, hosts_ref, inside_ref, sems
+    nodes, psi_ref, conn_ref, ham_ref, part_ref, slots_ref, ghosts_ref, hots_ref, hosts_ref, inside_ref
 ):
     elements, size = conn_ref.shape
-    copies = [pltpu.make_async_copy(ham_hbm.at[e], ham_ref.at[e], sems.at[e]) for e in range(elements)]
-    for copy in copies:
-        copy.start()
     slots_ref[...] = packed(conn_ref, elements, 0, IN_EL)
     ghosts_ref[...] = packed(conn_ref, elements, IN_EL, size) - nodes
     hot_into(hosts_ref, ghosts_ref[...] & 255)
@@ -145,7 +142,6 @@
     hot_into(hots_ref, slots & 255)
     pick_into(inside_ref, stacked(psi_ref[...]).astype(BF16), slots >> 8, hots_ref)
     for e in range(elements):
-        copies[e].wait()
         part_ref[:, e * size : (e + 1) * size] = jnp.dot(
             inside_ref[:, e * IN_EL : (e + 1) * IN_EL], ham_ref[e, :IN_EL, :], preferred_element_type=F32
         )
@@ -158,9 +154,13 @@
     return jnp.concatenate([values, jnp.zeros((bands, round_up(count, LANES) - count), values.dtype)], axis=1)
 
 
+def odd_domain():
+    return lax.rem(lax.axis_index("space"), 2) == 1
+
+
 def first_kernel(
     psi_ref, slots_ref, ghosts_ref, hots_ref, hosts_ref, ham_ref, face_ref, ghost_ref, part_ref,
-    own_ref, upper_ref, low_ref, sums, top_sums, inner, top, outside,
+    own_ref, upper_ref, low_ref, near_ref, far_ref, sums, top_sums, inner, top, outside,
 ):
     bands, own = psi_ref.shape
     elements, size = ham_ref.shape[:2]
@@ -176,14 +176,19 @@
         split_products(products, inner, top, pair[0])
     spread_into(sums, inner, slots_ref[...] >> 8)
     spread_into(top_sums, top, ghosts >> 8)
-    upper_ref[...] = unstacked(gathered_sum(top_sums[...], hosts_ref[...]), bands)[:, :face_count] / HALF_WIDTH
+    upper = unstacked(gathered_sum(top_sums[...], hosts_ref[...]), bands)[:, :face_count] / HALF_WIDTH
+    upper_ref[...] = upper
     total = unstacked(gathered_sum(sums[...], hots_ref[...]), bands)
     current = (total - CENTER * psi_ref[...]) / HALF_WIDTH
     own_ref[...] = current
     face = face_ref[...]
     face_hot = one_hot(face & 255)
     terms = halves(stacked(current))
-    low_ref[...] = pick(terms[0], face >> 8, face_hot, bands) + pick(terms[1], face >> 8, face_hot, bands)
+    low = pick(terms[0], face >> 8, face_hot, bands) + pick(terms[1], face >> 8, face_hot, bands)
+    low_ref[...] = low
+    odd = odd_domain()
+    near_ref[...] = jnp.where(odd, low, upper)
+    far_ref[...] = jnp.where(odd, upper, low)
 
 
 def far_kernel(own_in, slots_ref, hots_ref, face_ref, inside_ref, high_ref, faces_ref):
@@ -210,13 +215,16 @@
 
 
 def second_kernel(
-    inside_ref, high_ref, faces_ref, ghosts_ref, hosts_ref, ham_ref, low_in, upper_in, below_in, above_in,
+    inside_ref, high_ref, faces_ref, ghosts_ref, hosts_ref, ham_ref, low_in, upper_in, near_in, far_in,
     field_ref, upper_ref, top_sums, inside, top, outside,
 ):
     bands, face_count = upper_in.shape
     elements, size = ham_ref.shape[:2]
-    faces = stacked(widened(low_in[...] + below_in[...])).astype(BF16)
-    ghost = stacked(widened(upper_in[...] + above_in[...])).astype(BF16)
+    odd = odd_domain()
+    below = jnp.where(odd, near_in[...], far_in[...])
+    above = jnp.where(odd, far_in[...], near_in[...])
+    faces = stacked(widened(low_in[...] + below)).astype(BF16)
+    ghost = stacked(widened(upper_in[...] + above)).astype(BF16)
     ghosts = ghosts_ref[...]
     pick_into(outside, ghost, ghosts >> 8, hosts_ref)
     for tile in tiles(high_ref.shape[1]):
@@ -237,11 +245,14 @@
     upper_ref[...] = total[:, :face_count] * (2.0 / HALF_WIDTH)
 
 
-def third_kernel(psi_ref, slots_ref, hots_ref, ham_ref, face_ref, own_in, below_in, field_ref, own_ref, sums, inner):
+def third_kernel(
+    psi_ref, slots_ref, hots_ref, ham_ref, face_ref, own_in, near_in, far_in, field_ref, own_ref, sums, inner
+):
     bands, own = own_in.shape
     elements, size = ham_ref.shape[:2]
     face = face_ref[...]
-    added = gathered_sum(spread(below_in[...], face >> 8, own // LANES), one_hot(face & 255))
+    below = jnp.where(odd_domain(), near_in[...], far_in[...])
+    added = gathered_sum(spread(below, face >> 8, own // LANES), one_hot(face & 255))
     for pair in pairs(elements):
         products = [
             jnp.dot(field_ref[:, e * size : (e + 1) * size], ham_ref[e], preferred_element_type=F32) for e in pair
@@ -304,27 +315,28 @@
             (shape((bands, faces), BF16), own_field, shape(conn.shape, jnp.int32), shape((1, faces), jnp.int32)),
             [pltpu.with_memory_space_constraint(array, pltpu.HBM) for array in (psi, conn, face_rows)],
             (pltpu.VMEM(psi.shape, F32), pltpu.VMEM(face_rows.shape, jnp.int32), pltpu.SemaphoreType.DMA((3,))),
-            far=(0, 1, 2),
+            far=(0, 1, 2), flops=2 * 10**10, moved=4 * 10**7,
         )
     ghost = from_behind(values, "space", -1)
     with jax.named_scope("interior"):
-        part, near, slots, ghosts, hots, hosts = call(
+        part, slots, ghosts, hots, hosts = call(
             functools.partial(interior_kernel, nodes),
             (
-                shape((bands, elements * size), F32), shape(ham.shape, BF16),
+                shape((bands, elements * size), F32),
                 shape((1, inner_count), jnp.int32), shape((1, face_count), jnp.int32),
                 shape((LANES, inner_count), BF16), shape((LANES, face_count), BF16),
             ),
-            (wide, conn, ham), (inside_field, pltpu.SemaphoreType.DMA((elements,))), flops=4 * 10**9, moved=8 * 10**6, far=(2,),
+            (wide, conn, ham), (inside_field,), flops=4 * 10**9, moved=8 * 10**6,
         )
     with jax.named_scope("first_step"):
-        current, upper, low = call(
-            first_kernel, (own_field, face_field, face_field),
-            (wide, slots, ghosts, hots, hosts, near, face, ghost, part), (sums, top_sums, inner, top, outside),
+        current, upper, low, to_near, to_far = call(
+            first_kernel, (own_field, *[face_field] * 4),
+            (wide, slots, ghosts, hots, hosts, ham, face, ghost, part), (sums, top_sums, inner, top, outside),
             flops=4 * 10**9, moved=10**6,
         )
-    below = from_behind(upper, "space", 1)
-    above = from_behind(low, "space", -1)
+    domains = lax.axis_size("space")
+    from_near = lax.ppermute(to_near, "space", [(i, i ^ 1) for i in range(domains)])
+    from_far = lax.ppermute(to_far, "space", [(i, ((i + 1 ^ 1) - 1) % domains) for i in range(domains)])
     with jax.named_scope("off_face"):
         inside, high, faces = call(
             far_kernel,
@@ -334,13 +346,13 @@
     with jax.named_scope("second_step"):
         field, upper = call(
             second_kernel, (shape((bands, elements * size), BF16), face_field),
-            (inside, high, faces, ghosts, hosts, near, low, upper, below, above), (top_sums, inside_field, top, outside),
+            (inside, high, faces, ghosts, hosts, ham, low, upper, from_near, from_far), (top_sums, inside_field, top, outside),
             flops=4 * 10**9, moved=10**6,
         )
     from_below = from_behind(upper, "space", 1)
     with jax.named_scope("second_sums"):
         following = call(
-            third_kernel, own_field, (wide, slots, hots, near, face, current, below, field), (sums, inner),
+            third_kernel, own_field, (wide, slots, hots, ham, face, current, from_near, from_far, field), (sums, inner),
             flops=4 * 10**9, moved=8 * 10**6,
         )
     with jax.named_scope("last_faces"):
@@ -359,7 +371,8 @@
         terms_ref[pl.ds(total + source, bands), :] = lower
     terms = terms_ref[...]
     both = lax.dot_general(terms, terms, (((1,), (1,)), ((), ())), preferred_element_type=F32)
-    gram_ref[...] = both[:total, :total] + (both[:total, total:] + both[total:, :total]) + both[total:, total:]
+    gram = both[:total, :total] + (both[:total, total:] + both[total:, :total]) + both[total:, total:]
+    gram_ref[...] = jnp.concatenate([gram[: total // 2], gram[total // 2 :]], axis=1)
 
 
 def inverse_factor(matrix, block=8):
@@ -395,7 +408,9 @@
 
 def ortho_kernel(nodes, count, gram_ref, terms_ref, out_ref, inverse_ref):
     bands = out_ref.shape[0]
-    inverse_ref[...] = inverse_factor(gram_ref[...] / count)
+    total = inverse_ref.shape[0]
+    gram = jnp.concatenate([gram_ref[:, :total], gram_ref[:, total:]], axis=0)
+    inverse_ref[...] = inverse_factor(gram / count)
     first = pl.multiple_of(lax.axis_index("band") * bands, bands)
     upper, lower = halves(inverse_ref[pl.ds(first, bands), :])
     rows = jnp.concatenate(
@@ -429,7 +444,7 @@
     shape = jax.ShapeDtypeStruct
     blocks = [following] + [from_behind(short, "band", i) for i in range(1, groups)]
     with jax.named_scope("gram"):
-        terms, gram = call(gram_kernel, (shape((2 * total, own), BF16), shape((total, total), F32)), blocks)
+        terms, gram = call(gram_kernel, (shape((2 * total, own), BF16), shape((total // 2, 2 * total), F32)), blocks)
     with jax.named_scope("gram_sum"):
         gram = space_sum(gram)
     with jax.named_scope("orthonormal"):

time: 49.8 us -> 47.3 us (0.950)
  Pallas kernels: 19.1 us -> 17.2 us
  starting transfers between devices: 15 us -> 13.8 us
  waiting for transfers between devices: 15.4 us -> 16 us
    ppermute x7 -> x5, starting transfers between devices: 10.8 us -> 8.12 us  [from_behind(): return lax.ppermute(block, axis, route)]
    ppermute x0 -> x2, starting transfers between devices: none -> 2.14 us  [the longest x1 2.07 us: filter_field(): lax.ppermute(to_far, 'space', [(i, ((i + 1 ^ 1) - 1) % domains) for i in...]
    pallas_call x9, Pallas kernels: 19.1 us -> 17.2 us  [call(): pl.pallas_call(kernel, out_shape=out_shape, in_specs=[HBM if i in far els...]
    ppermute x7 -> x5, waiting for transfers between devices: 10.4 us -> 11.6 us  [from_behind(): return lax.ppermute(block, axis, route)]
    ppermute x4, starting transfers between devices: 4.22 us -> 3.52 us  [space_sum(): lax.ppermute(block, 'space', [(i, i ^ step * k) for i in range(size)])]
    ppermute x4, waiting for transfers between devices: 5 us -> 4.43 us  [space_sum(): lax.ppermute(block, 'space', [(i, i ^ step * k) for i in range(size)])]
  transfers between devices with their start and end apart: 11 -> 11, of which waited for: 7 -> 7; matrix products, arithmetic and copies ran while one was open for 0% -> 0% of each run, Pallas kernels for 20% -> 16%
where the time goes in v5:
time: 47.3 us; the launch traced here: 47.1 us
  Pallas kernels  17.2 us (36%)
  waiting for transfers between devices  16 us (34%)
  starting transfers between devices  13.8 us (29%)
    pallas_call x9, Pallas kernels, call(): pl.pallas_call(kernel, out_shape=out_shape, in_specs=[HBM if i in far els...  17.2 us
    ppermute x5, waiting for transfers between devices, from_behind(): return lax.ppermute(block, axis, route)  11.6 us
    ppermute x5, starting transfers between devices, from_behind(): return lax.ppermute(block, axis, route)  8.12 us
    ppermute x4, waiting for transfers between devices, space_sum(): lax.ppermute(block, 'space', [(i, i ^ step * k) for i in range(size)])  4.43 us
    ppermute x4, starting transfers between devices, space_sum(): lax.ppermute(block, 'space', [(i, i ^ step * k) for i in range(size)])  3.52 us
    ppermute x1, starting transfers between devices, filter_field(): lax.ppermute(to_far, 'space', [(i, ((i + 1 ^ 1) - 1) % domains) for i in...  2.07 us
  transfers between devices with their start and end apart: 11, of which 7 were waited for; matrix products, arithmetic and copies ran while one was open for 0% of the time, Pallas kernels for 16%

profile of v5, /device:TPU:0, one launch (start us, length us, event | category | flops | bytes accessed | tf_op | source)
XLA Modules:
  0.0 47.1 jit_solution(2384269991975356417)
XLA Ops:
  0.0 0.0 copy-start
  0.0 1.4 %face_values.1 = (bf16[16,640]{1,0:T(8,128)(2,1)S(1)}, f32[16,4352]{1,0:T(8,128)S(1)}, s32[12,512]{1,0:T(8,128)S(1)}, s32[1,640]{1,0:T(1,128)S(1)}) custom-call(f32[16,4116]{1,0:T(8,128)} %psi_hbm.1, s32[12,512]{1,0:T(8,128)} %conn_hbm.1, s32[588]{0:T(1024)} %face_hbm.1), custom_call_target="tpu_custom_call" | custom-call | flops 20000000000 | bytes 40000000 | tf_op jit(solution)/shard_map/face_values/pallas_call | solution.py:277
  1.4 3.4 %collective-permute-start = (bf16[16,640]{1,0:T(8,128)(2,1)S(1)}, bf16[16,640]{1,0:T(8,128)(2,1)S(1)}, u32[]{:S(2)}, u32[]{:S(2)}) collective-permute-start(bf16[16,640]{1,0:T(8,128)(2,1)S(1)} %get-tuple-element.35), channel_id=1, source_target_pairs={{4,0},{8,4},{12,8},{16,12},{20,16},{24,20},{28,24},{0,28},{5,1},{9... | collective-permute-start | bytes 61448 | tf_op jit(solution)/shard_map/ppermute | solution.py:291
  4.8 0.0 copy-done
  4.8 2.2 %interior.1 = (f32[16,6144]{1,0:T(8,128)S(1)}, s32[1,5376]{1,0:T(1,128)S(1)}, s32[1,768]{1,0:T(1,128)S(1)}, bf16[256,5376]{1,0:T(8,128)(2,1)S(1)}, bf16[256,768]{1,0:T(8,128)(2,1)S(1)}) custom-call(f32[16,4352]{1,0:T(8,128)S(1)} %get-tuple-element.28.psi_ref, s32[12,512]{1,0:T(8,128)S(1)} %get-tuple-element.29.conn_ref, bf16[12,512,512]{2,1,0:T(8,128)(2,1)S(1)} %copy-done), custom_call_target="tpu_custom_call" | custom-call | flops 4000000000 | bytes 8000000 | tf_op jit(solution)/shard_map/interior/pallas_call | solution.py:277
  7.0 0.0 collective-permute-done.ghost_ref
  7.0 2.9 %first_step.1 = (f32[16,4352]{1,0:T(8,128)S(1)}, f32[16,640]{1,0:T(8,128)S(1)}, f32[16,640]{1,0:T(8,128)S(1)}, f32[16,640]{1,0:T(8,128)S(1)}, f32[16,640]{1,0:T(8,128)S(1)}) custom-call(f32[16,4352]{1,0:T(8,128)S(1)} %get-tuple-element.28.psi_ref, s32[1,5376]{1,0:T(1,128)S(1)} %get-tuple-element.30.slots_ref, s32[1,768]{1,0:T(1,128)S(1)} %get-tuple-element.33.ghosts_ref, ...), custom_call_target="tpu_custom_call" | custom-call | flops 4000000000 | bytes 1000000 | tf_op jit(solution)/shard_map/first_step/pallas_call | solution.py:277
  10.0 0.1 collective-permute-start.1
  10.1 2.1 %collective-permute-start.2 = (f32[16,640]{1,0:T(8,128)S(1)}, f32[16,640]{1,0:T(8,128)S(1)}, u32[]{:S(2)}, u32[]{:S(2)}) collective-permute-start(f32[16,640]{1,0:T(8,128)S(1)} %get-tuple-element.39), channel_id=1, source_target_pairs={{0,28},{4,8},{8,4},{12,16},{16,12},{20,24},{24,20},{28,0},{1,29},{... | collective-permute-start | bytes 122888 | tf_op jit(solution)/shard_map/ppermute | solution.py:339
  12.1 2.7 %off_face.1 = (bf16[16,5376]{1,0:T(8,128)(2,1)S(1)}, s32[1,5376]{1,0:T(1,128)S(1)}, bf16[256,5376]{1,0:T(8,128)(2,1)S(1)}) custom-call(f32[16,4352]{1,0:T(8,128)S(1)} %get-tuple-element.37.own_in, s32[1,5376]{1,0:T(1,128)S(1)} %get-tuple-element.30.slots_ref, bf16[256,5376]{1,0:T(8,128)(2,1)S(1)} %get-tuple-element.31.hots_ref, ...), custom_call_target="tpu_custom_call" | custom-call | flops 4000000000 | bytes 1000000 | tf_op jit(solution)/shard_map/off_face/pallas_call | solution.py:277
  14.8 0.0 collective-permute-done.1.near_in
  14.8 0.0 collective-permute-done.2.far_in
  14.8 1.1 %second_step.1 = (bf16[16,6144]{1,0:T(8,128)(2,1)S(1)}, f32[16,640]{1,0:T(8,128)S(1)}) custom-call(bf16[16,5376]{1,0:T(8,128)(2,1)S(1)} %get-tuple-element.40.inside_ref, s32[1,5376]{1,0:T(1,128)S(1)} %get-tuple-element.41.high_ref, bf16[256,5376]{1,0:T(8,128)(2,1)S(1)} %get-tuple-element.42.faces_ref, s32[1,768]{1,0:T(1,128)S(1)} %get-tuple-element.33.ghosts_ref, ...), custom_call_target="tpu_custom_call" | custom-call | flops 4000000000 | bytes 1000000 | tf_op jit(solution)/shard_map/second_step/pallas_call | solution.py:277
  16.0 0.1 collective-permute-start.3
  16.0 2.8 %second_sums.1.own_in = f32[16,4352]{1,0:T(8,128)S(1)} custom-call(f32[16,4352]{1,0:T(8,128)S(1)} %get-tuple-element.28.psi_ref, s32[1,5376]{1,0:T(1,128)S(1)} %get-tuple-element.30.slots_ref, bf16[256,5376]{1,0:T(8,128)(2,1)S(1)} %get-tuple-element.31.hots_ref, bf16[12,512,512]{2,1,0:T(8,128)(2,1)S(1)} %copy-done, s32[1,640]{1,0:T(1,128)S(1)} %get-tuple-element.32.face_ref, ...), custom_call_target="tpu_custom_call" | custom-call | flops 4000000000 | bytes 8000000 | tf_op jit(solution)/shard_map/second_sums/pallas_call | solution.py:277
  18.8 1.5 %collective-permute-done.3.below_in = f32[16,640]{1,0:T(8,128)S(1)} collective-permute-done((f32[16,640]{1,0:T(8,128)S(1)}, f32[16,640]{1,0:T(8,128)S(1)}, u32[]{:S(2)}, u32[]{:S(2)}) %collective-permute-start.3) | collective-permute-done | bytes 40992 | tf_op jit(solution)/shard_map/ppermute | solution.py:291
  20.4 0.4 last_faces.1
  20.8 3.6 %collective-permute-start.6 = (bf16[16,4224]{1,0:T(8,128)(2,1)S(1)}, bf16[16,4224]{1,0:T(8,128)(2,1)S(1)}, u32[]{:S(2)}, u32[]{:S(2)}) collective-permute-start(bf16[16,4224]{1,0:T(8,128)(2,1)S(1)} %get-tuple-element.48), channel_id=1, source_target_pairs={{1,0},{2,1},{3,2},{0,3},{5,4},{6,5},{7,6},{4,7},{9,8},{10,9},{11,1... | collective-permute-start | bytes 405512 | tf_op jit(solution)/shard_map/ppermute | solution.py:291
  24.5 0.0 collective-permute-start.5
  24.5 1.0 %collective-permute-start.4 = (bf16[16,4224]{1,0:T(8,128)(2,1)S(1)}, bf16[16,4224]{1,0:T(8,128)(2,1)S(1)}, u32[]{:S(2)}, u32[]{:S(2)}) collective-permute-start(bf16[16,4224]{1,0:T(8,128)(2,1)S(1)} %get-tuple-element.48), channel_id=1, source_target_pairs={{3,0},{0,1},{1,2},{2,3},{7,4},{4,5},{5,6},{6,7},{11,8},{8,9},{9,10... | collective-permute-start | bytes 405512 | tf_op jit(solution)/shard_map/ppermute | solution.py:291
  25.5 3.0 %collective-permute-done.6.refs_3_ = bf16[16,4224]{1,0:T(8,128)(2,1)S(1)} collective-permute-done((bf16[16,4224]{1,0:T(8,128)(2,1)S(1)}, bf16[16,4224]{1,0:T(8,128)(2,1)S(1)}, u32[]{:S(2)}, u32[]{:S(2)}) %collective-permute-start.6) | collective-permute-done | bytes 135200 | tf_op jit(solution)/shard_map/ppermute | solution.py:291
  28.5 7.1 %collective-permute-done.5.refs_2_ = bf16[16,4224]{1,0:T(8,128)(2,1)S(1)} collective-permute-done((bf16[16,4224]{1,0:T(8,128)(2,1)S(1)}, bf16[16,4224]{1,0:T(8,128)(2,1)S(1)}, u32[]{:S(2)}, u32[]{:S(2)}) %collective-permute-start.5) | collective-permute-done | bytes 135200 | tf_op jit(solution)/shard_map/ppermute | solution.py:291
  35.6 0.0 collective-permute-done.4.refs_1_
  35.6 0.9 %gram.1 = (bf16[128,4352]{1,0:T(8,128)(2,1)S(1)}, f32[32,128]{1,0:T(8,128)S(1)}) custom-call(f32[16,4352]{1,0:T(8,128)S(1)} %get-tuple-element.47.refs_0_, bf16[16,4224]{1,0:T(8,128)(2,1)S(1)} %collective-permute-done.4.refs_1_, bf16[16,4224]{1,0:T(8,128)(2,1)S(1)} %collective-permute-done.5.refs_2_, bf16[16,4224]{1,0:T(8,128)(2,1)S(1)} %collective-permute-done.6.refs_3_), custom_call_target="tpu_custom_call" | custom-call | tf_op jit(solution)/shard_map/gram/pallas_call | solution.py:277
  36.5 0.0 collective-permute-start.7
  36.5 1.2 %collective-permute-done.7 = f32[32,128]{1,0:T(8,128)S(1)} collective-permute-done((f32[32,128]{1,0:T(8,128)S(1)}, f32[32,128]{1,0:T(8,128)S(1)}, u32[]{:S(2)}, u32[]{:S(2)}) %collective-permute-start.7) | collective-permute-done | bytes 16416 | tf_op jit(solution)/shard_map/gram_sum/ppermute | solution.py:431
  37.7 2.3 %collective-permute-start.10 = (f32[32,128]{1,0:T(8,128)S(1)}, f32[32,128]{1,0:T(8,128)S(1)}, u32[]{:S(2)}, u32[]{:S(2)}) collective-permute-start(f32[32,128]{1,0:T(8,128)S(1)} %add.12), channel_id=1, source_target_pairs={{0,24},{4,28},{8,16},{12,20},{16,8},{20,12},{24,0},{28,4},{1,25},{... | collective-permute-start | bytes 49160 | tf_op jit(solution)/shard_map/gram_sum/ppermute | solution.py:431
  40.0 0.7 %collective-permute-start.9 = (f32[32,128]{1,0:T(8,128)S(1)}, f32[32,128]{1,0:T(8,128)S(1)}, u32[]{:S(2)}, u32[]{:S(2)}) collective-permute-start(f32[32,128]{1,0:T(8,128)S(1)} %add.12), channel_id=1, source_target_pairs={{0,16},{4,20},{8,24},{12,28},{16,0},{20,4},{24,8},{28,12},{1,17},{... | collective-permute-start | bytes 49160 | tf_op jit(solution)/shard_map/gram_sum/ppermute | solution.py:431
  40.7 0.5 %collective-permute-start.8 = (f32[32,128]{1,0:T(8,128)S(1)}, f32[32,128]{1,0:T(8,128)S(1)}, u32[]{:S(2)}, u32[]{:S(2)}) collective-permute-start(f32[32,128]{1,0:T(8,128)S(1)} %add.12), channel_id=1, source_target_pairs={{0,8},{4,12},{8,0},{12,4},{16,24},{20,28},{24,16},{28,20},{1,9},{5... | collective-permute-start | bytes 49160 | tf_op jit(solution)/shard_map/gram_sum/ppermute | solution.py:431
  41.2 1.1 %collective-permute-done.10 = f32[32,128]{1,0:T(8,128)S(1)} collective-permute-done((f32[32,128]{1,0:T(8,128)S(1)}, f32[32,128]{1,0:T(8,128)S(1)}, u32[]{:S(2)}, u32[]{:S(2)}) %collective-permute-start.10) | collective-permute-done | bytes 16416 | tf_op jit(solution)/shard_map/gram_sum/ppermute | solution.py:431
  42.3 1.4 %collective-permute-done.9 = f32[32,128]{1,0:T(8,128)S(1)} collective-permute-done((f32[32,128]{1,0:T(8,128)S(1)}, f32[32,128]{1,0:T(8,128)S(1)}, u32[]{:S(2)}, u32[]{:S(2)}) %collective-permute-start.9) | collective-permute-done | bytes 16416 | tf_op jit(solution)/shard_map/gram_sum/ppermute | solution.py:431
  43.7 0.7 %collective-permute-done.8 = f32[32,128]{1,0:T(8,128)S(1)} collective-permute-done((f32[32,128]{1,0:T(8,128)S(1)}, f32[32,128]{1,0:T(8,128)S(1)}, u32[]{:S(2)}, u32[]{:S(2)}) %collective-permute-start.8) | collective-permute-done | bytes 16416 | tf_op jit(solution)/shard_map/gram_sum/ppermute | solution.py:431
  44.4 2.7 %orthonormal.1 = f32[16,4116]{1,0:T(8,128)} custom-call(f32[32,128]{1,0:T(8,128)S(1)} %add_add_fusion.gram_ref, bf16[128,4352]{1,0:T(8,128)(2,1)S(1)} %get-tuple-element.50.terms_ref), custom_call_target="tpu_custom_call" | custom-call | tf_op jit(solution)/shard_map/orthonormal/pallas_call | solution.py:277
  (2 shorter events, 0.0 us)
Async XLA Ops:
  0.0 4.8 %copy-start = (bf16[12,512,512]{2,1,0:T(8,128)(2,1)S(1)}, bf16[12,512,512]{2,1,0:T(8,128)(2,1)}, u32[]{:S(2)}) copy-start(bf16[12,512,512]{2,1,0:T(8,128)(2,1)} %ham_ref.7) | copy-start | bytes 18874372
  1.4 5.6 %collective-permute-start = (bf16[16,640]{1,0:T(8,128)(2,1)S(1)}, bf16[16,640]{1,0:T(8,128)(2,1)S(1)}, u32[]{:S(2)}, u32[]{:S(2)}) collective-permute-start(bf16[16,640]{1,0:T(8,128)(2,1)S(1)} %get-tuple-element.35), channel_id=1, source_target_pairs={{4,0},{8,4},{12,8},{16,12},{20,16},{24,20},{28,24},{0,28},{5,1},{9... | collective-permute-start | bytes 61448 | tf_op jit(solution)/shard_map/ppermute | solution.py:291
  10.0 4.8 %collective-permute-start.1 = (f32[16,640]{1,0:T(8,128)S(1)}, f32[16,640]{1,0:T(8,128)S(1)}, u32[]{:S(2)}, u32[]{:S(2)}) collective-permute-start(f32[16,640]{1,0:T(8,128)S(1)} %get-tuple-element.38), channel_id=1, source_target_pairs={{0,4},{4,0},{8,12},{12,8},{16,20},{20,16},{24,28},{28,24},{1,5},{5... | collective-permute-start | bytes 122888 | tf_op jit(solution)/shard_map/ppermute | solution.py:338
  10.1 4.8 %collective-permute-start.2 = (f32[16,640]{1,0:T(8,128)S(1)}, f32[16,640]{1,0:T(8,128)S(1)}, u32[]{:S(2)}, u32[]{:S(2)}) collective-permute-start(f32[16,640]{1,0:T(8,128)S(1)} %get-tuple-element.39), channel_id=1, source_target_pairs={{0,28},{4,8},{8,4},{12,16},{16,12},{20,24},{24,20},{28,0},{1,29},{... | collective-permute-start | bytes 122888 | tf_op jit(solution)/shard_map/ppermute | solution.py:339
  16.0 4.4 %collective-permute-start.3 = (f32[16,640]{1,0:T(8,128)S(1)}, f32[16,640]{1,0:T(8,128)S(1)}, u32[]{:S(2)}, u32[]{:S(2)}) collective-permute-start(f32[16,640]{1,0:T(8,128)S(1)} %get-tuple-element.46), channel_id=1, source_target_pairs={{28,0},{0,4},{4,8},{8,12},{12,16},{16,20},{20,24},{24,28},{29,1},{... | collective-permute-start | bytes 122888 | tf_op jit(solution)/shard_map/ppermute | solution.py:291
  20.8 7.7 %collective-permute-start.6 = (bf16[16,4224]{1,0:T(8,128)(2,1)S(1)}, bf16[16,4224]{1,0:T(8,128)(2,1)S(1)}, u32[]{:S(2)}, u32[]{:S(2)}) collective-permute-start(bf16[16,4224]{1,0:T(8,128)(2,1)S(1)} %get-tuple-element.48), channel_id=1, source_target_pairs={{1,0},{2,1},{3,2},{0,3},{5,4},{6,5},{7,6},{4,7},{9,8},{10,9},{11,1... | collective-permute-start | bytes 405512 | tf_op jit(solution)/shard_map/ppermute | solution.py:291
  24.5 11.1 %collective-permute-start.5 = (bf16[16,4224]{1,0:T(8,128)(2,1)S(1)}, bf16[16,4224]{1,0:T(8,128)(2,1)S(1)}, u32[]{:S(2)}, u32[]{:S(2)}) collective-permute-start(bf16[16,4224]{1,0:T(8,128)(2,1)S(1)} %get-tuple-element.48), channel_id=1, source_target_pairs={{2,0},{3,1},{0,2},{1,3},{6,4},{7,5},{4,6},{5,7},{10,8},{11,9},{8,1... | collective-permute-start | bytes 405512 | tf_op jit(solution)/shard_map/ppermute | solution.py:291
  24.5 11.1 %collective-permute-start.4 = (bf16[16,4224]{1,0:T(8,128)(2,1)S(1)}, bf16[16,4224]{1,0:T(8,128)(2,1)S(1)}, u32[]{:S(2)}, u32[]{:S(2)}) collective-permute-start(bf16[16,4224]{1,0:T(8,128)(2,1)S(1)} %get-tuple-element.48), channel_id=1, source_target_pairs={{3,0},{0,1},{1,2},{2,3},{7,4},{4,5},{5,6},{6,7},{11,8},{8,9},{9,10... | collective-permute-start | bytes 405512 | tf_op jit(solution)/shard_map/ppermute | solution.py:291
  36.5 1.2 %collective-permute-start.7 = (f32[32,128]{1,0:T(8,128)S(1)}, f32[32,128]{1,0:T(8,128)S(1)}, u32[]{:S(2)}, u32[]{:S(2)}) collective-permute-start(f32[32,128]{1,0:T(8,128)S(1)} %get-tuple-element.49), channel_id=1, source_target_pairs={{0,4},{4,0},{8,12},{12,8},{16,20},{20,16},{24,28},{28,24},{1,5},{5... | collective-permute-start | bytes 49160 | tf_op jit(solution)/shard_map/gram_sum/ppermute | solution.py:431
  37.7 4.6 %collective-permute-start.10 = (f32[32,128]{1,0:T(8,128)S(1)}, f32[32,128]{1,0:T(8,128)S(1)}, u32[]{:S(2)}, u32[]{:S(2)}) collective-permute-start(f32[32,128]{1,0:T(8,128)S(1)} %add.12), channel_id=1, source_target_pairs={{0,24},{4,28},{8,16},{12,20},{16,8},{20,12},{24,0},{28,4},{1,25},{... | collective-permute-start | bytes 49160 | tf_op jit(solution)/shard_map/gram_sum/ppermute | solution.py:431
  40.0 3.7 %collective-permute-start.9 = (f32[32,128]{1,0:T(8,128)S(1)}, f32[32,128]{1,0:T(8,128)S(1)}, u32[]{:S(2)}, u32[]{:S(2)}) collective-permute-start(f32[32,128]{1,0:T(8,128)S(1)} %add.12), channel_id=1, source_target_pairs={{0,16},{4,20},{8,24},{12,28},{16,0},{20,4},{24,8},{28,12},{1,17},{... | collective-permute-start | bytes 49160 | tf_op jit(solution)/shard_map/gram_sum/ppermute | solution.py:431
  40.7 3.7 %collective-permute-start.8 = (f32[32,128]{1,0:T(8,128)S(1)}, f32[32,128]{1,0:T(8,128)S(1)}, u32[]{:S(2)}, u32[]{:S(2)}) collective-permute-start(f32[32,128]{1,0:T(8,128)S(1)} %add.12), channel_id=1, source_target_pairs={{0,8},{4,12},{8,0},{12,4},{16,24},{20,28},{24,16},{28,20},{1,9},{5... | collective-permute-start | bytes 49160 | tf_op jit(solution)/shard_map/gram_sum/ppermute | solution.py:431

commit v6 on v5

--- a/solution.py
+++ b/solution.py
@@ -18,7 +18,7 @@
 BF16 = jnp.bfloat16
 VMEM = pl.BlockSpec(memory_space=pltpu.VMEM)
 HBM = pl.BlockSpec(memory_space=pltpu.HBM)
-LIMIT = 40 * 1024 * 1024
+LIMIT = 24 * 1024 * 1024
 
 
 def round_up(count, unit):
@@ -291,6 +291,17 @@
     return lax.ppermute(block, axis, route)
 
 
+def paired(groups):
+    return groups & (groups - 1) == 0
+
+
+def partner(block, axis, distance):
+    size = lax.axis_size(axis)
+    if paired(size):
+        return lax.ppermute(block, axis, [(i, i ^ distance) for i in range(size)])
+    return from_behind(block, axis, distance)
+
+
 def filter_field(psi, ham, conn, face_rows):
     bands, nodes = psi.shape
     elements, size = conn.shape
@@ -335,8 +346,8 @@
             flops=4 * 10**9, moved=10**6,
         )
     domains = lax.axis_size("space")
+    from_far = lax.ppermute(to_far, "space", [(i, ((i + 1 ^ 1) - 1) % domains) for i in range(domains)])
     from_near = lax.ppermute(to_near, "space", [(i, i ^ 1) for i in range(domains)])
-    from_far = lax.ppermute(to_far, "space", [(i, ((i + 1 ^ 1) - 1) % domains) for i in range(domains)])
     with jax.named_scope("off_face"):
         inside, high, faces = call(
             far_kernel,
@@ -365,13 +376,23 @@
     total = bands * len(blocks)
     me = lax.axis_index("band")
     for distance, block in enumerate(blocks):
-        source = pl.multiple_of(lax.rem(me - distance + len(blocks), len(blocks)) * bands, bands)
-        upper, lower = halves(widened(block[...].astype(F32)))
+        source = me ^ distance if paired(len(blocks)) else lax.rem(me - distance + len(blocks), len(blocks))
+        source = pl.multiple_of(source * bands, bands)
+        if distance == 0:
+            upper, lower = halves(block[...])
+            terms_ref[total:, :] = lower
+        else:
+            upper = widened(block[...])
         terms_ref[pl.ds(source, bands), :] = upper
-        terms_ref[pl.ds(total + source, bands), :] = lower
     terms = terms_ref[...]
     both = lax.dot_general(terms, terms, (((1,), (1,)), ((), ())), preferred_element_type=F32)
-    gram = both[:total, :total] + (both[:total, total:] + both[total:, :total]) + both[total:, total:]
+    down = jnp.concatenate([both[total:]] * len(blocks), axis=0)
+    across = jnp.concatenate([both[:, total:]] * len(blocks), axis=1)
+    corner = jnp.concatenate([down[:, total:]] * len(blocks), axis=1)
+    own_row = lax.broadcasted_iota(jnp.int32, (total, total), 0) // bands == me
+    own_column = lax.broadcasted_iota(jnp.int32, (total, total), 1) // bands == me
+    cross = jnp.where(own_row, down[:, :total], 0.0) + jnp.where(own_column, across[:total], 0.0)
+    gram = both[:total, :total] + (cross + jnp.where(own_row & own_column, corner, 0.0))
     gram_ref[...] = jnp.concatenate([gram[: total // 2], gram[total // 2 :]], axis=1)
 
 
@@ -412,10 +433,11 @@
     gram = jnp.concatenate([gram_ref[:, :total], gram_ref[:, total:]], axis=0)
     inverse_ref[...] = inverse_factor(gram / count)
     first = pl.multiple_of(lax.axis_index("band") * bands, bands)
-    upper, lower = halves(inverse_ref[pl.ds(first, bands), :])
-    rows = jnp.concatenate(
-        [jnp.concatenate([upper, upper], axis=1), jnp.concatenate([lower, lower], axis=1)], axis=0
-    )
+    own = inverse_ref[pl.ds(first, bands), :]
+    column = lax.broadcasted_iota(jnp.int32, own.shape, 1)
+    diagonal = jnp.where(column // bands == lax.axis_index("band"), own, 0.0)
+    diagonal = sum(diagonal[:, i : i + bands] for i in range(0, total, bands))
+    rows = jnp.concatenate(halves(jnp.concatenate([own, diagonal], axis=1)), axis=0)
     both = jnp.dot(rows, terms_ref[...], preferred_element_type=F32)
     out_ref[...] = (both[:bands] + both[bands:])[:, :nodes]
 
@@ -442,9 +464,9 @@
     total = groups * bands
     own = round_up(nodes, LANES)
     shape = jax.ShapeDtypeStruct
-    blocks = [following] + [from_behind(short, "band", i) for i in range(1, groups)]
+    blocks = [following] + [partner(short, "band", i) for i in range(1, groups)]
     with jax.named_scope("gram"):
-        terms, gram = call(gram_kernel, (shape((2 * total, own), BF16), shape((total // 2, 2 * total), F32)), blocks)
+        terms, gram = call(gram_kernel, (shape((total + bands, own), BF16), shape((total // 2, 2 * total), F32)), blocks)
     with jax.named_scope("gram_sum"):
         gram = space_sum(gram)
     with jax.named_scope("orthonormal"):

time: 47.3 us -> 46.4 us (0.981)
  waiting for transfers between devices: 16 us -> 15.5 us
    ppermute x5 -> x2, waiting for transfers between devices: 11.6 us -> 1.52 us  [from_behind(): return lax.ppermute(block, axis, route)]
    ppermute x0 -> x3, waiting for transfers between devices: none -> 9.45 us  [partner(): return lax.ppermute(block, axis, [(i, i ^ distance) for i in range(size)])]
    ppermute x5 -> x2, starting transfers between devices: 8.12 us -> 3.63 us  [from_behind(): return lax.ppermute(block, axis, route)]
    ppermute x0 -> x3, starting transfers between devices: none -> 4.45 us  [partner(): return lax.ppermute(block, axis, [(i, i ^ distance) for i in range(size)])]
  transfers between devices with their start and end apart: 11 -> 11, of which waited for: 7 -> 7; matrix products, arithmetic and copies ran while one was open for 0% -> 0% of each run, Pallas kernels for 16% -> 17%
where the time goes in v6:
time: 46.4 us; the launch traced here: 46.2 us
  Pallas kernels  16.9 us (36%)
  waiting for transfers between devices  15.5 us (33%)
  starting transfers between devices  13.7 us (30%)
    pallas_call x9, Pallas kernels, call(): pl.pallas_call(kernel, out_shape=out_shape, in_specs=[HBM if i in far els...  16.9 us
    ppermute x3, waiting for transfers between devices, partner(): return lax.ppermute(block, axis, [(i, i ^ distance) for i in range(size)])  9.45 us
    ppermute x4, waiting for transfers between devices, space_sum(): lax.ppermute(block, 'space', [(i, i ^ step * k) for i in range(size)])  4.49 us
    ppermute x3, starting transfers between devices, partner(): return lax.ppermute(block, axis, [(i, i ^ distance) for i in range(size)])  4.45 us
    ppermute x2, starting transfers between devices, from_behind(): return lax.ppermute(block, axis, route)  3.63 us
    ppermute x4, starting transfers between devices, space_sum(): lax.ppermute(block, 'space', [(i, i ^ step * k) for i in range(size)])  3.51 us
    ppermute x1, starting transfers between devices, filter_field(): lax.ppermute(to_far, 'space', [(i, ((i + 1 ^ 1) - 1) % domains) for i in...  2.08 us
    ppermute x2, waiting for transfers between devices, from_behind(): return lax.ppermute(block, axis, route)  1.52 us
  transfers between devices with their start and end apart: 11, of which 7 were waited for; matrix products, arithmetic and copies ran while one was open for 0% of the time, Pallas kernels for 17%

profile of v6, /device:TPU:0, one launch (start us, length us, event | category | flops | bytes accessed | tf_op | source)
XLA Modules:
  0.0 46.2 jit_solution(14886089836113546303)
XLA Ops:
  0.0 0.0 copy-start
  0.0 1.4 %face_values.1 = (bf16[16,640]{1,0:T(8,128)(2,1)S(1)}, f32[16,4352]{1,0:T(8,128)S(1)}, s32[12,512]{1,0:T(8,128)S(1)}, s32[1,640]{1,0:T(1,128)S(1)}) custom-call(f32[16,4116]{1,0:T(8,128)} %psi_hbm.1, s32[12,512]{1,0:T(8,128)} %conn_hbm.1, s32[588]{0:T(1024)} %face_hbm.1), custom_call_target="tpu_custom_call" | custom-call | flops 20000000000 | bytes 40000000 | tf_op jit(solution)/shard_map/face_values/pallas_call | solution.py:277
  1.4 3.4 %collective-permute-start = (bf16[16,640]{1,0:T(8,128)(2,1)S(1)}, bf16[16,640]{1,0:T(8,128)(2,1)S(1)}, u32[]{:S(2)}, u32[]{:S(2)}) collective-permute-start(bf16[16,640]{1,0:T(8,128)(2,1)S(1)} %get-tuple-element.35), channel_id=1, source_target_pairs={{4,0},{8,4},{12,8},{16,12},{20,16},{24,20},{28,24},{0,28},{5,1},{9... | collective-permute-start | bytes 61448 | tf_op jit(solution)/shard_map/ppermute | solution.py:291
  4.8 0.0 copy-done
  4.8 2.2 %interior.1 = (f32[16,6144]{1,0:T(8,128)S(1)}, s32[1,5376]{1,0:T(1,128)S(1)}, s32[1,768]{1,0:T(1,128)S(1)}, bf16[256,5376]{1,0:T(8,128)(2,1)S(1)}, bf16[256,768]{1,0:T(8,128)(2,1)S(1)}) custom-call(f32[16,4352]{1,0:T(8,128)S(1)} %get-tuple-element.28.psi_ref, s32[12,512]{1,0:T(8,128)S(1)} %get-tuple-element.29.conn_ref, bf16[12,512,512]{2,1,0:T(8,128)(2,1)S(1)} %copy-done), custom_call_target="tpu_custom_call" | custom-call | flops 4000000000 | bytes 8000000 | tf_op jit(solution)/shard_map/interior/pallas_call | solution.py:277
  7.0 0.0 collective-permute-done.ghost_ref
  7.0 2.9 %first_step.1 = (f32[16,4352]{1,0:T(8,128)S(1)}, f32[16,640]{1,0:T(8,128)S(1)}, f32[16,640]{1,0:T(8,128)S(1)}, f32[16,640]{1,0:T(8,128)S(1)}, f32[16,640]{1,0:T(8,128)S(1)}) custom-call(f32[16,4352]{1,0:T(8,128)S(1)} %get-tuple-element.28.psi_ref, s32[1,5376]{1,0:T(1,128)S(1)} %get-tuple-element.30.slots_ref, s32[1,768]{1,0:T(1,128)S(1)} %get-tuple-element.33.ghosts_ref, ...), custom_call_target="tpu_custom_call" | custom-call | flops 4000000000 | bytes 1000000 | tf_op jit(solution)/shard_map/first_step/pallas_call | solution.py:277
  10.0 0.1 collective-permute-start.1
  10.1 2.1 %collective-permute-start.2 = (f32[16,640]{1,0:T(8,128)S(1)}, f32[16,640]{1,0:T(8,128)S(1)}, u32[]{:S(2)}, u32[]{:S(2)}) collective-permute-start(f32[16,640]{1,0:T(8,128)S(1)} %get-tuple-element.39), channel_id=1, source_target_pairs={{0,28},{4,8},{8,4},{12,16},{16,12},{20,24},{24,20},{28,0},{1,29},{... | collective-permute-start | bytes 122888 | tf_op jit(solution)/shard_map/ppermute | solution.py:349
  12.1 2.7 %off_face.1 = (bf16[16,5376]{1,0:T(8,128)(2,1)S(1)}, s32[1,5376]{1,0:T(1,128)S(1)}, bf16[256,5376]{1,0:T(8,128)(2,1)S(1)}) custom-call(f32[16,4352]{1,0:T(8,128)S(1)} %get-tuple-element.37.own_in, s32[1,5376]{1,0:T(1,128)S(1)} %get-tuple-element.30.slots_ref, bf16[256,5376]{1,0:T(8,128)(2,1)S(1)} %get-tuple-element.31.hots_ref, ...), custom_call_target="tpu_custom_call" | custom-call | flops 4000000000 | bytes 1000000 | tf_op jit(solution)/shard_map/off_face/pallas_call | solution.py:277
  14.8 0.0 collective-permute-done.1.near_in
  14.8 0.0 collective-permute-done.2.far_in
  14.8 1.1 %second_step.1 = (bf16[16,6144]{1,0:T(8,128)(2,1)S(1)}, f32[16,640]{1,0:T(8,128)S(1)}) custom-call(bf16[16,5376]{1,0:T(8,128)(2,1)S(1)} %get-tuple-element.40.inside_ref, s32[1,5376]{1,0:T(1,128)S(1)} %get-tuple-element.41.high_ref, bf16[256,5376]{1,0:T(8,128)(2,1)S(1)} %get-tuple-element.42.faces_ref, s32[1,768]{1,0:T(1,128)S(1)} %get-tuple-element.33.ghosts_ref, ...), custom_call_target="tpu_custom_call" | custom-call | flops 4000000000 | bytes 1000000 | tf_op jit(solution)/shard_map/second_step/pallas_call | solution.py:277
  16.0 0.2 collective-permute-start.3
  16.2 2.8 %second_sums.1.own_in = f32[16,4352]{1,0:T(8,128)S(1)} custom-call(f32[16,4352]{1,0:T(8,128)S(1)} %get-tuple-element.28.psi_ref, s32[1,5376]{1,0:T(1,128)S(1)} %get-tuple-element.30.slots_ref, bf16[256,5376]{1,0:T(8,128)(2,1)S(1)} %get-tuple-element.31.hots_ref, bf16[12,512,512]{2,1,0:T(8,128)(2,1)S(1)} %copy-done, s32[1,640]{1,0:T(1,128)S(1)} %get-tuple-element.32.face_ref, ...), custom_call_target="tpu_custom_call" | custom-call | flops 4000000000 | bytes 8000000 | tf_op jit(solution)/shard_map/second_sums/pallas_call | solution.py:277
  19.0 1.5 %collective-permute-done.3.below_in = f32[16,640]{1,0:T(8,128)S(1)} collective-permute-done((f32[16,640]{1,0:T(8,128)S(1)}, f32[16,640]{1,0:T(8,128)S(1)}, u32[]{:S(2)}, u32[]{:S(2)}) %collective-permute-start.3) | collective-permute-done | bytes 40992 | tf_op jit(solution)/shard_map/ppermute | solution.py:291
  20.5 0.5 last_faces.1
  21.0 3.7 %collective-permute-start.6 = (bf16[16,4224]{1,0:T(8,128)(2,1)S(1)}, bf16[16,4224]{1,0:T(8,128)(2,1)S(1)}, u32[]{:S(2)}, u32[]{:S(2)}) collective-permute-start(bf16[16,4224]{1,0:T(8,128)(2,1)S(1)} %get-tuple-element.48), channel_id=1, source_target_pairs={{0,3},{1,2},{2,1},{3,0},{4,7},{5,6},{6,5},{7,4},{8,11},{9,10},{10,... | collective-permute-start | bytes 405512 | tf_op jit(solution)/shard_map/ppermute | solution.py:301
  24.7 0.0 collective-permute-start.5
  24.7 0.8 %collective-permute-start.4 = (bf16[16,4224]{1,0:T(8,128)(2,1)S(1)}, bf16[16,4224]{1,0:T(8,128)(2,1)S(1)}, u32[]{:S(2)}, u32[]{:S(2)}) collective-permute-start(bf16[16,4224]{1,0:T(8,128)(2,1)S(1)} %get-tuple-element.48), channel_id=1, source_target_pairs={{0,1},{1,0},{2,3},{3,2},{4,5},{5,4},{6,7},{7,6},{8,9},{9,8},{10,11... | collective-permute-start | bytes 405512 | tf_op jit(solution)/shard_map/ppermute | solution.py:301
  25.5 3.9 %collective-permute-done.6.refs_3_ = bf16[16,4224]{1,0:T(8,128)(2,1)S(1)} collective-permute-done((bf16[16,4224]{1,0:T(8,128)(2,1)S(1)}, bf16[16,4224]{1,0:T(8,128)(2,1)S(1)}, u32[]{:S(2)}, u32[]{:S(2)}) %collective-permute-start.6) | collective-permute-done | bytes 135200 | tf_op jit(solution)/shard_map/ppermute | solution.py:301
  29.4 5.5 %collective-permute-done.5.refs_2_ = bf16[16,4224]{1,0:T(8,128)(2,1)S(1)} collective-permute-done((bf16[16,4224]{1,0:T(8,128)(2,1)S(1)}, bf16[16,4224]{1,0:T(8,128)(2,1)S(1)}, u32[]{:S(2)}, u32[]{:S(2)}) %collective-permute-start.5) | collective-permute-done | bytes 135200 | tf_op jit(solution)/shard_map/ppermute | solution.py:301
  34.9 0.0 collective-permute-done.4.refs_1_
  34.9 0.6 %gram.1 = (bf16[80,4352]{1,0:T(8,128)(2,1)S(1)}, f32[32,128]{1,0:T(8,128)S(1)}) custom-call(f32[16,4352]{1,0:T(8,128)S(1)} %get-tuple-element.47.refs_0_, bf16[16,4224]{1,0:T(8,128)(2,1)S(1)} %collective-permute-done.4.refs_1_, bf16[16,4224]{1,0:T(8,128)(2,1)S(1)} %collective-permute-done.5.refs_2_, bf16[16,4224]{1,0:T(8,128)(2,1)S(1)} %collective-permute-done.6.refs_3_), custom_call_target="tpu_custom_call" | custom-call | tf_op jit(solution)/shard_map/gram/pallas_call | solution.py:277
  35.5 0.0 collective-permute-start.7
  35.5 1.2 %collective-permute-done.7 = f32[32,128]{1,0:T(8,128)S(1)} collective-permute-done((f32[32,128]{1,0:T(8,128)S(1)}, f32[32,128]{1,0:T(8,128)S(1)}, u32[]{:S(2)}, u32[]{:S(2)}) %collective-permute-start.7) | collective-permute-done | bytes 16416 | tf_op jit(solution)/shard_map/gram_sum/ppermute | solution.py:453
  36.7 2.7 %collective-permute-start.10 = (f32[32,128]{1,0:T(8,128)S(1)}, f32[32,128]{1,0:T(8,128)S(1)}, u32[]{:S(2)}, u32[]{:S(2)}) collective-permute-start(f32[32,128]{1,0:T(8,128)S(1)} %add.12), channel_id=1, source_target_pairs={{0,24},{4,28},{8,16},{12,20},{16,8},{20,12},{24,0},{28,4},{1,25},{... | collective-permute-start | bytes 49160 | tf_op jit(solution)/shard_map/gram_sum/ppermute | solution.py:453
  39.4 0.3 collective-permute-start.9
  39.8 0.4 collective-permute-start.8
  40.2 1.1 %collective-permute-done.10 = f32[32,128]{1,0:T(8,128)S(1)} collective-permute-done((f32[32,128]{1,0:T(8,128)S(1)}, f32[32,128]{1,0:T(8,128)S(1)}, u32[]{:S(2)}, u32[]{:S(2)}) %collective-permute-start.10) | collective-permute-done | bytes 16416 | tf_op jit(solution)/shard_map/gram_sum/ppermute | solution.py:453
  41.4 1.8 %collective-permute-done.9 = f32[32,128]{1,0:T(8,128)S(1)} collective-permute-done((f32[32,128]{1,0:T(8,128)S(1)}, f32[32,128]{1,0:T(8,128)S(1)}, u32[]{:S(2)}, u32[]{:S(2)}) %collective-permute-start.9) | collective-permute-done | bytes 16416 | tf_op jit(solution)/shard_map/gram_sum/ppermute | solution.py:453
  43.2 0.3 collective-permute-done.8
  43.5 2.7 %orthonormal.1 = f32[16,4116]{1,0:T(8,128)} custom-call(f32[32,128]{1,0:T(8,128)S(1)} %add_add_fusion.gram_ref, bf16[80,4352]{1,0:T(8,128)(2,1)S(1)} %get-tuple-element.50.terms_ref), custom_call_target="tpu_custom_call" | custom-call | tf_op jit(solution)/shard_map/orthonormal/pallas_call | solution.py:277
  (2 shorter events, 0.0 us)
Async XLA Ops:
  0.0 4.8 %copy-start = (bf16[12,512,512]{2,1,0:T(8,128)(2,1)S(1)}, bf16[12,512,512]{2,1,0:T(8,128)(2,1)}, u32[]{:S(2)}) copy-start(bf16[12,512,512]{2,1,0:T(8,128)(2,1)} %ham_ref.7) | copy-start | bytes 18874372
  1.4 5.6 %collective-permute-start = (bf16[16,640]{1,0:T(8,128)(2,1)S(1)}, bf16[16,640]{1,0:T(8,128)(2,1)S(1)}, u32[]{:S(2)}, u32[]{:S(2)}) collective-permute-start(bf16[16,640]{1,0:T(8,128)(2,1)S(1)} %get-tuple-element.35), channel_id=1, source_target_pairs={{4,0},{8,4},{12,8},{16,12},{20,16},{24,20},{28,24},{0,28},{5,1},{9... | collective-permute-start | bytes 61448 | tf_op jit(solution)/shard_map/ppermute | solution.py:291
  10.0 4.9 %collective-permute-start.1 = (f32[16,640]{1,0:T(8,128)S(1)}, f32[16,640]{1,0:T(8,128)S(1)}, u32[]{:S(2)}, u32[]{:S(2)}) collective-permute-start(f32[16,640]{1,0:T(8,128)S(1)} %get-tuple-element.38), channel_id=1, source_target_pairs={{0,4},{4,0},{8,12},{12,8},{16,20},{20,16},{24,28},{28,24},{1,5},{5... | collective-permute-start | bytes 122888 | tf_op jit(solution)/shard_map/ppermute | solution.py:350
  10.1 4.8 %collective-permute-start.2 = (f32[16,640]{1,0:T(8,128)S(1)}, f32[16,640]{1,0:T(8,128)S(1)}, u32[]{:S(2)}, u32[]{:S(2)}) collective-permute-start(f32[16,640]{1,0:T(8,128)S(1)} %get-tuple-element.39), channel_id=1, source_target_pairs={{0,28},{4,8},{8,4},{12,16},{16,12},{20,24},{24,20},{28,0},{1,29},{... | collective-permute-start | bytes 122888 | tf_op jit(solution)/shard_map/ppermute | solution.py:349
  16.0 4.6 %collective-permute-start.3 = (f32[16,640]{1,0:T(8,128)S(1)}, f32[16,640]{1,0:T(8,128)S(1)}, u32[]{:S(2)}, u32[]{:S(2)}) collective-permute-start(f32[16,640]{1,0:T(8,128)S(1)} %get-tuple-element.46), channel_id=1, source_target_pairs={{28,0},{0,4},{4,8},{8,12},{12,16},{16,20},{20,24},{24,28},{29,1},{... | collective-permute-start | bytes 122888 | tf_op jit(solution)/shard_map/ppermute | solution.py:291
  21.0 8.4 %collective-permute-start.6 = (bf16[16,4224]{1,0:T(8,128)(2,1)S(1)}, bf16[16,4224]{1,0:T(8,128)(2,1)S(1)}, u32[]{:S(2)}, u32[]{:S(2)}) collective-permute-start(bf16[16,4224]{1,0:T(8,128)(2,1)S(1)} %get-tuple-element.48), channel_id=1, source_target_pairs={{0,3},{1,2},{2,1},{3,0},{4,7},{5,6},{6,5},{7,4},{8,11},{9,10},{10,... | collective-permute-start | bytes 405512 | tf_op jit(solution)/shard_map/ppermute | solution.py:301
  24.7 10.2 %collective-permute-start.5 = (bf16[16,4224]{1,0:T(8,128)(2,1)S(1)}, bf16[16,4224]{1,0:T(8,128)(2,1)S(1)}, u32[]{:S(2)}, u32[]{:S(2)}) collective-permute-start(bf16[16,4224]{1,0:T(8,128)(2,1)S(1)} %get-tuple-element.48), channel_id=1, source_target_pairs={{0,2},{1,3},{2,0},{3,1},{4,6},{5,7},{6,4},{7,5},{8,10},{9,11},{10,... | collective-permute-start | bytes 405512 | tf_op jit(solution)/shard_map/ppermute | solution.py:301
  24.7 10.2 %collective-permute-start.4 = (bf16[16,4224]{1,0:T(8,128)(2,1)S(1)}, bf16[16,4224]{1,0:T(8,128)(2,1)S(1)}, u32[]{:S(2)}, u32[]{:S(2)}) collective-permute-start(bf16[16,4224]{1,0:T(8,128)(2,1)S(1)} %get-tuple-element.48), channel_id=1, source_target_pairs={{0,1},{1,0},{2,3},{3,2},{4,5},{5,4},{6,7},{7,6},{8,9},{9,8},{10,11... | collective-permute-start | bytes 405512 | tf_op jit(solution)/shard_map/ppermute | solution.py:301
  35.5 1.2 %collective-permute-start.7 = (f32[32,128]{1,0:T(8,128)S(1)}, f32[32,128]{1,0:T(8,128)S(1)}, u32[]{:S(2)}, u32[]{:S(2)}) collective-permute-start(f32[32,128]{1,0:T(8,128)S(1)} %get-tuple-element.49), channel_id=1, source_target_pairs={{0,4},{4,0},{8,12},{12,8},{16,20},{20,16},{24,28},{28,24},{1,5},{5... | collective-permute-start | bytes 49160 | tf_op jit(solution)/shard_map/gram_sum/ppermute | solution.py:453
  36.7 4.6 %collective-permute-start.10 = (f32[32,128]{1,0:T(8,128)S(1)}, f32[32,128]{1,0:T(8,128)S(1)}, u32[]{:S(2)}, u32[]{:S(2)}) collective-permute-start(f32[32,128]{1,0:T(8,128)S(1)} %add.12), channel_id=1, source_target_pairs={{0,24},{4,28},{8,16},{12,20},{16,8},{20,12},{24,0},{28,4},{1,25},{... | collective-permute-start | bytes 49160 | tf_op jit(solution)/shard_map/gram_sum/ppermute | solution.py:453
  39.4 3.7 %collective-permute-start.9 = (f32[32,128]{1,0:T(8,128)S(1)}, f32[32,128]{1,0:T(8,128)S(1)}, u32[]{:S(2)}, u32[]{:S(2)}) collective-permute-start(f32[32,128]{1,0:T(8,128)S(1)} %add.12), channel_id=1, source_target_pairs={{0,16},{4,20},{8,24},{12,28},{16,0},{20,4},{24,8},{28,12},{1,17},{... | collective-permute-start | bytes 49160 | tf_op jit(solution)/shard_map/gram_sum/ppermute | solution.py:453
  39.8 3.7 %collective-permute-start.8 = (f32[32,128]{1,0:T(8,128)S(1)}, f32[32,128]{1,0:T(8,128)S(1)}, u32[]{:S(2)}, u32[]{:S(2)}) collective-permute-start(f32[32,128]{1,0:T(8,128)S(1)} %add.12), channel_id=1, source_target_pairs={{0,8},{4,12},{8,0},{12,4},{16,24},{20,28},{24,16},{28,20},{1,9},{5... | collective-permute-start | bytes 49160 | tf_op jit(solution)/shard_map/gram_sum/ppermute | solution.py:453

commit v7 on v6

--- a/solution.py
+++ b/solution.py
@@ -82,16 +82,23 @@
         out_ref[:, tile] = pick(rows, high[:, tile], hots_ref[:, tile], out_ref.shape[0]).astype(out_ref.dtype)
 
 
-def spread_into(sums_ref, values_ref, high):
-    bands = values_ref.shape[0]
-    blocks = sums_ref.shape[0] // (2 * bands)
-    for tile in tiles(high.shape[1]):
-        at = high[:, tile]
-        upper, lower = (part.astype(F32) for part in halves(values_ref[:, tile]))
-        for i in range(blocks):
-            here = at == i
-            sums_ref[i * bands : (i + 1) * bands, tile] = jnp.where(here, upper, 0.0).astype(BF16)
-            sums_ref[(blocks + i) * bands : (blocks + i + 1) * bands, tile] = jnp.where(here, lower, 0.0).astype(BF16)
+def spread_once(values, high, blocks):
+    return jnp.concatenate([jnp.where(high == i, values, 0.0).astype(BF16) for i in range(blocks)], axis=0)
+
+
+def scatter_sum(values_ref, high, hots_ref, blocks, once=False):
+    total = None
+    for tile in tiles(high.shape[1], 2 * LANES):
+        rows = (spread_once if once else spread)(values_ref[:, tile], high[:, tile], blocks)
+        part = lax.dot_general(
+            rows, hots_ref[:, tile],
+            (((1,), (1,)), ((), ())), preferred_element_type=F32,
+        )
+        total = part if total is None else total + part
+    if once:
+        return total
+    count = total.shape[0] // 2
+    return total[:count] + total[count:]
 
 
 def split_products(products, inner_ref, top_ref, first):
@@ -160,7 +167,7 @@
 
 def first_kernel(
     psi_ref, slots_ref, ghosts_ref, hots_ref, hosts_ref, ham_ref, face_ref, ghost_ref, part_ref,
-    own_ref, upper_ref, low_ref, near_ref, far_ref, sums, top_sums, inner, top, outside,
+    own_ref, upper_ref, low_ref, near_ref, far_ref, inner, top, outside,
 ):
     bands, own = psi_ref.shape
     elements, size = ham_ref.shape[:2]
@@ -174,11 +181,10 @@
             for e in pair
         ]
         split_products(products, inner, top, pair[0])
-    spread_into(sums, inner, slots_ref[...] >> 8)
-    spread_into(top_sums, top, ghosts >> 8)
-    upper = unstacked(gathered_sum(top_sums[...], hosts_ref[...]), bands)[:, :face_count] / HALF_WIDTH
+    upper = scatter_sum(top, ghosts >> 8, hosts_ref, round_up(face_count, LANES) // LANES)
+    upper = unstacked(upper, bands)[:, :face_count] / HALF_WIDTH
     upper_ref[...] = upper
-    total = unstacked(gathered_sum(sums[...], hots_ref[...]), bands)
+    total = unstacked(scatter_sum(inner, slots_ref[...] >> 8, hots_ref, own // LANES, True), bands)
     current = (total - CENTER * psi_ref[...]) / HALF_WIDTH
     own_ref[...] = current
     face = face_ref[...]
@@ -216,7 +222,7 @@
 
 def second_kernel(
     inside_ref, high_ref, faces_ref, ghosts_ref, hosts_ref, ham_ref, low_in, upper_in, near_in, far_in,
-    field_ref, upper_ref, top_sums, inside, top, outside,
+    field_ref, upper_ref, inside, top, outside,
 ):
     bands, face_count = upper_in.shape
     elements, size = ham_ref.shape[:2]
@@ -240,13 +246,12 @@
             product = jnp.dot(values, ham_ref[e, :, size - 128 :], preferred_element_type=F32)
             products.append(product[:, 128 - FACE_EL :])
         top[:, pair[0] * FACE_EL : (pair[-1] + 1) * FACE_EL] = jnp.concatenate(products, axis=1)
-    spread_into(top_sums, top, ghosts >> 8)
-    total = unstacked(gathered_sum(top_sums[...], hosts_ref[...]), bands)
+    total = unstacked(scatter_sum(top, ghosts >> 8, hosts_ref, round_up(face_count, LANES) // LANES), bands)
     upper_ref[...] = total[:, :face_count] * (2.0 / HALF_WIDTH)
 
 
 def third_kernel(
-    psi_ref, slots_ref, hots_ref, ham_ref, face_ref, own_in, near_in, far_in, field_ref, own_ref, sums, inner
+    psi_ref, slots_ref, hots_ref, ham_ref, face_ref, own_in, near_in, far_in, field_ref, own_ref, inner
 ):
     bands, own = own_in.shape
     elements, size = ham_ref.shape[:2]
@@ -258,8 +263,7 @@
             jnp.dot(field_ref[:, e * size : (e + 1) * size], ham_ref[e], preferred_element_type=F32) for e in pair
         ]
         split_products(products, inner, None, pair[0])
-    spread_into(sums, inner, slots_ref[...] >> 8)
-    total = unstacked(gathered_sum(sums[...], hots_ref[...]), bands)
+    total = unstacked(scatter_sum(inner, slots_ref[...] >> 8, hots_ref, own // LANES, True), bands)
     current = own_in[...] + unstacked(added, bands)
     own_ref[...] = 2.0 * ((total - CENTER * current) / HALF_WIDTH) - psi_ref[...]
 
@@ -313,8 +317,6 @@
     shape = jax.ShapeDtypeStruct
     face_field = shape((bands, faces), F32)
     own_field = shape((bands, own), F32)
-    sums = pltpu.VMEM((2 * own // LANES * bands, inner_count), BF16)
-    top_sums = pltpu.VMEM((2 * round_up(faces, LANES) // LANES * bands, face_count), BF16)
     inner = pltpu.VMEM((bands, inner_count), F32)
     top = pltpu.VMEM((bands, face_count), F32)
     inside_field = pltpu.VMEM((bands, inner_count), BF16)
@@ -342,7 +344,7 @@
     with jax.named_scope("first_step"):
         current, upper, low, to_near, to_far = call(
             first_kernel, (own_field, *[face_field] * 4),
-            (wide, slots, ghosts, hots, hosts, ham, face, ghost, part), (sums, top_sums, inner, top, outside),
+            (wide, slots, ghosts, hots, hosts, ham, face, ghost, part), (inner, top, outside),
             flops=4 * 10**9, moved=10**6,
         )
     domains = lax.axis_size("space")
@@ -357,13 +359,13 @@
     with jax.named_scope("second_step"):
         field, upper = call(
             second_kernel, (shape((bands, elements * size), BF16), face_field),
-            (inside, high, faces, ghosts, hosts, ham, low, upper, from_near, from_far), (top_sums, inside_field, top, outside),
+            (inside, high, faces, ghosts, hosts, ham, low, upper, from_near, from_far), (inside_field, top, outside),
             flops=4 * 10**9, moved=10**6,
         )
     from_below = from_behind(upper, "space", 1)
     with jax.named_scope("second_sums"):
         following = call(
-            third_kernel, own_field, (wide, slots, hots, ham, face, current, from_near, from_far, field), (sums, inner),
+            third_kernel, own_field, (wide, slots, hots, ham, face, current, from_near, from_far, field), (inner,),
             flops=4 * 10**9, moved=8 * 10**6,
         )
     with jax.named_scope("last_faces"):

time: 46.4 us -> 45.2 us (0.974)
  Pallas kernels: 16.9 us -> 15.4 us
    pallas_call x9, Pallas kernels: 16.9 us -> 15.4 us  [call(): pl.pallas_call(kernel, out_shape=out_shape, in_specs=[HBM if i in far els...]
    ppermute x2, waiting for transfers between devices: 1.52 us -> 2.29 us  [from_behind(): return lax.ppermute(block, axis, route)]
    ppermute x3, waiting for transfers between devices: 9.45 us -> 8.69 us  [partner(): return lax.ppermute(block, axis, [(i, i ^ distance) for i in range(size)])]
  transfers between devices with their start and end apart: 11 -> 11, of which waited for: 7 -> 7; matrix products, arithmetic and copies ran while one was open for 0% -> 0% of each run, Pallas kernels for 17% -> 15%
where the time goes in v7:
time: 45.2 us; the launch traced here: 45.1 us
  waiting for transfers between devices  15.9 us (35%)
  Pallas kernels  15.4 us (34%)
  starting transfers between devices  13.7 us (30%)
    pallas_call x9, Pallas kernels, call(): pl.pallas_call(kernel, out_shape=out_shape, in_specs=[HBM if i in far els...  15.4 us
    ppermute x3, waiting for transfers between devices, partner(): return lax.ppermute(block, axis, [(i, i ^ distance) for i in range(size)])  8.69 us
    ppermute x4, waiting for transfers between devices, space_sum(): lax.ppermute(block, 'space', [(i, i ^ step * k) for i in range(size)])  4.91 us
    ppermute x3, starting transfers between devices, partner(): return lax.ppermute(block, axis, [(i, i ^ distance) for i in range(size)])  4.45 us
    ppermute x4, starting transfers between devices, space_sum(): lax.ppermute(block, 'space', [(i, i ^ step * k) for i in range(size)])  3.63 us
    ppermute x2, starting transfers between devices, from_behind(): return lax.ppermute(block, axis, route)  3.44 us
    ppermute x2, waiting for transfers between devices, from_behind(): return lax.ppermute(block, axis, route)  2.29 us
    ppermute x1, starting transfers between devices, filter_field(): lax.ppermute(to_far, 'space', [(i, ((i + 1 ^ 1) - 1) % domains) for i in...  2.07 us
  transfers between devices with their start and end apart: 11, of which 7 were waited for; matrix products, arithmetic and copies ran while one was open for 0% of the time, Pallas kernels for 15%

profile of v7, /device:TPU:0, one launch (start us, length us, event | category | flops | bytes accessed | tf_op | source)
XLA Modules:
  0.0 45.1 jit_solution(1257776545514743070)
XLA Ops:
  0.0 0.0 copy-start
  0.0 1.4 %face_values.1 = (bf16[16,640]{1,0:T(8,128)(2,1)S(1)}, f32[16,4352]{1,0:T(8,128)S(1)}, s32[12,512]{1,0:T(8,128)S(1)}, s32[1,640]{1,0:T(1,128)S(1)}) custom-call(f32[16,4116]{1,0:T(8,128)} %psi_hbm.1, s32[12,512]{1,0:T(8,128)} %conn_hbm.1, s32[588]{0:T(1024)} %face_hbm.1), custom_call_target="tpu_custom_call" | custom-call | flops 20000000000 | bytes 40000000 | tf_op jit(solution)/shard_map/face_values/pallas_call | solution.py:281
  1.4 3.4 %collective-permute-start = (bf16[16,640]{1,0:T(8,128)(2,1)S(1)}, bf16[16,640]{1,0:T(8,128)(2,1)S(1)}, u32[]{:S(2)}, u32[]{:S(2)}) collective-permute-start(bf16[16,640]{1,0:T(8,128)(2,1)S(1)} %get-tuple-element.35), channel_id=1, source_target_pairs={{4,0},{8,4},{12,8},{16,12},{20,16},{24,20},{28,24},{0,28},{5,1},{9... | collective-permute-start | bytes 61448 | tf_op jit(solution)/shard_map/ppermute | solution.py:295
  4.8 0.0 copy-done
  4.8 2.2 %interior.1 = (f32[16,6144]{1,0:T(8,128)S(1)}, s32[1,5376]{1,0:T(1,128)S(1)}, s32[1,768]{1,0:T(1,128)S(1)}, bf16[256,5376]{1,0:T(8,128)(2,1)S(1)}, bf16[256,768]{1,0:T(8,128)(2,1)S(1)}) custom-call(f32[16,4352]{1,0:T(8,128)S(1)} %get-tuple-element.28.psi_ref, s32[12,512]{1,0:T(8,128)S(1)} %get-tuple-element.29.conn_ref, bf16[12,512,512]{2,1,0:T(8,128)(2,1)S(1)} %copy-done), custom_call_target="tpu_custom_call" | custom-call | flops 4000000000 | bytes 8000000 | tf_op jit(solution)/shard_map/interior/pallas_call | solution.py:281
  7.0 0.0 collective-permute-done.ghost_ref
  7.0 2.2 %first_step.1 = (f32[16,4352]{1,0:T(8,128)S(1)}, f32[16,640]{1,0:T(8,128)S(1)}, f32[16,640]{1,0:T(8,128)S(1)}, f32[16,640]{1,0:T(8,128)S(1)}, f32[16,640]{1,0:T(8,128)S(1)}) custom-call(f32[16,4352]{1,0:T(8,128)S(1)} %get-tuple-element.28.psi_ref, s32[1,5376]{1,0:T(1,128)S(1)} %get-tuple-element.30.slots_ref, s32[1,768]{1,0:T(1,128)S(1)} %get-tuple-element.33.ghosts_ref, ...), custom_call_target="tpu_custom_call" | custom-call | flops 4000000000 | bytes 1000000 | tf_op jit(solution)/shard_map/first_step/pallas_call | solution.py:281
  9.2 0.1 collective-permute-start.1
  9.3 2.1 %collective-permute-start.2 = (f32[16,640]{1,0:T(8,128)S(1)}, f32[16,640]{1,0:T(8,128)S(1)}, u32[]{:S(2)}, u32[]{:S(2)}) collective-permute-start(f32[16,640]{1,0:T(8,128)S(1)} %get-tuple-element.39), channel_id=1, source_target_pairs={{0,28},{4,8},{8,4},{12,16},{16,12},{20,24},{24,20},{28,0},{1,29},{... | collective-permute-start | bytes 122888 | tf_op jit(solution)/shard_map/ppermute | solution.py:351
  11.4 2.7 %off_face.1 = (bf16[16,5376]{1,0:T(8,128)(2,1)S(1)}, s32[1,5376]{1,0:T(1,128)S(1)}, bf16[256,5376]{1,0:T(8,128)(2,1)S(1)}) custom-call(f32[16,4352]{1,0:T(8,128)S(1)} %get-tuple-element.37.own_in, s32[1,5376]{1,0:T(1,128)S(1)} %get-tuple-element.30.slots_ref, bf16[256,5376]{1,0:T(8,128)(2,1)S(1)} %get-tuple-element.31.hots_ref, ...), custom_call_target="tpu_custom_call" | custom-call | flops 4000000000 | bytes 1000000 | tf_op jit(solution)/shard_map/off_face/pallas_call | solution.py:281
  14.1 0.0 collective-permute-done.1.near_in
  14.1 0.0 collective-permute-done.2.far_in
  14.1 1.1 %second_step.1 = (bf16[16,6144]{1,0:T(8,128)(2,1)S(1)}, f32[16,640]{1,0:T(8,128)S(1)}) custom-call(bf16[16,5376]{1,0:T(8,128)(2,1)S(1)} %get-tuple-element.40.inside_ref, s32[1,5376]{1,0:T(1,128)S(1)} %get-tuple-element.41.high_ref, bf16[256,5376]{1,0:T(8,128)(2,1)S(1)} %get-tuple-element.42.faces_ref, s32[1,768]{1,0:T(1,128)S(1)} %get-tuple-element.33.ghosts_ref, ...), custom_call_target="tpu_custom_call" | custom-call | flops 4000000000 | bytes 1000000 | tf_op jit(solution)/shard_map/second_step/pallas_call | solution.py:281
  15.2 0.1 collective-permute-start.3
  15.3 2.0 %second_sums.1.own_in = f32[16,4352]{1,0:T(8,128)S(1)} custom-call(f32[16,4352]{1,0:T(8,128)S(1)} %get-tuple-element.28.psi_ref, s32[1,5376]{1,0:T(1,128)S(1)} %get-tuple-element.30.slots_ref, bf16[256,5376]{1,0:T(8,128)(2,1)S(1)} %get-tuple-element.31.hots_ref, bf16[12,512,512]{2,1,0:T(8,128)(2,1)S(1)} %copy-done, s32[1,640]{1,0:T(1,128)S(1)} %get-tuple-element.32.face_ref, ...), custom_call_target="tpu_custom_call" | custom-call | flops 4000000000 | bytes 8000000 | tf_op jit(solution)/shard_map/second_sums/pallas_call | solution.py:281
  17.3 2.3 %collective-permute-done.3.below_in = f32[16,640]{1,0:T(8,128)S(1)} collective-permute-done((f32[16,640]{1,0:T(8,128)S(1)}, f32[16,640]{1,0:T(8,128)S(1)}, u32[]{:S(2)}, u32[]{:S(2)}) %collective-permute-start.3) | collective-permute-done | bytes 40992 | tf_op jit(solution)/shard_map/ppermute | solution.py:295
  19.6 0.5 last_faces.1
  20.0 3.7 %collective-permute-start.6 = (bf16[16,4224]{1,0:T(8,128)(2,1)S(1)}, bf16[16,4224]{1,0:T(8,128)(2,1)S(1)}, u32[]{:S(2)}, u32[]{:S(2)}) collective-permute-start(bf16[16,4224]{1,0:T(8,128)(2,1)S(1)} %get-tuple-element.48), channel_id=1, source_target_pairs={{0,3},{1,2},{2,1},{3,0},{4,7},{5,6},{6,5},{7,4},{8,11},{9,10},{10,... | collective-permute-start | bytes 405512 | tf_op jit(solution)/shard_map/ppermute | solution.py:305
  23.7 0.0 collective-permute-start.5
  23.7 0.8 %collective-permute-start.4 = (bf16[16,4224]{1,0:T(8,128)(2,1)S(1)}, bf16[16,4224]{1,0:T(8,128)(2,1)S(1)}, u32[]{:S(2)}, u32[]{:S(2)}) collective-permute-start(bf16[16,4224]{1,0:T(8,128)(2,1)S(1)} %get-tuple-element.48), channel_id=1, source_target_pairs={{0,1},{1,0},{2,3},{3,2},{4,5},{5,4},{6,7},{7,6},{8,9},{9,8},{10,11... | collective-permute-start | bytes 405512 | tf_op jit(solution)/shard_map/ppermute | solution.py:305
  24.5 3.5 %collective-permute-done.6.refs_3_ = bf16[16,4224]{1,0:T(8,128)(2,1)S(1)} collective-permute-done((bf16[16,4224]{1,0:T(8,128)(2,1)S(1)}, bf16[16,4224]{1,0:T(8,128)(2,1)S(1)}, u32[]{:S(2)}, u32[]{:S(2)}) %collective-permute-start.6) | collective-permute-done | bytes 135200 | tf_op jit(solution)/shard_map/ppermute | solution.py:305
  28.0 5.2 %collective-permute-done.5.refs_2_ = bf16[16,4224]{1,0:T(8,128)(2,1)S(1)} collective-permute-done((bf16[16,4224]{1,0:T(8,128)(2,1)S(1)}, bf16[16,4224]{1,0:T(8,128)(2,1)S(1)}, u32[]{:S(2)}, u32[]{:S(2)}) %collective-permute-start.5) | collective-permute-done | bytes 135200 | tf_op jit(solution)/shard_map/ppermute | solution.py:305
  33.2 0.0 collective-permute-done.4.refs_1_
  33.2 0.6 %gram.1 = (bf16[80,4352]{1,0:T(8,128)(2,1)S(1)}, f32[32,128]{1,0:T(8,128)S(1)}) custom-call(f32[16,4352]{1,0:T(8,128)S(1)} %get-tuple-element.47.refs_0_, bf16[16,4224]{1,0:T(8,128)(2,1)S(1)} %collective-permute-done.4.refs_1_, bf16[16,4224]{1,0:T(8,128)(2,1)S(1)} %collective-permute-done.5.refs_2_, bf16[16,4224]{1,0:T(8,128)(2,1)S(1)} %collective-permute-done.6.refs_3_), custom_call_target="tpu_custom_call" | custom-call | tf_op jit(solution)/shard_map/gram/pallas_call | solution.py:281
  33.8 0.0 collective-permute-start.7
  33.8 1.2 %collective-permute-done.7 = f32[32,128]{1,0:T(8,128)S(1)} collective-permute-done((f32[32,128]{1,0:T(8,128)S(1)}, f32[32,128]{1,0:T(8,128)S(1)}, u32[]{:S(2)}, u32[]{:S(2)}) %collective-permute-start.7) | collective-permute-done | bytes 16416 | tf_op jit(solution)/shard_map/gram_sum/ppermute | solution.py:455
  35.0 2.8 %collective-permute-start.10 = (f32[32,128]{1,0:T(8,128)S(1)}, f32[32,128]{1,0:T(8,128)S(1)}, u32[]{:S(2)}, u32[]{:S(2)}) collective-permute-start(f32[32,128]{1,0:T(8,128)S(1)} %add.12), channel_id=1, source_target_pairs={{0,24},{4,28},{8,16},{12,20},{16,8},{20,12},{24,0},{28,4},{1,25},{... | collective-permute-start | bytes 49160 | tf_op jit(solution)/shard_map/gram_sum/ppermute | solution.py:455
  37.8 0.8 %collective-permute-start.9 = (f32[32,128]{1,0:T(8,128)S(1)}, f32[32,128]{1,0:T(8,128)S(1)}, u32[]{:S(2)}, u32[]{:S(2)}) collective-permute-start(f32[32,128]{1,0:T(8,128)S(1)} %add.12), channel_id=1, source_target_pairs={{0,16},{4,20},{8,24},{12,28},{16,0},{20,4},{24,8},{28,12},{1,17},{... | collective-permute-start | bytes 49160 | tf_op jit(solution)/shard_map/gram_sum/ppermute | solution.py:455
  38.6 0.0 collective-permute-start.8
  38.6 1.0 %collective-permute-done.10 = f32[32,128]{1,0:T(8,128)S(1)} collective-permute-done((f32[32,128]{1,0:T(8,128)S(1)}, f32[32,128]{1,0:T(8,128)S(1)}, u32[]{:S(2)}, u32[]{:S(2)}) %collective-permute-start.10) | collective-permute-done | bytes 16416 | tf_op jit(solution)/shard_map/gram_sum/ppermute | solution.py:455
  39.6 1.9 %collective-permute-done.9 = f32[32,128]{1,0:T(8,128)S(1)} collective-permute-done((f32[32,128]{1,0:T(8,128)S(1)}, f32[32,128]{1,0:T(8,128)S(1)}, u32[]{:S(2)}, u32[]{:S(2)}) %collective-permute-start.9) | collective-permute-done | bytes 16416 | tf_op jit(solution)/shard_map/gram_sum/ppermute | solution.py:455
  41.6 0.8 %collective-permute-done.8 = f32[32,128]{1,0:T(8,128)S(1)} collective-permute-done((f32[32,128]{1,0:T(8,128)S(1)}, f32[32,128]{1,0:T(8,128)S(1)}, u32[]{:S(2)}, u32[]{:S(2)}) %collective-permute-start.8) | collective-permute-done | bytes 16416 | tf_op jit(solution)/shard_map/gram_sum/ppermute | solution.py:455
  42.3 2.7 %orthonormal.1 = f32[16,4116]{1,0:T(8,128)} custom-call(f32[32,128]{1,0:T(8,128)S(1)} %add_add_fusion.gram_ref, bf16[80,4352]{1,0:T(8,128)(2,1)S(1)} %get-tuple-element.50.terms_ref), custom_call_target="tpu_custom_call" | custom-call | tf_op jit(solution)/shard_map/orthonormal/pallas_call | solution.py:281
  (2 shorter events, 0.0 us)
Async XLA Ops:
  0.0 4.8 %copy-start = (bf16[12,512,512]{2,1,0:T(8,128)(2,1)S(1)}, bf16[12,512,512]{2,1,0:T(8,128)(2,1)}, u32[]{:S(2)}) copy-start(bf16[12,512,512]{2,1,0:T(8,128)(2,1)} %ham_ref.7) | copy-start | bytes 18874372
  1.4 5.6 %collective-permute-start = (bf16[16,640]{1,0:T(8,128)(2,1)S(1)}, bf16[16,640]{1,0:T(8,128)(2,1)S(1)}, u32[]{:S(2)}, u32[]{:S(2)}) collective-permute-start(bf16[16,640]{1,0:T(8,128)(2,1)S(1)} %get-tuple-element.35), channel_id=1, source_target_pairs={{4,0},{8,4},{12,8},{16,12},{20,16},{24,20},{28,24},{0,28},{5,1},{9... | collective-permute-start | bytes 61448 | tf_op jit(solution)/shard_map/ppermute | solution.py:295
  9.2 4.8 %collective-permute-start.1 = (f32[16,640]{1,0:T(8,128)S(1)}, f32[16,640]{1,0:T(8,128)S(1)}, u32[]{:S(2)}, u32[]{:S(2)}) collective-permute-start(f32[16,640]{1,0:T(8,128)S(1)} %get-tuple-element.38), channel_id=1, source_target_pairs={{0,4},{4,0},{8,12},{12,8},{16,20},{20,16},{24,28},{28,24},{1,5},{5... | collective-permute-start | bytes 122888 | tf_op jit(solution)/shard_map/ppermute | solution.py:352
  9.3 4.8 %collective-permute-start.2 = (f32[16,640]{1,0:T(8,128)S(1)}, f32[16,640]{1,0:T(8,128)S(1)}, u32[]{:S(2)}, u32[]{:S(2)}) collective-permute-start(f32[16,640]{1,0:T(8,128)S(1)} %get-tuple-element.39), channel_id=1, source_target_pairs={{0,28},{4,8},{8,4},{12,16},{16,12},{20,24},{24,20},{28,0},{1,29},{... | collective-permute-start | bytes 122888 | tf_op jit(solution)/shard_map/ppermute | solution.py:351
  15.2 4.4 %collective-permute-start.3 = (f32[16,640]{1,0:T(8,128)S(1)}, f32[16,640]{1,0:T(8,128)S(1)}, u32[]{:S(2)}, u32[]{:S(2)}) collective-permute-start(f32[16,640]{1,0:T(8,128)S(1)} %get-tuple-element.46), channel_id=1, source_target_pairs={{28,0},{0,4},{4,8},{8,12},{12,16},{16,20},{20,24},{24,28},{29,1},{... | collective-permute-start | bytes 122888 | tf_op jit(solution)/shard_map/ppermute | solution.py:295
  20.0 7.9 %collective-permute-start.6 = (bf16[16,4224]{1,0:T(8,128)(2,1)S(1)}, bf16[16,4224]{1,0:T(8,128)(2,1)S(1)}, u32[]{:S(2)}, u32[]{:S(2)}) collective-permute-start(bf16[16,4224]{1,0:T(8,128)(2,1)S(1)} %get-tuple-element.48), channel_id=1, source_target_pairs={{0,3},{1,2},{2,1},{3,0},{4,7},{5,6},{6,5},{7,4},{8,11},{9,10},{10,... | collective-permute-start | bytes 405512 | tf_op jit(solution)/shard_map/ppermute | solution.py:305
  23.7 9.5 %collective-permute-start.5 = (bf16[16,4224]{1,0:T(8,128)(2,1)S(1)}, bf16[16,4224]{1,0:T(8,128)(2,1)S(1)}, u32[]{:S(2)}, u32[]{:S(2)}) collective-permute-start(bf16[16,4224]{1,0:T(8,128)(2,1)S(1)} %get-tuple-element.48), channel_id=1, source_target_pairs={{0,2},{1,3},{2,0},{3,1},{4,6},{5,7},{6,4},{7,5},{8,10},{9,11},{10,... | collective-permute-start | bytes 405512 | tf_op jit(solution)/shard_map/ppermute | solution.py:305
  23.7 9.5 %collective-permute-start.4 = (bf16[16,4224]{1,0:T(8,128)(2,1)S(1)}, bf16[16,4224]{1,0:T(8,128)(2,1)S(1)}, u32[]{:S(2)}, u32[]{:S(2)}) collective-permute-start(bf16[16,4224]{1,0:T(8,128)(2,1)S(1)} %get-tuple-element.48), channel_id=1, source_target_pairs={{0,1},{1,0},{2,3},{3,2},{4,5},{5,4},{6,7},{7,6},{8,9},{9,8},{10,11... | collective-permute-start | bytes 405512 | tf_op jit(solution)/shard_map/ppermute | solution.py:305
  33.8 1.2 %collective-permute-start.7 = (f32[32,128]{1,0:T(8,128)S(1)}, f32[32,128]{1,0:T(8,128)S(1)}, u32[]{:S(2)}, u32[]{:S(2)}) collective-permute-start(f32[32,128]{1,0:T(8,128)S(1)} %get-tuple-element.49), channel_id=1, source_target_pairs={{0,4},{4,0},{8,12},{12,8},{16,20},{20,16},{24,28},{28,24},{1,5},{5... | collective-permute-start | bytes 49160 | tf_op jit(solution)/shard_map/gram_sum/ppermute | solution.py:455
  35.0 4.6 %collective-permute-start.10 = (f32[32,128]{1,0:T(8,128)S(1)}, f32[32,128]{1,0:T(8,128)S(1)}, u32[]{:S(2)}, u32[]{:S(2)}) collective-permute-start(f32[32,128]{1,0:T(8,128)S(1)} %add.12), channel_id=1, source_target_pairs={{0,24},{4,28},{8,16},{12,20},{16,8},{20,12},{24,0},{28,4},{1,25},{... | collective-permute-start | bytes 49160 | tf_op jit(solution)/shard_map/gram_sum/ppermute | solution.py:455
  37.8 3.7 %collective-permute-start.9 = (f32[32,128]{1,0:T(8,128)S(1)}, f32[32,128]{1,0:T(8,128)S(1)}, u32[]{:S(2)}, u32[]{:S(2)}) collective-permute-start(f32[32,128]{1,0:T(8,128)S(1)} %add.12), channel_id=1, source_target_pairs={{0,16},{4,20},{8,24},{12,28},{16,0},{20,4},{24,8},{28,12},{1,17},{... | collective-permute-start | bytes 49160 | tf_op jit(solution)/shard_map/gram_sum/ppermute | solution.py:455
  38.6 3.7 %collective-permute-start.8 = (f32[32,128]{1,0:T(8,128)S(1)}, f32[32,128]{1,0:T(8,128)S(1)}, u32[]{:S(2)}, u32[]{:S(2)}) collective-permute-start(f32[32,128]{1,0:T(8,128)S(1)} %add.12), channel_id=1, source_target_pairs={{0,8},{4,12},{8,0},{12,4},{16,24},{20,28},{24,16},{28,20},{1,9},{5... | collective-permute-start | bytes 49160 | tf_op jit(solution)/shard_map/gram_sum/ppermute | solution.py:455

commit v8 on v7

--- a/solution.py
+++ b/solution.py
@@ -62,10 +62,8 @@
     return jnp.concatenate(rows, axis=0)
 
 
-def gathered_sum(rows, low_hot):
-    both = lax.dot_general(rows, low_hot, (((1,), (1,)), ((), ())), preferred_element_type=F32)
-    count = both.shape[0] // 2
-    return both[:count] + both[count:]
+def lane_sums(rows, low_hot):
+    return lax.dot_general(rows, low_hot, (((1,), (1,)), ((), ())), preferred_element_type=F32)
 
 
 def tiles(count, width=LANES):
@@ -167,7 +165,7 @@
 
 def first_kernel(
     psi_ref, slots_ref, ghosts_ref, hots_ref, hosts_ref, ham_ref, face_ref, ghost_ref, part_ref,
-    own_ref, upper_ref, low_ref, near_ref, far_ref, inner, top, outside,
+    own_ref, upper_ref, near_ref, far_ref, inner, top, outside,
 ):
     bands, own = psi_ref.shape
     elements, size = ham_ref.shape[:2]
@@ -189,25 +187,25 @@
     own_ref[...] = current
     face = face_ref[...]
     face_hot = one_hot(face & 255)
-    terms = halves(stacked(current))
-    low = pick(terms[0], face >> 8, face_hot, bands) + pick(terms[1], face >> 8, face_hot, bands)
-    low_ref[...] = low
+    low = pick(stacked(current).astype(BF16), face >> 8, face_hot, bands)
     odd = odd_domain()
-    near_ref[...] = jnp.where(odd, low, upper)
-    far_ref[...] = jnp.where(odd, upper, low)
-
-
-def far_kernel(own_in, slots_ref, hots_ref, face_ref, inside_ref, high_ref, faces_ref):
+    near_ref[...] = jnp.where(odd, low, upper).astype(BF16)
+    far_ref[...] = jnp.where(odd, upper, low).astype(BF16)
+
+
+def far_kernel(own_in, slots_ref, hots_ref, face_ref, low_ref, inside_ref, high_ref, faces_ref):
     bands, own = own_in.shape
     blocks = round_up(own // LANES, 16)
     face = face_ref[...]
     number = lax.broadcasted_iota(jnp.int32, (blocks, face.shape[1]), 1)
     held = lax.broadcasted_iota(jnp.int32, number.shape, 0) == (face >> 8)
     digits = [jnp.where(held, digit, 0).astype(F32).astype(BF16) for digit in ((number >> 8) + 1, number & 255)]
+    face_hot = one_hot(face & 255)
     table = lax.dot_general(
-        jnp.concatenate(digits, axis=0), one_hot(face & 255), (((1,), (1,)), ((), ())), preferred_element_type=F32
+        jnp.concatenate(digits, axis=0), face_hot, (((1,), (1,)), ((), ())), preferred_element_type=F32
     ).astype(BF16)
-    rows = stacked(own_in[...]).astype(BF16)
+    rows, rest = halves(stacked(own_in[...]))
+    low_ref[...] = pick(rows, face >> 8, face_hot, bands) + pick(rest, face >> 8, face_hot, bands)
     for tile in tiles(slots_ref.shape[1]):
         high = slots_ref[:, tile] >> 8
         hot = hots_ref[:, tile]
@@ -227,8 +225,9 @@
     bands, face_count = upper_in.shape
     elements, size = ham_ref.shape[:2]
     odd = odd_domain()
-    below = jnp.where(odd, near_in[...], far_in[...])
-    above = jnp.where(odd, far_in[...], near_in[...])
+    near, far = near_in[...].astype(F32), far_in[...].astype(F32)
+    below = jnp.where(odd, near, far)
+    above = jnp.where(odd, far, near)
     faces = stacked(widened(low_in[...] + below)).astype(BF16)
     ghost = stacked(widened(upper_in[...] + above)).astype(BF16)
     ghosts = ghosts_ref[...]
@@ -247,7 +246,7 @@
             products.append(product[:, 128 - FACE_EL :])
         top[:, pair[0] * FACE_EL : (pair[-1] + 1) * FACE_EL] = jnp.concatenate(products, axis=1)
     total = unstacked(scatter_sum(top, ghosts >> 8, hosts_ref, round_up(face_count, LANES) // LANES), bands)
-    upper_ref[...] = total[:, :face_count] * (2.0 / HALF_WIDTH)
+    upper_ref[...] = (total[:, :face_count] * (2.0 / HALF_WIDTH)).astype(BF16)
 
 
 def third_kernel(
@@ -256,8 +255,8 @@
     bands, own = own_in.shape
     elements, size = ham_ref.shape[:2]
     face = face_ref[...]
-    below = jnp.where(odd_domain(), near_in[...], far_in[...])
-    added = gathered_sum(spread(below, face >> 8, own // LANES), one_hot(face & 255))
+    below = jnp.where(odd_domain(), near_in[...].astype(F32), far_in[...].astype(F32))
+    added = lane_sums(spread_once(below, face >> 8, own // LANES), one_hot(face & 255))
     for pair in pairs(elements):
         products = [
             jnp.dot(field_ref[:, e * size : (e + 1) * size], ham_ref[e], preferred_element_type=F32) for e in pair
@@ -271,7 +270,7 @@
 def last_kernel(own_in, face_ref, below_in, out_ref, short_ref):
     bands, own = own_in.shape
     face = face_ref[...]
-    added = gathered_sum(spread(below_in[...], face >> 8, own // LANES), one_hot(face & 255))
+    added = lane_sums(spread_once(below_in[...].astype(F32), face >> 8, own // LANES), one_hot(face & 255))
     total = own_in[...] + unstacked(added, bands)
     out_ref[...] = total
     short_ref[...] = total[:, : short_ref.shape[1]].astype(BF16)
@@ -342,8 +341,8 @@
             (wide, conn, ham), (inside_field,), flops=4 * 10**9, moved=8 * 10**6,
         )
     with jax.named_scope("first_step"):
-        current, upper, low, to_near, to_far = call(
-            first_kernel, (own_field, *[face_field] * 4),
+        current, upper, to_near, to_far = call(
+            first_kernel, (own_field, face_field, *[shape(face_field.shape, BF16)] * 2),
             (wide, slots, ghosts, hots, hosts, ham, face, ghost, part), (inner, top, outside),
             flops=4 * 10**9, moved=10**6,
         )
@@ -351,14 +350,14 @@
     from_far = lax.ppermute(to_far, "space", [(i, ((i + 1 ^ 1) - 1) % domains) for i in range(domains)])
     from_near = lax.ppermute(to_near, "space", [(i, i ^ 1) for i in range(domains)])
     with jax.named_scope("off_face"):
-        inside, high, faces = call(
+        low, inside, high, faces = call(
             far_kernel,
-            (shape((bands, inner_count), BF16), shape((1, inner_count), jnp.int32), shape((LANES, inner_count), BF16)),
+            (face_field, shape((bands, inner_count), BF16), shape((1, inner_count), jnp.int32), shape((LANES, inner_count), BF16)),
             (current, slots, hots, face), flops=4 * 10**9, moved=10**6,
         )
     with jax.named_scope("second_step"):
         field, upper = call(
-            second_kernel, (shape((bands, elements * size), BF16), face_field),
+            second_kernel, (shape((bands, elements * size), BF16), shape(face_field.shape, BF16)),
             (inside, high, faces, ghosts, hosts, ham, low, upper, from_near, from_far), (inside_field, top, outside),
             flops=4 * 10**9, moved=10**6,
         )
@@ -398,30 +397,30 @@
     gram_ref[...] = jnp.concatenate([gram[: total // 2], gram[total // 2 :]], axis=1)
 
 
-def inverse_factor(matrix, block=8):
+def inverse_factor(matrix, block=16):
     size = matrix.shape[0]
     width = 2 * size
     lane = lax.broadcasted_iota(jnp.int32, (8, width), 1)
     row = lax.broadcasted_iota(jnp.int32, (8, width), 0)
-    zero = jnp.zeros((size, size), F32)
-    wide = jnp.concatenate([matrix, zero], axis=1)
+    wide = jnp.concatenate([matrix, jnp.zeros((size, size), F32)], axis=1)
     groups = [wide[8 * g : 8 * g + 8] + jnp.where(lane == row + (size + 8 * g), 1.0, 0.0) for g in range(size // 8)]
     for k in range(0, size, block):
-        start = k // 8
         columns = [
-            [jnp.broadcast_to(groups[g][:, k + q : k + q + 1], (8, width)) for g in range(start, size // 8)]
-            for q in range(block)
+            {g: jnp.broadcast_to(groups[g][:, j : j + 1], (8, width)) for g in range(k // 8, size // 8)}
+            for j in range(k, k + block)
         ]
         for q in range(block):
-            at = k + q - 8 * start
-            scale = 1.0 / columns[q][0][at : at + 1]
-            column = [jnp.where(row > at, columns[q][0], 0.0)] + columns[q][1:]
+            first, at = divmod(k + q, 8)
+            scale = 1.0 / columns[q][first][at : at + 1]
+            column = {g: rows for g, rows in columns[q].items() if g >= first}
+            column[first] = jnp.where(row > at, column[first], 0.0)
             for p in range(q + 1, block):
-                factor = columns[p][0][at : at + 1] * scale
-                columns[p] = [value - weight * factor for value, weight in zip(columns[p], column)]
-            factor = groups[start][at : at + 1] * scale
-            for g, weight in enumerate(column):
-                groups[start + g] = groups[start + g] - weight * factor
+                factor = columns[p][first][at : at + 1] * scale
+                for g, weight in column.items():
+                    columns[p][g] = columns[p][g] - weight * factor
+            factor = groups[first][at : at + 1] * scale
+            for g, weight in column.items():
+                groups[g] = groups[g] - weight * factor
     out = []
     for g, rows in enumerate(groups):
         pivot = jnp.sum(jnp.where(lane == row + 8 * g, rows, 0.0), axis=1, keepdims=True)

time: 45.2 us -> 44.2 us (0.978)
  Pallas kernels: 15.4 us -> 14.6 us
    pallas_call x9, Pallas kernels: 15.4 us -> 14.6 us  [call(): pl.pallas_call(kernel, out_shape=out_shape, in_specs=[HBM if i in far els...]
where the time goes in v8:
time: 44.2 us; the launch traced here: 44.1 us
  waiting for transfers between devices  15.8 us (36%)
  Pallas kernels  14.6 us (33%)
  starting transfers between devices  13.6 us (31%)
    pallas_call x9, Pallas kernels, call(): pl.pallas_call(kernel, out_shape=out_shape, in_specs=[HBM if i in far els...  14.6 us
    ppermute x3, waiting for transfers between devices, partner(): return lax.ppermute(block, axis, [(i, i ^ distance) for i in range(size)])  8.9 us
    ppermute x4, waiting for transfers between devices, space_sum(): lax.ppermute(block, 'space', [(i, i ^ step * k) for i in range(size)])  4.83 us
    ppermute x3, starting transfers between devices, partner(): return lax.ppermute(block, axis, [(i, i ^ distance) for i in range(size)])  4.45 us
    ppermute x4, starting transfers between devices, space_sum(): lax.ppermute(block, 'space', [(i, i ^ step * k) for i in range(size)])  3.51 us
    ppermute x2, starting transfers between devices, from_behind(): return lax.ppermute(block, axis, route)  3.44 us
    ppermute x1, starting transfers between devices, filter_field(): lax.ppermute(to_far, 'space', [(i, ((i + 1 ^ 1) - 1) % domains) for i in...  2.07 us
    ppermute x2, waiting for transfers between devices, from_behind(): return lax.ppermute(block, axis, route)  2.07 us
  transfers between devices with their start and end apart: 11, of which 7 were waited for; matrix products, arithmetic and copies ran while one was open for 0% of the time, Pallas kernels for 15%

profile of v8, /device:TPU:0, one launch (start us, length us, event | category | flops | bytes accessed | tf_op | source)
XLA Modules:
  0.0 44.1 jit_solution(18023388806647029721)
XLA Ops:
  0.0 0.0 copy-start
  0.0 1.4 %face_values.1 = (bf16[16,640]{1,0:T(8,128)(2,1)S(1)}, f32[16,4352]{1,0:T(8,128)S(1)}, s32[12,512]{1,0:T(8,128)S(1)}, s32[1,640]{1,0:T(1,128)S(1)}) custom-call(f32[16,4116]{1,0:T(8,128)} %psi_hbm.1, s32[12,512]{1,0:T(8,128)} %conn_hbm.1, s32[588]{0:T(1024)} %face_hbm.1), custom_call_target="tpu_custom_call" | custom-call | flops 20000000000 | bytes 40000000 | tf_op jit(solution)/shard_map/face_values/pallas_call | solution.py:280
  1.4 3.4 %collective-permute-start = (bf16[16,640]{1,0:T(8,128)(2,1)S(1)}, bf16[16,640]{1,0:T(8,128)(2,1)S(1)}, u32[]{:S(2)}, u32[]{:S(2)}) collective-permute-start(bf16[16,640]{1,0:T(8,128)(2,1)S(1)} %get-tuple-element.35), channel_id=1, source_target_pairs={{4,0},{8,4},{12,8},{16,12},{20,16},{24,20},{28,24},{0,28},{5,1},{9... | collective-permute-start | bytes 61448 | tf_op jit(solution)/shard_map/ppermute | solution.py:294
  4.8 0.0 copy-done
  4.8 2.2 %interior.1 = (f32[16,6144]{1,0:T(8,128)S(1)}, s32[1,5376]{1,0:T(1,128)S(1)}, s32[1,768]{1,0:T(1,128)S(1)}, bf16[256,5376]{1,0:T(8,128)(2,1)S(1)}, bf16[256,768]{1,0:T(8,128)(2,1)S(1)}) custom-call(f32[16,4352]{1,0:T(8,128)S(1)} %get-tuple-element.28.psi_ref, s32[12,512]{1,0:T(8,128)S(1)} %get-tuple-element.29.conn_ref, bf16[12,512,512]{2,1,0:T(8,128)(2,1)S(1)} %copy-done), custom_call_target="tpu_custom_call" | custom-call | flops 4000000000 | bytes 8000000 | tf_op jit(solution)/shard_map/interior/pallas_call | solution.py:280
  7.0 0.0 collective-permute-done.ghost_ref
  7.0 1.8 %first_step.1 = (f32[16,4352]{1,0:T(8,128)S(1)}, f32[16,640]{1,0:T(8,128)S(1)}, bf16[16,640]{1,0:T(8,128)(2,1)S(1)}, bf16[16,640]{1,0:T(8,128)(2,1)S(1)}) custom-call(f32[16,4352]{1,0:T(8,128)S(1)} %get-tuple-element.28.psi_ref, s32[1,5376]{1,0:T(1,128)S(1)} %get-tuple-element.30.slots_ref, s32[1,768]{1,0:T(1,128)S(1)} %get-tuple-element.33.ghosts_ref, ...), custom_call_target="tpu_custom_call" | custom-call | flops 4000000000 | bytes 1000000 | tf_op jit(solution)/shard_map/first_step/pallas_call | solution.py:280
  8.8 0.1 collective-permute-start.1
  8.9 2.1 %collective-permute-start.2 = (bf16[16,640]{1,0:T(8,128)(2,1)S(1)}, bf16[16,640]{1,0:T(8,128)(2,1)S(1)}, u32[]{:S(2)}, u32[]{:S(2)}) collective-permute-start(bf16[16,640]{1,0:T(8,128)(2,1)S(1)} %get-tuple-element.39), channel_id=1, source_target_pairs={{0,28},{4,8},{8,4},{12,16},{16,12},{20,24},{24,20},{28,0},{1,29},{... | collective-permute-start | bytes 61448 | tf_op jit(solution)/shard_map/ppermute | solution.py:350
  11.0 2.5 %off_face.1 = (f32[16,640]{1,0:T(8,128)S(1)}, bf16[16,5376]{1,0:T(8,128)(2,1)S(1)}, s32[1,5376]{1,0:T(1,128)S(1)}, bf16[256,5376]{1,0:T(8,128)(2,1)S(1)}) custom-call(f32[16,4352]{1,0:T(8,128)S(1)} %get-tuple-element.37.own_in, s32[1,5376]{1,0:T(1,128)S(1)} %get-tuple-element.30.slots_ref, bf16[256,5376]{1,0:T(8,128)(2,1)S(1)} %get-tuple-element.31.hots_ref, ...), custom_call_target="tpu_custom_call" | custom-call | flops 4000000000 | bytes 1000000 | tf_op jit(solution)/shard_map/off_face/pallas_call | solution.py:280
  13.5 0.0 collective-permute-done.1.near_in
  13.5 0.0 collective-permute-done.2.far_in
  13.5 1.1 %second_step.1 = (bf16[16,6144]{1,0:T(8,128)(2,1)S(1)}, bf16[16,640]{1,0:T(8,128)(2,1)S(1)}) custom-call(bf16[16,5376]{1,0:T(8,128)(2,1)S(1)} %get-tuple-element.40.inside_ref, s32[1,5376]{1,0:T(1,128)S(1)} %get-tuple-element.41.high_ref, bf16[256,5376]{1,0:T(8,128)(2,1)S(1)} %get-tuple-element.42.faces_ref, s32[1,768]{1,0:T(1,128)S(1)} %get-tuple-element.33.ghosts_ref, ...), custom_call_target="tpu_custom_call" | custom-call | flops 4000000000 | bytes 1000000 | tf_op jit(solution)/shard_map/second_step/pallas_call | solution.py:280
  14.7 0.1 collective-permute-start.3
  14.7 2.0 %second_sums.1.own_in = f32[16,4352]{1,0:T(8,128)S(1)} custom-call(f32[16,4352]{1,0:T(8,128)S(1)} %get-tuple-element.28.psi_ref, s32[1,5376]{1,0:T(1,128)S(1)} %get-tuple-element.30.slots_ref, bf16[256,5376]{1,0:T(8,128)(2,1)S(1)} %get-tuple-element.31.hots_ref, bf16[12,512,512]{2,1,0:T(8,128)(2,1)S(1)} %copy-done, s32[1,640]{1,0:T(1,128)S(1)} %get-tuple-element.32.face_ref, ...), custom_call_target="tpu_custom_call" | custom-call | flops 4000000000 | bytes 8000000 | tf_op jit(solution)/shard_map/second_sums/pallas_call | solution.py:280
  16.7 2.1 %collective-permute-done.3.below_in = bf16[16,640]{1,0:T(8,128)(2,1)S(1)} collective-permute-done((bf16[16,640]{1,0:T(8,128)(2,1)S(1)}, bf16[16,640]{1,0:T(8,128)(2,1)S(1)}, u32[]{:S(2)}, u32[]{:S(2)}) %collective-permute-start.3) | collective-permute-done | bytes 20512 | tf_op jit(solution)/shard_map/ppermute | solution.py:294
  18.8 0.4 last_faces.1
  19.2 3.7 %collective-permute-start.6 = (bf16[16,4224]{1,0:T(8,128)(2,1)S(1)}, bf16[16,4224]{1,0:T(8,128)(2,1)S(1)}, u32[]{:S(2)}, u32[]{:S(2)}) collective-permute-start(bf16[16,4224]{1,0:T(8,128)(2,1)S(1)} %get-tuple-element.48), channel_id=1, source_target_pairs={{0,3},{1,2},{2,1},{3,0},{4,7},{5,6},{6,5},{7,4},{8,11},{9,10},{10,... | collective-permute-start | bytes 405512 | tf_op jit(solution)/shard_map/ppermute | solution.py:304
  22.8 0.0 collective-permute-start.5
  22.8 0.8 %collective-permute-start.4 = (bf16[16,4224]{1,0:T(8,128)(2,1)S(1)}, bf16[16,4224]{1,0:T(8,128)(2,1)S(1)}, u32[]{:S(2)}, u32[]{:S(2)}) collective-permute-start(bf16[16,4224]{1,0:T(8,128)(2,1)S(1)} %get-tuple-element.48), channel_id=1, source_target_pairs={{0,1},{1,0},{2,3},{3,2},{4,5},{5,4},{6,7},{7,6},{8,9},{9,8},{10,11... | collective-permute-start | bytes 405512 | tf_op jit(solution)/shard_map/ppermute | solution.py:304
  23.6 3.4 %collective-permute-done.6.refs_3_ = bf16[16,4224]{1,0:T(8,128)(2,1)S(1)} collective-permute-done((bf16[16,4224]{1,0:T(8,128)(2,1)S(1)}, bf16[16,4224]{1,0:T(8,128)(2,1)S(1)}, u32[]{:S(2)}, u32[]{:S(2)}) %collective-permute-start.6) | collective-permute-done | bytes 135200 | tf_op jit(solution)/shard_map/ppermute | solution.py:304
  27.1 5.5 %collective-permute-done.5.refs_2_ = bf16[16,4224]{1,0:T(8,128)(2,1)S(1)} collective-permute-done((bf16[16,4224]{1,0:T(8,128)(2,1)S(1)}, bf16[16,4224]{1,0:T(8,128)(2,1)S(1)}, u32[]{:S(2)}, u32[]{:S(2)}) %collective-permute-start.5) | collective-permute-done | bytes 135200 | tf_op jit(solution)/shard_map/ppermute | solution.py:304
  32.5 0.0 collective-permute-done.4.refs_1_
  32.5 0.6 %gram.1 = (bf16[80,4352]{1,0:T(8,128)(2,1)S(1)}, f32[32,128]{1,0:T(8,128)S(1)}) custom-call(f32[16,4352]{1,0:T(8,128)S(1)} %get-tuple-element.47.refs_0_, bf16[16,4224]{1,0:T(8,128)(2,1)S(1)} %collective-permute-done.4.refs_1_, bf16[16,4224]{1,0:T(8,128)(2,1)S(1)} %collective-permute-done.5.refs_2_, bf16[16,4224]{1,0:T(8,128)(2,1)S(1)} %collective-permute-done.6.refs_3_), custom_call_target="tpu_custom_call" | custom-call | tf_op jit(solution)/shard_map/gram/pallas_call | solution.py:280
  33.1 0.0 collective-permute-start.7
  33.2 1.2 %collective-permute-done.7 = f32[32,128]{1,0:T(8,128)S(1)} collective-permute-done((f32[32,128]{1,0:T(8,128)S(1)}, f32[32,128]{1,0:T(8,128)S(1)}, u32[]{:S(2)}, u32[]{:S(2)}) %collective-permute-start.7) | collective-permute-done | bytes 16416 | tf_op jit(solution)/shard_map/gram_sum/ppermute | solution.py:454
  34.3 2.7 %collective-permute-start.10 = (f32[32,128]{1,0:T(8,128)S(1)}, f32[32,128]{1,0:T(8,128)S(1)}, u32[]{:S(2)}, u32[]{:S(2)}) collective-permute-start(f32[32,128]{1,0:T(8,128)S(1)} %add.12), channel_id=1, source_target_pairs={{0,24},{4,28},{8,16},{12,20},{16,8},{20,12},{24,0},{28,4},{1,25},{... | collective-permute-start | bytes 49160 | tf_op jit(solution)/shard_map/gram_sum/ppermute | solution.py:454
  37.1 0.7 %collective-permute-start.9 = (f32[32,128]{1,0:T(8,128)S(1)}, f32[32,128]{1,0:T(8,128)S(1)}, u32[]{:S(2)}, u32[]{:S(2)}) collective-permute-start(f32[32,128]{1,0:T(8,128)S(1)} %add.12), channel_id=1, source_target_pairs={{0,16},{4,20},{8,24},{12,28},{16,0},{20,4},{24,8},{28,12},{1,17},{... | collective-permute-start | bytes 49160 | tf_op jit(solution)/shard_map/gram_sum/ppermute | solution.py:454
  37.7 0.1 collective-permute-start.8
  37.8 1.1 %collective-permute-done.10 = f32[32,128]{1,0:T(8,128)S(1)} collective-permute-done((f32[32,128]{1,0:T(8,128)S(1)}, f32[32,128]{1,0:T(8,128)S(1)}, u32[]{:S(2)}, u32[]{:S(2)}) %collective-permute-start.10) | collective-permute-done | bytes 16416 | tf_op jit(solution)/shard_map/gram_sum/ppermute | solution.py:454
  39.0 1.8 %collective-permute-done.9 = f32[32,128]{1,0:T(8,128)S(1)} collective-permute-done((f32[32,128]{1,0:T(8,128)S(1)}, f32[32,128]{1,0:T(8,128)S(1)}, u32[]{:S(2)}, u32[]{:S(2)}) %collective-permute-start.9) | collective-permute-done | bytes 16416 | tf_op jit(solution)/shard_map/gram_sum/ppermute | solution.py:454
  40.8 0.7 %collective-permute-done.8 = f32[32,128]{1,0:T(8,128)S(1)} collective-permute-done((f32[32,128]{1,0:T(8,128)S(1)}, f32[32,128]{1,0:T(8,128)S(1)}, u32[]{:S(2)}, u32[]{:S(2)}) %collective-permute-start.8) | collective-permute-done | bytes 16416 | tf_op jit(solution)/shard_map/gram_sum/ppermute | solution.py:454
  41.5 2.6 %orthonormal.1 = f32[16,4116]{1,0:T(8,128)} custom-call(f32[32,128]{1,0:T(8,128)S(1)} %add_add_fusion.gram_ref, bf16[80,4352]{1,0:T(8,128)(2,1)S(1)} %get-tuple-element.50.terms_ref), custom_call_target="tpu_custom_call" | custom-call | tf_op jit(solution)/shard_map/orthonormal/pallas_call | solution.py:280
  (2 shorter events, 0.0 us)
Async XLA Ops:
  0.0 4.8 %copy-start = (bf16[12,512,512]{2,1,0:T(8,128)(2,1)S(1)}, bf16[12,512,512]{2,1,0:T(8,128)(2,1)}, u32[]{:S(2)}) copy-start(bf16[12,512,512]{2,1,0:T(8,128)(2,1)} %ham_ref.7) | copy-start | bytes 18874372
  1.4 5.6 %collective-permute-start = (bf16[16,640]{1,0:T(8,128)(2,1)S(1)}, bf16[16,640]{1,0:T(8,128)(2,1)S(1)}, u32[]{:S(2)}, u32[]{:S(2)}) collective-permute-start(bf16[16,640]{1,0:T(8,128)(2,1)S(1)} %get-tuple-element.35), channel_id=1, source_target_pairs={{4,0},{8,4},{12,8},{16,12},{20,16},{24,20},{28,24},{0,28},{5,1},{9... | collective-permute-start | bytes 61448 | tf_op jit(solution)/shard_map/ppermute | solution.py:294
  8.8 4.7 %collective-permute-start.1 = (bf16[16,640]{1,0:T(8,128)(2,1)S(1)}, bf16[16,640]{1,0:T(8,128)(2,1)S(1)}, u32[]{:S(2)}, u32[]{:S(2)}) collective-permute-start(bf16[16,640]{1,0:T(8,128)(2,1)S(1)} %get-tuple-element.38), channel_id=1, source_target_pairs={{0,4},{4,0},{8,12},{12,8},{16,20},{20,16},{24,28},{28,24},{1,5},{5... | collective-permute-start | bytes 61448 | tf_op jit(solution)/shard_map/ppermute | solution.py:351
  8.9 4.6 %collective-permute-start.2 = (bf16[16,640]{1,0:T(8,128)(2,1)S(1)}, bf16[16,640]{1,0:T(8,128)(2,1)S(1)}, u32[]{:S(2)}, u32[]{:S(2)}) collective-permute-start(bf16[16,640]{1,0:T(8,128)(2,1)S(1)} %get-tuple-element.39), channel_id=1, source_target_pairs={{0,28},{4,8},{8,4},{12,16},{16,12},{20,24},{24,20},{28,0},{1,29},{... | collective-permute-start | bytes 61448 | tf_op jit(solution)/shard_map/ppermute | solution.py:350
  14.7 4.2 %collective-permute-start.3 = (bf16[16,640]{1,0:T(8,128)(2,1)S(1)}, bf16[16,640]{1,0:T(8,128)(2,1)S(1)}, u32[]{:S(2)}, u32[]{:S(2)}) collective-permute-start(bf16[16,640]{1,0:T(8,128)(2,1)S(1)} %get-tuple-element.46), channel_id=1, source_target_pairs={{28,0},{0,4},{4,8},{8,12},{12,16},{16,20},{20,24},{24,28},{29,1},{... | collective-permute-start | bytes 61448 | tf_op jit(solution)/shard_map/ppermute | solution.py:294
  19.2 7.9 %collective-permute-start.6 = (bf16[16,4224]{1,0:T(8,128)(2,1)S(1)}, bf16[16,4224]{1,0:T(8,128)(2,1)S(1)}, u32[]{:S(2)}, u32[]{:S(2)}) collective-permute-start(bf16[16,4224]{1,0:T(8,128)(2,1)S(1)} %get-tuple-element.48), channel_id=1, source_target_pairs={{0,3},{1,2},{2,1},{3,0},{4,7},{5,6},{6,5},{7,4},{8,11},{9,10},{10,... | collective-permute-start | bytes 405512 | tf_op jit(solution)/shard_map/ppermute | solution.py:304
  22.8 9.7 %collective-permute-start.5 = (bf16[16,4224]{1,0:T(8,128)(2,1)S(1)}, bf16[16,4224]{1,0:T(8,128)(2,1)S(1)}, u32[]{:S(2)}, u32[]{:S(2)}) collective-permute-start(bf16[16,4224]{1,0:T(8,128)(2,1)S(1)} %get-tuple-element.48), channel_id=1, source_target_pairs={{0,2},{1,3},{2,0},{3,1},{4,6},{5,7},{6,4},{7,5},{8,10},{9,11},{10,... | collective-permute-start | bytes 405512 | tf_op jit(solution)/shard_map/ppermute | solution.py:304
  22.8 9.7 %collective-permute-start.4 = (bf16[16,4224]{1,0:T(8,128)(2,1)S(1)}, bf16[16,4224]{1,0:T(8,128)(2,1)S(1)}, u32[]{:S(2)}, u32[]{:S(2)}) collective-permute-start(bf16[16,4224]{1,0:T(8,128)(2,1)S(1)} %get-tuple-element.48), channel_id=1, source_target_pairs={{0,1},{1,0},{2,3},{3,2},{4,5},{5,4},{6,7},{7,6},{8,9},{9,8},{10,11... | collective-permute-start | bytes 405512 | tf_op jit(solution)/shard_map/ppermute | solution.py:304
  33.1 1.2 %collective-permute-start.7 = (f32[32,128]{1,0:T(8,128)S(1)}, f32[32,128]{1,0:T(8,128)S(1)}, u32[]{:S(2)}, u32[]{:S(2)}) collective-permute-start(f32[32,128]{1,0:T(8,128)S(1)} %get-tuple-element.49), channel_id=1, source_target_pairs={{0,4},{4,0},{8,12},{12,8},{16,20},{20,16},{24,28},{28,24},{1,5},{5... | collective-permute-start | bytes 49160 | tf_op jit(solution)/shard_map/gram_sum/ppermute | solution.py:454
  34.3 4.6 %collective-permute-start.10 = (f32[32,128]{1,0:T(8,128)S(1)}, f32[32,128]{1,0:T(8,128)S(1)}, u32[]{:S(2)}, u32[]{:S(2)}) collective-permute-start(f32[32,128]{1,0:T(8,128)S(1)} %add.12), channel_id=1, source_target_pairs={{0,24},{4,28},{8,16},{12,20},{16,8},{20,12},{24,0},{28,4},{1,25},{... | collective-permute-start | bytes 49160 | tf_op jit(solution)/shard_map/gram_sum/ppermute | solution.py:454
  37.1 3.7 %collective-permute-start.9 = (f32[32,128]{1,0:T(8,128)S(1)}, f32[32,128]{1,0:T(8,128)S(1)}, u32[]{:S(2)}, u32[]{:S(2)}) collective-permute-start(f32[32,128]{1,0:T(8,128)S(1)} %add.12), channel_id=1, source_target_pairs={{0,16},{4,20},{8,24},{12,28},{16,0},{20,4},{24,8},{28,12},{1,17},{... | collective-permute-start | bytes 49160 | tf_op jit(solution)/shard_map/gram_sum/ppermute | solution.py:454
  37.7 3.7 %collective-permute-start.8 = (f32[32,128]{1,0:T(8,128)S(1)}, f32[32,128]{1,0:T(8,128)S(1)}, u32[]{:S(2)}, u32[]{:S(2)}) collective-permute-start(f32[32,128]{1,0:T(8,128)S(1)} %add.12), channel_id=1, source_target_pairs={{0,8},{4,12},{8,0},{12,4},{16,24},{20,28},{24,16},{28,20},{1,9},{5... | collective-permute-start | bytes 49160 | tf_op jit(solution)/shard_map/gram_sum/ppermute | solution.py:454

commit v9 on v8

--- a/solution.py
+++ b/solution.py
@@ -136,9 +136,7 @@
     copies[2].wait()
 
 
-def interior_kernel(
-    nodes, psi_ref, conn_ref, ham_ref, part_ref, slots_ref, ghosts_ref, hots_ref, hosts_ref, inside_ref
-):
+def near_kernel(nodes, psi_ref, conn_ref, inside_ref, slots_ref, ghosts_ref, hots_ref, hosts_ref):
     elements, size = conn_ref.shape
     slots_ref[...] = packed(conn_ref, elements, 0, IN_EL)
     ghosts_ref[...] = packed(conn_ref, elements, IN_EL, size) - nodes
@@ -146,6 +144,10 @@
     slots = slots_ref[...]
     hot_into(hots_ref, slots & 255)
     pick_into(inside_ref, stacked(psi_ref[...]).astype(BF16), slots >> 8, hots_ref)
+
+
+def interior_kernel(inside_ref, ham_ref, part_ref):
+    elements, size = ham_ref.shape[:2]
     for e in range(elements):
         part_ref[:, e * size : (e + 1) * size] = jnp.dot(
             inside_ref[:, e * IN_EL : (e + 1) * IN_EL], ham_ref[e, :IN_EL, :], preferred_element_type=F32
@@ -330,15 +332,18 @@
             far=(0, 1, 2), flops=2 * 10**10, moved=4 * 10**7,
         )
     ghost = from_behind(values, "space", -1)
-    with jax.named_scope("interior"):
-        part, slots, ghosts, hots, hosts = call(
-            functools.partial(interior_kernel, nodes),
+    with jax.named_scope("near_values"):
+        inside, slots, ghosts, hots, hosts = call(
+            functools.partial(near_kernel, nodes),
             (
-                shape((bands, elements * size), F32),
-                shape((1, inner_count), jnp.int32), shape((1, face_count), jnp.int32),
+                shape((bands, inner_count), BF16), shape((1, inner_count), jnp.int32), shape((1, face_count), jnp.int32),
                 shape((LANES, inner_count), BF16), shape((LANES, face_count), BF16),
             ),
-            (wide, conn, ham), (inside_field,), flops=4 * 10**9, moved=8 * 10**6,
+            (wide, conn),
+        )
+    with jax.named_scope("interior"):
+        part = call(
+            interior_kernel, shape((bands, elements * size), F32), (inside, ham), flops=4 * 10**9, moved=8 * 10**6
         )
     with jax.named_scope("first_step"):
         current, upper, to_near, to_far = call(

time: 44.2 us -> 44 us (level)
    pallas_call x9 -> x10, Pallas kernels: 14.6 us -> 14.8 us  [call(): pl.pallas_call(kernel, out_shape=out_shape, in_specs=[HBM if i in far els...]
  transfers between devices with their start and end apart: 11 -> 11, of which waited for: 7 -> 7; matrix products, arithmetic and copies ran while one was open for 0% -> 0% of each run, Pallas kernels for 15% -> 16%
where the time goes in v9:
time: 44 us; the launch traced here: 43.9 us
  waiting for transfers between devices  15.8 us (36%)
  Pallas kernels  14.8 us (34%)
  starting transfers between devices  13.2 us (30%)
    pallas_call x10, Pallas kernels, call(): pl.pallas_call(kernel, out_shape=out_shape, in_specs=[HBM if i in far els...  14.8 us
    ppermute x3, waiting for transfers between devices, partner(): return lax.ppermute(block, axis, [(i, i ^ distance) for i in range(size)])  9.28 us
    ppermute x3, starting transfers between devices, partner(): return lax.ppermute(block, axis, [(i, i ^ distance) for i in range(size)])  4.45 us
    ppermute x4, waiting for transfers between devices, space_sum(): lax.ppermute(block, 'space', [(i, i ^ step * k) for i in range(size)])  4.44 us
    ppermute x4, starting transfers between devices, space_sum(): lax.ppermute(block, 'space', [(i, i ^ step * k) for i in range(size)])  3.51 us
    ppermute x2, starting transfers between devices, from_behind(): return lax.ppermute(block, axis, route)  3.44 us
    ppermute x2, waiting for transfers between devices, from_behind(): return lax.ppermute(block, axis, route)  2.07 us
    ppermute x1, starting transfers between devices, filter_field(): lax.ppermute(to_far, 'space', [(i, ((i + 1 ^ 1) - 1) % domains) for i in...  1.71 us
  transfers between devices with their start and end apart: 11, of which 7 were waited for; matrix products, arithmetic and copies ran while one was open for 0% of the time, Pallas kernels for 16%

profile of v9, /device:TPU:0, one launch (start us, length us, event | category | flops | bytes accessed | tf_op | source)
XLA Modules:
  0.0 43.9 jit_solution(12380101283819711688)
XLA Ops:
  0.0 0.0 copy-start
  0.0 1.4 %face_values.1 = (bf16[16,640]{1,0:T(8,128)(2,1)S(1)}, f32[16,4352]{1,0:T(8,128)S(1)}, s32[12,512]{1,0:T(8,128)S(1)}, s32[1,640]{1,0:T(1,128)S(1)}) custom-call(f32[16,4116]{1,0:T(8,128)} %psi_hbm.1, s32[12,512]{1,0:T(8,128)} %conn_hbm.1, s32[588]{0:T(1024)} %face_hbm.1), custom_call_target="tpu_custom_call" | custom-call | flops 20000000000 | bytes 40000000 | tf_op jit(solution)/shard_map/face_values/pallas_call | solution.py:282
  1.4 3.4 %collective-permute-start = (bf16[16,640]{1,0:T(8,128)(2,1)S(1)}, bf16[16,640]{1,0:T(8,128)(2,1)S(1)}, u32[]{:S(2)}, u32[]{:S(2)}) collective-permute-start(bf16[16,640]{1,0:T(8,128)(2,1)S(1)} %get-tuple-element.35), channel_id=1, source_target_pairs={{4,0},{8,4},{12,8},{16,12},{20,16},{24,20},{28,24},{0,28},{5,1},{9... | collective-permute-start | bytes 61448 | tf_op jit(solution)/shard_map/ppermute | solution.py:296
  4.8 1.6 %near_values.1 = (bf16[16,5376]{1,0:T(8,128)(2,1)S(1)}, s32[1,5376]{1,0:T(1,128)S(1)}, s32[1,768]{1,0:T(1,128)S(1)}, bf16[256,5376]{1,0:T(8,128)(2,1)S(1)}, bf16[256,768]{1,0:T(8,128)(2,1)S(1)}) custom-call(f32[16,4352]{1,0:T(8,128)S(1)} %get-tuple-element.28.psi_ref, s32[12,512]{1,0:T(8,128)S(1)} %get-tuple-element.29.conn_ref), custom_call_target="tpu_custom_call" | custom-call | tf_op jit(solution)/shard_map/near_values/pallas_call | solution.py:282
  6.4 0.0 copy-done
  6.4 0.8 %interior.1.part_ref = f32[16,6144]{1,0:T(8,128)S(1)} custom-call(bf16[16,5376]{1,0:T(8,128)(2,1)S(1)} %get-tuple-element.36.inside_ref, bf16[12,512,512]{2,1,0:T(8,128)(2,1)S(1)} %copy-done), custom_call_target="tpu_custom_call" | custom-call | flops 4000000000 | bytes 8000000 | tf_op jit(solution)/shard_map/interior/pallas_call | solution.py:282
  7.3 0.0 collective-permute-done.ghost_ref
  7.3 1.8 %first_step.1 = (f32[16,4352]{1,0:T(8,128)S(1)}, f32[16,640]{1,0:T(8,128)S(1)}, bf16[16,640]{1,0:T(8,128)(2,1)S(1)}, bf16[16,640]{1,0:T(8,128)(2,1)S(1)}) custom-call(f32[16,4352]{1,0:T(8,128)S(1)} %get-tuple-element.28.psi_ref, s32[1,5376]{1,0:T(1,128)S(1)} %get-tuple-element.30.slots_ref, s32[1,768]{1,0:T(1,128)S(1)} %get-tuple-element.33.ghosts_ref, ...), custom_call_target="tpu_custom_call" | custom-call | flops 4000000000 | bytes 1000000 | tf_op jit(solution)/shard_map/first_step/pallas_call | solution.py:282
  9.0 0.1 collective-permute-start.1
  9.1 1.7 %collective-permute-start.2 = (bf16[16,640]{1,0:T(8,128)(2,1)S(1)}, bf16[16,640]{1,0:T(8,128)(2,1)S(1)}, u32[]{:S(2)}, u32[]{:S(2)}) collective-permute-start(bf16[16,640]{1,0:T(8,128)(2,1)S(1)} %get-tuple-element.39), channel_id=1, source_target_pairs={{0,28},{4,8},{8,4},{12,16},{16,12},{20,24},{24,20},{28,0},{1,29},{... | collective-permute-start | bytes 61448 | tf_op jit(solution)/shard_map/ppermute | solution.py:355
  10.8 2.5 %off_face.1 = (f32[16,640]{1,0:T(8,128)S(1)}, bf16[16,5376]{1,0:T(8,128)(2,1)S(1)}, s32[1,5376]{1,0:T(1,128)S(1)}, bf16[256,5376]{1,0:T(8,128)(2,1)S(1)}) custom-call(f32[16,4352]{1,0:T(8,128)S(1)} %get-tuple-element.37.own_in, s32[1,5376]{1,0:T(1,128)S(1)} %get-tuple-element.30.slots_ref, bf16[256,5376]{1,0:T(8,128)(2,1)S(1)} %get-tuple-element.31.hots_ref, ...), custom_call_target="tpu_custom_call" | custom-call | flops 4000000000 | bytes 1000000 | tf_op jit(solution)/shard_map/off_face/pallas_call | solution.py:282
  13.3 0.0 collective-permute-done.1.near_in
  13.4 0.0 collective-permute-done.2.far_in
  13.4 1.1 %second_step.1 = (bf16[16,6144]{1,0:T(8,128)(2,1)S(1)}, bf16[16,640]{1,0:T(8,128)(2,1)S(1)}) custom-call(bf16[16,5376]{1,0:T(8,128)(2,1)S(1)} %get-tuple-element.40.inside_ref, s32[1,5376]{1,0:T(1,128)S(1)} %get-tuple-element.41.high_ref, bf16[256,5376]{1,0:T(8,128)(2,1)S(1)} %get-tuple-element.42.faces_ref, s32[1,768]{1,0:T(1,128)S(1)} %get-tuple-element.33.ghosts_ref, ...), custom_call_target="tpu_custom_call" | custom-call | flops 4000000000 | bytes 1000000 | tf_op jit(solution)/shard_map/second_step/pallas_call | solution.py:282
  14.5 0.1 collective-permute-start.3
  14.6 2.0 %second_sums.1.own_in = f32[16,4352]{1,0:T(8,128)S(1)} custom-call(f32[16,4352]{1,0:T(8,128)S(1)} %get-tuple-element.28.psi_ref, s32[1,5376]{1,0:T(1,128)S(1)} %get-tuple-element.30.slots_ref, bf16[256,5376]{1,0:T(8,128)(2,1)S(1)} %get-tuple-element.31.hots_ref, bf16[12,512,512]{2,1,0:T(8,128)(2,1)S(1)} %copy-done, s32[1,640]{1,0:T(1,128)S(1)} %get-tuple-element.32.face_ref, ...), custom_call_target="tpu_custom_call" | custom-call | flops 4000000000 | bytes 8000000 | tf_op jit(solution)/shard_map/second_sums/pallas_call | solution.py:282
  16.6 2.1 %collective-permute-done.3.below_in = bf16[16,640]{1,0:T(8,128)(2,1)S(1)} collective-permute-done((bf16[16,640]{1,0:T(8,128)(2,1)S(1)}, bf16[16,640]{1,0:T(8,128)(2,1)S(1)}, u32[]{:S(2)}, u32[]{:S(2)}) %collective-permute-start.3) | collective-permute-done | bytes 20512 | tf_op jit(solution)/shard_map/ppermute | solution.py:296
  18.6 0.4 last_faces.1
  19.0 3.7 %collective-permute-start.6 = (bf16[16,4224]{1,0:T(8,128)(2,1)S(1)}, bf16[16,4224]{1,0:T(8,128)(2,1)S(1)}, u32[]{:S(2)}, u32[]{:S(2)}) collective-permute-start(bf16[16,4224]{1,0:T(8,128)(2,1)S(1)} %get-tuple-element.48), channel_id=1, source_target_pairs={{0,3},{1,2},{2,1},{3,0},{4,7},{5,6},{6,5},{7,4},{8,11},{9,10},{10,... | collective-permute-start | bytes 405512 | tf_op jit(solution)/shard_map/ppermute | solution.py:306
  22.7 0.0 collective-permute-start.5
  22.7 0.8 %collective-permute-start.4 = (bf16[16,4224]{1,0:T(8,128)(2,1)S(1)}, bf16[16,4224]{1,0:T(8,128)(2,1)S(1)}, u32[]{:S(2)}, u32[]{:S(2)}) collective-permute-start(bf16[16,4224]{1,0:T(8,128)(2,1)S(1)} %get-tuple-element.48), channel_id=1, source_target_pairs={{0,1},{1,0},{2,3},{3,2},{4,5},{5,4},{6,7},{7,6},{8,9},{9,8},{10,11... | collective-permute-start | bytes 405512 | tf_op jit(solution)/shard_map/ppermute | solution.py:306
  23.5 3.8 %collective-permute-done.6.refs_3_ = bf16[16,4224]{1,0:T(8,128)(2,1)S(1)} collective-permute-done((bf16[16,4224]{1,0:T(8,128)(2,1)S(1)}, bf16[16,4224]{1,0:T(8,128)(2,1)S(1)}, u32[]{:S(2)}, u32[]{:S(2)}) %collective-permute-start.6) | collective-permute-done | bytes 135200 | tf_op jit(solution)/shard_map/ppermute | solution.py:306
  27.2 5.5 %collective-permute-done.5.refs_2_ = bf16[16,4224]{1,0:T(8,128)(2,1)S(1)} collective-permute-done((bf16[16,4224]{1,0:T(8,128)(2,1)S(1)}, bf16[16,4224]{1,0:T(8,128)(2,1)S(1)}, u32[]{:S(2)}, u32[]{:S(2)}) %collective-permute-start.5) | collective-permute-done | bytes 135200 | tf_op jit(solution)/shard_map/ppermute | solution.py:306
  32.7 0.0 collective-permute-done.4.refs_1_
  32.7 0.6 %gram.1 = (bf16[80,4352]{1,0:T(8,128)(2,1)S(1)}, f32[32,128]{1,0:T(8,128)S(1)}) custom-call(f32[16,4352]{1,0:T(8,128)S(1)} %get-tuple-element.47.refs_0_, bf16[16,4224]{1,0:T(8,128)(2,1)S(1)} %collective-permute-done.4.refs_1_, bf16[16,4224]{1,0:T(8,128)(2,1)S(1)} %collective-permute-done.5.refs_2_, bf16[16,4224]{1,0:T(8,128)(2,1)S(1)} %collective-permute-done.6.refs_3_), custom_call_target="tpu_custom_call" | custom-call | tf_op jit(solution)/shard_map/gram/pallas_call | solution.py:282
  33.3 0.0 collective-permute-start.7
  33.4 1.2 %collective-permute-done.7 = f32[32,128]{1,0:T(8,128)S(1)} collective-permute-done((f32[32,128]{1,0:T(8,128)S(1)}, f32[32,128]{1,0:T(8,128)S(1)}, u32[]{:S(2)}, u32[]{:S(2)}) %collective-permute-start.7) | collective-permute-done | bytes 16416 | tf_op jit(solution)/shard_map/gram_sum/ppermute | solution.py:459
  34.5 2.5 %collective-permute-start.10 = (f32[32,128]{1,0:T(8,128)S(1)}, f32[32,128]{1,0:T(8,128)S(1)}, u32[]{:S(2)}, u32[]{:S(2)}) collective-permute-start(f32[32,128]{1,0:T(8,128)S(1)} %add.12), channel_id=1, source_target_pairs={{0,24},{4,28},{8,16},{12,20},{16,8},{20,12},{24,0},{28,4},{1,25},{... | collective-permute-start | bytes 49160 | tf_op jit(solution)/shard_map/gram_sum/ppermute | solution.py:459
  37.0 0.5 %collective-permute-start.9 = (f32[32,128]{1,0:T(8,128)S(1)}, f32[32,128]{1,0:T(8,128)S(1)}, u32[]{:S(2)}, u32[]{:S(2)}) collective-permute-start(f32[32,128]{1,0:T(8,128)S(1)} %add.12), channel_id=1, source_target_pairs={{0,16},{4,20},{8,24},{12,28},{16,0},{20,4},{24,8},{28,12},{1,17},{... | collective-permute-start | bytes 49160 | tf_op jit(solution)/shard_map/gram_sum/ppermute | solution.py:459
  37.6 0.5 %collective-permute-start.8 = (f32[32,128]{1,0:T(8,128)S(1)}, f32[32,128]{1,0:T(8,128)S(1)}, u32[]{:S(2)}, u32[]{:S(2)}) collective-permute-start(f32[32,128]{1,0:T(8,128)S(1)} %add.12), channel_id=1, source_target_pairs={{0,8},{4,12},{8,0},{12,4},{16,24},{20,28},{24,16},{28,20},{1,9},{5... | collective-permute-start | bytes 49160 | tf_op jit(solution)/shard_map/gram_sum/ppermute | solution.py:459
  38.0 1.1 %collective-permute-done.10 = f32[32,128]{1,0:T(8,128)S(1)} collective-permute-done((f32[32,128]{1,0:T(8,128)S(1)}, f32[32,128]{1,0:T(8,128)S(1)}, u32[]{:S(2)}, u32[]{:S(2)}) %collective-permute-start.10) | collective-permute-done | bytes 16416 | tf_op jit(solution)/shard_map/gram_sum/ppermute | solution.py:459
  39.2 1.6 %collective-permute-done.9 = f32[32,128]{1,0:T(8,128)S(1)} collective-permute-done((f32[32,128]{1,0:T(8,128)S(1)}, f32[32,128]{1,0:T(8,128)S(1)}, u32[]{:S(2)}, u32[]{:S(2)}) %collective-permute-start.9) | collective-permute-done | bytes 16416 | tf_op jit(solution)/shard_map/gram_sum/ppermute | solution.py:459
  40.8 0.5 %collective-permute-done.8 = f32[32,128]{1,0:T(8,128)S(1)} collective-permute-done((f32[32,128]{1,0:T(8,128)S(1)}, f32[32,128]{1,0:T(8,128)S(1)}, u32[]{:S(2)}, u32[]{:S(2)}) %collective-permute-start.8) | collective-permute-done | bytes 16416 | tf_op jit(solution)/shard_map/gram_sum/ppermute | solution.py:459
  41.3 2.6 %orthonormal.1 = f32[16,4116]{1,0:T(8,128)} custom-call(f32[32,128]{1,0:T(8,128)S(1)} %add_add_fusion.gram_ref, bf16[80,4352]{1,0:T(8,128)(2,1)S(1)} %get-tuple-element.50.terms_ref), custom_call_target="tpu_custom_call" | custom-call | tf_op jit(solution)/shard_map/orthonormal/pallas_call | solution.py:282
  (2 shorter events, 0.0 us)
Async XLA Ops:
  0.0 6.4 %copy-start = (bf16[12,512,512]{2,1,0:T(8,128)(2,1)S(1)}, bf16[12,512,512]{2,1,0:T(8,128)(2,1)}, u32[]{:S(2)}) copy-start(bf16[12,512,512]{2,1,0:T(8,128)(2,1)} %ham_ref.7) | copy-start | bytes 18874372
  1.4 5.8 %collective-permute-start = (bf16[16,640]{1,0:T(8,128)(2,1)S(1)}, bf16[16,640]{1,0:T(8,128)(2,1)S(1)}, u32[]{:S(2)}, u32[]{:S(2)}) collective-permute-start(bf16[16,640]{1,0:T(8,128)(2,1)S(1)} %get-tuple-element.35), channel_id=1, source_target_pairs={{4,0},{8,4},{12,8},{16,12},{20,16},{24,20},{28,24},{0,28},{5,1},{9... | collective-permute-start | bytes 61448 | tf_op jit(solution)/shard_map/ppermute | solution.py:296
  9.0 4.3 %collective-permute-start.1 = (bf16[16,640]{1,0:T(8,128)(2,1)S(1)}, bf16[16,640]{1,0:T(8,128)(2,1)S(1)}, u32[]{:S(2)}, u32[]{:S(2)}) collective-permute-start(bf16[16,640]{1,0:T(8,128)(2,1)S(1)} %get-tuple-element.38), channel_id=1, source_target_pairs={{0,4},{4,0},{8,12},{12,8},{16,20},{20,16},{24,28},{28,24},{1,5},{5... | collective-permute-start | bytes 61448 | tf_op jit(solution)/shard_map/ppermute | solution.py:356
  9.1 4.2 %collective-permute-start.2 = (bf16[16,640]{1,0:T(8,128)(2,1)S(1)}, bf16[16,640]{1,0:T(8,128)(2,1)S(1)}, u32[]{:S(2)}, u32[]{:S(2)}) collective-permute-start(bf16[16,640]{1,0:T(8,128)(2,1)S(1)} %get-tuple-element.39), channel_id=1, source_target_pairs={{0,28},{4,8},{8,4},{12,16},{16,12},{20,24},{24,20},{28,0},{1,29},{... | collective-permute-start | bytes 61448 | tf_op jit(solution)/shard_map/ppermute | solution.py:355
  14.5 4.2 %collective-permute-start.3 = (bf16[16,640]{1,0:T(8,128)(2,1)S(1)}, bf16[16,640]{1,0:T(8,128)(2,1)S(1)}, u32[]{:S(2)}, u32[]{:S(2)}) collective-permute-start(bf16[16,640]{1,0:T(8,128)(2,1)S(1)} %get-tuple-element.46), channel_id=1, source_target_pairs={{28,0},{0,4},{4,8},{8,12},{12,16},{16,20},{20,24},{24,28},{29,1},{... | collective-permute-start | bytes 61448 | tf_op jit(solution)/shard_map/ppermute | solution.py:296
  19.0 8.2 %collective-permute-start.6 = (bf16[16,4224]{1,0:T(8,128)(2,1)S(1)}, bf16[16,4224]{1,0:T(8,128)(2,1)S(1)}, u32[]{:S(2)}, u32[]{:S(2)}) collective-permute-start(bf16[16,4224]{1,0:T(8,128)(2,1)S(1)} %get-tuple-element.48), channel_id=1, source_target_pairs={{0,3},{1,2},{2,1},{3,0},{4,7},{5,6},{6,5},{7,4},{8,11},{9,10},{10,... | collective-permute-start | bytes 405512 | tf_op jit(solution)/shard_map/ppermute | solution.py:306
  22.7 10.1 %collective-permute-start.5 = (bf16[16,4224]{1,0:T(8,128)(2,1)S(1)}, bf16[16,4224]{1,0:T(8,128)(2,1)S(1)}, u32[]{:S(2)}, u32[]{:S(2)}) collective-permute-start(bf16[16,4224]{1,0:T(8,128)(2,1)S(1)} %get-tuple-element.48), channel_id=1, source_target_pairs={{0,2},{1,3},{2,0},{3,1},{4,6},{5,7},{6,4},{7,5},{8,10},{9,11},{10,... | collective-permute-start | bytes 405512 | tf_op jit(solution)/shard_map/ppermute | solution.py:306
  22.7 10.1 %collective-permute-start.4 = (bf16[16,4224]{1,0:T(8,128)(2,1)S(1)}, bf16[16,4224]{1,0:T(8,128)(2,1)S(1)}, u32[]{:S(2)}, u32[]{:S(2)}) collective-permute-start(bf16[16,4224]{1,0:T(8,128)(2,1)S(1)} %get-tuple-element.48), channel_id=1, source_target_pairs={{0,1},{1,0},{2,3},{3,2},{4,5},{5,4},{6,7},{7,6},{8,9},{9,8},{10,11... | collective-permute-start | bytes 405512 | tf_op jit(solution)/shard_map/ppermute | solution.py:306
  33.3 1.2 %collective-permute-start.7 = (f32[32,128]{1,0:T(8,128)S(1)}, f32[32,128]{1,0:T(8,128)S(1)}, u32[]{:S(2)}, u32[]{:S(2)}) collective-permute-start(f32[32,128]{1,0:T(8,128)S(1)} %get-tuple-element.49), channel_id=1, source_target_pairs={{0,4},{4,0},{8,12},{12,8},{16,20},{20,16},{24,28},{28,24},{1,5},{5... | collective-permute-start | bytes 49160 | tf_op jit(solution)/shard_map/gram_sum/ppermute | solution.py:459
  34.5 4.6 %collective-permute-start.10 = (f32[32,128]{1,0:T(8,128)S(1)}, f32[32,128]{1,0:T(8,128)S(1)}, u32[]{:S(2)}, u32[]{:S(2)}) collective-permute-start(f32[32,128]{1,0:T(8,128)S(1)} %add.12), channel_id=1, source_target_pairs={{0,24},{4,28},{8,16},{12,20},{16,8},{20,12},{24,0},{28,4},{1,25},{... | collective-permute-start | bytes 49160 | tf_op jit(solution)/shard_map/gram_sum/ppermute | solution.py:459
  37.0 3.7 %collective-permute-start.9 = (f32[32,128]{1,0:T(8,128)S(1)}, f32[32,128]{1,0:T(8,128)S(1)}, u32[]{:S(2)}, u32[]{:S(2)}) collective-permute-start(f32[32,128]{1,0:T(8,128)S(1)} %add.12), channel_id=1, source_target_pairs={{0,16},{4,20},{8,24},{12,28},{16,0},{20,4},{24,8},{28,12},{1,17},{... | collective-permute-start | bytes 49160 | tf_op jit(solution)/shard_map/gram_sum/ppermute | solution.py:459
  37.6 3.7 %collective-permute-start.8 = (f32[32,128]{1,0:T(8,128)S(1)}, f32[32,128]{1,0:T(8,128)S(1)}, u32[]{:S(2)}, u32[]{:S(2)}) collective-permute-start(f32[32,128]{1,0:T(8,128)S(1)} %add.12), channel_id=1, source_target_pairs={{0,8},{4,12},{8,0},{12,4},{16,24},{20,28},{24,16},{28,20},{1,9},{5... | collective-permute-start | bytes 49160 | tf_op jit(solution)/shard_map/gram_sum/ppermute | solution.py:459

commit v10 on v9

--- a/solution.py
+++ b/solution.py
@@ -10,6 +10,7 @@
 FACE_EL = 64
 IN_EL = 448
 LANES = 256
+FACE_LANES = 128
 
 CENTER = 6.25
 HALF_WIDTH = 7.5
@@ -25,14 +26,14 @@
     return -(-count // unit) * unit
 
 
-def one_hot(low):
-    rows = lax.broadcasted_iota(jnp.int32, (LANES, low.shape[1]), 0)
+def one_hot(low, lanes=LANES):
+    rows = lax.broadcasted_iota(jnp.int32, (lanes, low.shape[1]), 0)
     return jnp.where(rows == low, 1.0, 0.0).astype(BF16)
 
 
-def stacked(field):
-    blocks = field.shape[1] // LANES
-    return jnp.concatenate([field[:, i * LANES : (i + 1) * LANES] for i in range(blocks)], axis=0)
+def stacked(field, lanes=LANES):
+    blocks = field.shape[1] // lanes
+    return jnp.concatenate([field[:, i * lanes : (i + 1) * lanes] for i in range(blocks)], axis=0)
 
 
 def unstacked(rows, bands):
@@ -201,7 +202,7 @@
     face = face_ref[...]
     number = lax.broadcasted_iota(jnp.int32, (blocks, face.shape[1]), 1)
     held = lax.broadcasted_iota(jnp.int32, number.shape, 0) == (face >> 8)
-    digits = [jnp.where(held, digit, 0).astype(F32).astype(BF16) for digit in ((number >> 8) + 1, number & 255)]
+    digits = [jnp.where(held, digit, 0).astype(F32).astype(BF16) for digit in (number // FACE_LANES + 1, number % FACE_LANES)]
     face_hot = one_hot(face & 255)
     table = lax.dot_general(
         jnp.concatenate(digits, axis=0), face_hot, (((1,), (1,)), ((), ())), preferred_element_type=F32
@@ -216,7 +217,7 @@
         block = jnp.sum(jnp.where(held, both[:blocks], 0.0), axis=0, keepdims=True).astype(jnp.int32)
         lane = jnp.sum(jnp.where(held, both[blocks:], 0.0), axis=0, keepdims=True).astype(jnp.int32)
         high_ref[:, tile] = block - 1
-        faces_ref[:, tile] = one_hot(jnp.where(block > 0, lane, -1))
+        faces_ref[:, tile] = one_hot(jnp.where(block > 0, lane, -1), FACE_LANES)
         inside_ref[:, tile] = jnp.where(block > 0, 0.0, pick(rows, high, hot, bands)).astype(BF16)
 
 
@@ -230,7 +231,7 @@
     near, far = near_in[...].astype(F32), far_in[...].astype(F32)
     below = jnp.where(odd, near, far)
     above = jnp.where(odd, far, near)
-    faces = stacked(widened(low_in[...] + below)).astype(BF16)
+    faces = stacked(low_in[...] + below, FACE_LANES).astype(BF16)
     ghost = stacked(widened(upper_in[...] + above)).astype(BF16)
     ghosts = ghosts_ref[...]
     pick_into(outside, ghost, ghosts >> 8, hosts_ref)
@@ -357,7 +358,7 @@
     with jax.named_scope("off_face"):
         low, inside, high, faces = call(
             far_kernel,
-            (face_field, shape((bands, inner_count), BF16), shape((1, inner_count), jnp.int32), shape((LANES, inner_count), BF16)),
+            (face_field, shape((bands, inner_count), BF16), shape((1, inner_count), jnp.int32), shape((FACE_LANES, inner_count), BF16)),
             (current, slots, hots, face), flops=4 * 10**9, moved=10**6,
         )
     with jax.named_scope("second_step"):
@@ -444,8 +445,9 @@
     diagonal = jnp.where(column // bands == lax.axis_index("band"), own, 0.0)
     diagonal = sum(diagonal[:, i : i + bands] for i in range(0, total, bands))
     rows = jnp.concatenate(halves(jnp.concatenate([own, diagonal], axis=1)), axis=0)
-    both = jnp.dot(rows, terms_ref[...], preferred_element_type=F32)
-    out_ref[...] = (both[:bands] + both[bands:])[:, :nodes]
+    for tile in tiles(nodes, 2 * LANES):
+        both = jnp.dot(rows, terms_ref[:, tile], preferred_element_type=F32)
+        out_ref[:, tile] = both[:bands] + both[bands:]
 
 
 def space_sum(block):

time: 44 us -> 43.7 us (level)
  Pallas kernels: 14.8 us -> 14 us
    pallas_call x10, Pallas kernels: 14.8 us -> 14 us  [call(): pl.pallas_call(kernel, out_shape=out_shape, in_specs=[HBM if i in far els...]
    ppermute x1, waiting for transfers between devices: 0.01 us -> 0.47 us  [filter_field(): lax.ppermute(to_far, 'space', [(i, ((i + 1 ^ 1) - 1) % domains) for i in...]
  transfers between devices with their start and end apart: 11 -> 11, of which waited for: 7 -> 8; matrix products, arithmetic and copies ran while one was open for 0% -> 0% of each run, Pallas kernels for 16% -> 15%
where the time goes in v10:
time: 43.7 us; the launch traced here: 43.5 us
  waiting for transfers between devices  16.2 us (37%)
  Pallas kernels  14 us (32%)
  starting transfers between devices  13.2 us (30%)
    pallas_call x10, Pallas kernels, call(): pl.pallas_call(kernel, out_shape=out_shape, in_specs=[HBM if i in far els...  14 us
    ppermute x3, waiting for transfers between devices, partner(): return lax.ppermute(block, axis, [(i, i ^ distance) for i in range(size)])  8.96 us
    ppermute x4, waiting for transfers between devices, space_sum(): lax.ppermute(block, 'space', [(i, i ^ step * k) for i in range(size)])  4.72 us
    ppermute x3, starting transfers between devices, partner(): return lax.ppermute(block, axis, [(i, i ^ distance) for i in range(size)])  4.45 us
    ppermute x4, starting transfers between devices, space_sum(): lax.ppermute(block, 'space', [(i, i ^ step * k) for i in range(size)])  3.51 us
    ppermute x2, starting transfers between devices, from_behind(): return lax.ppermute(block, axis, route)  3.44 us
    ppermute x2, waiting for transfers between devices, from_behind(): return lax.ppermute(block, axis, route)  2.07 us
    ppermute x1, starting transfers between devices, filter_field(): lax.ppermute(to_far, 'space', [(i, ((i + 1 ^ 1) - 1) % domains) for i in...  1.71 us
  transfers between devices with their start and end apart: 11, of which 8 were waited for; matrix products, arithmetic and copies ran while one was open for 0% of the time, Pallas kernels for 15%

profile of v10, /device:TPU:0, one launch (start us, length us, event | category | flops | bytes accessed | tf_op | source)
XLA Modules:
  0.0 43.5 jit_solution(7062789497396438794)
XLA Ops:
  0.0 0.0 copy-start
  0.0 1.4 %face_values.1 = (bf16[16,640]{1,0:T(8,128)(2,1)S(1)}, f32[16,4352]{1,0:T(8,128)S(1)}, s32[12,512]{1,0:T(8,128)S(1)}, s32[1,640]{1,0:T(1,128)S(1)}) custom-call(f32[16,4116]{1,0:T(8,128)} %psi_hbm.1, s32[12,512]{1,0:T(8,128)} %conn_hbm.1, s32[588]{0:T(1024)} %face_hbm.1), custom_call_target="tpu_custom_call" | custom-call | flops 20000000000 | bytes 40000000 | tf_op jit(solution)/shard_map/face_values/pallas_call | solution.py:283
  1.4 3.4 %collective-permute-start = (bf16[16,640]{1,0:T(8,128)(2,1)S(1)}, bf16[16,640]{1,0:T(8,128)(2,1)S(1)}, u32[]{:S(2)}, u32[]{:S(2)}) collective-permute-start(bf16[16,640]{1,0:T(8,128)(2,1)S(1)} %get-tuple-element.35), channel_id=1, source_target_pairs={{4,0},{8,4},{12,8},{16,12},{20,16},{24,20},{28,24},{0,28},{5,1},{9... | collective-permute-start | bytes 61448 | tf_op jit(solution)/shard_map/ppermute | solution.py:297
  4.8 1.6 %near_values.1 = (bf16[16,5376]{1,0:T(8,128)(2,1)S(1)}, s32[1,5376]{1,0:T(1,128)S(1)}, s32[1,768]{1,0:T(1,128)S(1)}, bf16[256,5376]{1,0:T(8,128)(2,1)S(1)}, bf16[256,768]{1,0:T(8,128)(2,1)S(1)}) custom-call(f32[16,4352]{1,0:T(8,128)S(1)} %get-tuple-element.28.psi_ref, s32[12,512]{1,0:T(8,128)S(1)} %get-tuple-element.29.conn_ref), custom_call_target="tpu_custom_call" | custom-call | tf_op jit(solution)/shard_map/near_values/pallas_call | solution.py:283
  6.4 0.0 copy-done
  6.4 0.8 %interior.1.part_ref = f32[16,6144]{1,0:T(8,128)S(1)} custom-call(bf16[16,5376]{1,0:T(8,128)(2,1)S(1)} %get-tuple-element.36.inside_ref, bf16[12,512,512]{2,1,0:T(8,128)(2,1)S(1)} %copy-done), custom_call_target="tpu_custom_call" | custom-call | flops 4000000000 | bytes 8000000 | tf_op jit(solution)/shard_map/interior/pallas_call | solution.py:283
  7.3 0.0 collective-permute-done.ghost_ref
  7.3 1.8 %first_step.1 = (f32[16,4352]{1,0:T(8,128)S(1)}, f32[16,640]{1,0:T(8,128)S(1)}, bf16[16,640]{1,0:T(8,128)(2,1)S(1)}, bf16[16,640]{1,0:T(8,128)(2,1)S(1)}) custom-call(f32[16,4352]{1,0:T(8,128)S(1)} %get-tuple-element.28.psi_ref, s32[1,5376]{1,0:T(1,128)S(1)} %get-tuple-element.30.slots_ref, s32[1,768]{1,0:T(1,128)S(1)} %get-tuple-element.33.ghosts_ref, ...), custom_call_target="tpu_custom_call" | custom-call | flops 4000000000 | bytes 1000000 | tf_op jit(solution)/shard_map/first_step/pallas_call | solution.py:283
  9.0 0.1 collective-permute-start.1
  9.1 1.7 %collective-permute-start.2 = (bf16[16,640]{1,0:T(8,128)(2,1)S(1)}, bf16[16,640]{1,0:T(8,128)(2,1)S(1)}, u32[]{:S(2)}, u32[]{:S(2)}) collective-permute-start(bf16[16,640]{1,0:T(8,128)(2,1)S(1)} %get-tuple-element.39), channel_id=1, source_target_pairs={{0,28},{4,8},{8,4},{12,16},{16,12},{20,24},{24,20},{28,0},{1,29},{... | collective-permute-start | bytes 61448 | tf_op jit(solution)/shard_map/ppermute | solution.py:356
  10.8 2.0 %off_face.1 = (f32[16,640]{1,0:T(8,128)S(1)}, bf16[16,5376]{1,0:T(8,128)(2,1)S(1)}, s32[1,5376]{1,0:T(1,128)S(1)}, bf16[128,5376]{1,0:T(8,128)(2,1)S(1)}) custom-call(f32[16,4352]{1,0:T(8,128)S(1)} %get-tuple-element.37.own_in, s32[1,5376]{1,0:T(1,128)S(1)} %get-tuple-element.30.slots_ref, bf16[256,5376]{1,0:T(8,128)(2,1)S(1)} %get-tuple-element.31.hots_ref, ...), custom_call_target="tpu_custom_call" | custom-call | flops 4000000000 | bytes 1000000 | tf_op jit(solution)/shard_map/off_face/pallas_call | solution.py:283
  12.8 0.0 collective-permute-done.1.near_in
  12.8 0.5 %collective-permute-done.2.far_in = bf16[16,640]{1,0:T(8,128)(2,1)S(1)} collective-permute-done((bf16[16,640]{1,0:T(8,128)(2,1)S(1)}, bf16[16,640]{1,0:T(8,128)(2,1)S(1)}, u32[]{:S(2)}, u32[]{:S(2)}) %collective-permute-start.2) | collective-permute-done | bytes 20512 | tf_op jit(solution)/shard_map/ppermute | solution.py:356
  13.3 0.9 %second_step.1 = (bf16[16,6144]{1,0:T(8,128)(2,1)S(1)}, bf16[16,640]{1,0:T(8,128)(2,1)S(1)}) custom-call(bf16[16,5376]{1,0:T(8,128)(2,1)S(1)} %get-tuple-element.40.inside_ref, s32[1,5376]{1,0:T(1,128)S(1)} %get-tuple-element.41.high_ref, bf16[128,5376]{1,0:T(8,128)(2,1)S(1)} %get-tuple-element.42.faces_ref, s32[1,768]{1,0:T(1,128)S(1)} %get-tuple-element.33.ghosts_ref, ...), custom_call_target="tpu_custom_call" | custom-call | flops 4000000000 | bytes 1000000 | tf_op jit(solution)/shard_map/second_step/pallas_call | solution.py:283
  14.2 0.1 collective-permute-start.3
  14.2 2.0 %second_sums.1.own_in = f32[16,4352]{1,0:T(8,128)S(1)} custom-call(f32[16,4352]{1,0:T(8,128)S(1)} %get-tuple-element.28.psi_ref, s32[1,5376]{1,0:T(1,128)S(1)} %get-tuple-element.30.slots_ref, bf16[256,5376]{1,0:T(8,128)(2,1)S(1)} %get-tuple-element.31.hots_ref, bf16[12,512,512]{2,1,0:T(8,128)(2,1)S(1)} %copy-done, s32[1,640]{1,0:T(1,128)S(1)} %get-tuple-element.32.face_ref, ...), custom_call_target="tpu_custom_call" | custom-call | flops 4000000000 | bytes 8000000 | tf_op jit(solution)/shard_map/second_sums/pallas_call | solution.py:283
  16.3 2.1 %collective-permute-done.3.below_in = bf16[16,640]{1,0:T(8,128)(2,1)S(1)} collective-permute-done((bf16[16,640]{1,0:T(8,128)(2,1)S(1)}, bf16[16,640]{1,0:T(8,128)(2,1)S(1)}, u32[]{:S(2)}, u32[]{:S(2)}) %collective-permute-start.3) | collective-permute-done | bytes 20512 | tf_op jit(solution)/shard_map/ppermute | solution.py:297
  18.3 0.4 last_faces.1
  18.7 3.7 %collective-permute-start.6 = (bf16[16,4224]{1,0:T(8,128)(2,1)S(1)}, bf16[16,4224]{1,0:T(8,128)(2,1)S(1)}, u32[]{:S(2)}, u32[]{:S(2)}) collective-permute-start(bf16[16,4224]{1,0:T(8,128)(2,1)S(1)} %get-tuple-element.48), channel_id=1, source_target_pairs={{0,3},{1,2},{2,1},{3,0},{4,7},{5,6},{6,5},{7,4},{8,11},{9,10},{10,... | collective-permute-start | bytes 405512 | tf_op jit(solution)/shard_map/ppermute | solution.py:307
  22.3 0.0 collective-permute-start.5
  22.3 0.8 %collective-permute-start.4 = (bf16[16,4224]{1,0:T(8,128)(2,1)S(1)}, bf16[16,4224]{1,0:T(8,128)(2,1)S(1)}, u32[]{:S(2)}, u32[]{:S(2)}) collective-permute-start(bf16[16,4224]{1,0:T(8,128)(2,1)S(1)} %get-tuple-element.48), channel_id=1, source_target_pairs={{0,1},{1,0},{2,3},{3,2},{4,5},{5,4},{6,7},{7,6},{8,9},{9,8},{10,11... | collective-permute-start | bytes 405512 | tf_op jit(solution)/shard_map/ppermute | solution.py:307
  23.1 3.5 %collective-permute-done.6.refs_3_ = bf16[16,4224]{1,0:T(8,128)(2,1)S(1)} collective-permute-done((bf16[16,4224]{1,0:T(8,128)(2,1)S(1)}, bf16[16,4224]{1,0:T(8,128)(2,1)S(1)}, u32[]{:S(2)}, u32[]{:S(2)}) %collective-permute-start.6) | collective-permute-done | bytes 135200 | tf_op jit(solution)/shard_map/ppermute | solution.py:307
  26.6 5.5 %collective-permute-done.5.refs_2_ = bf16[16,4224]{1,0:T(8,128)(2,1)S(1)} collective-permute-done((bf16[16,4224]{1,0:T(8,128)(2,1)S(1)}, bf16[16,4224]{1,0:T(8,128)(2,1)S(1)}, u32[]{:S(2)}, u32[]{:S(2)}) %collective-permute-start.5) | collective-permute-done | bytes 135200 | tf_op jit(solution)/shard_map/ppermute | solution.py:307
  32.1 0.0 collective-permute-done.4.refs_1_
  32.1 0.6 %gram.1 = (bf16[80,4352]{1,0:T(8,128)(2,1)S(1)}, f32[32,128]{1,0:T(8,128)S(1)}) custom-call(f32[16,4352]{1,0:T(8,128)S(1)} %get-tuple-element.47.refs_0_, bf16[16,4224]{1,0:T(8,128)(2,1)S(1)} %collective-permute-done.4.refs_1_, bf16[16,4224]{1,0:T(8,128)(2,1)S(1)} %collective-permute-done.5.refs_2_, bf16[16,4224]{1,0:T(8,128)(2,1)S(1)} %collective-permute-done.6.refs_3_), custom_call_target="tpu_custom_call" | custom-call | tf_op jit(solution)/shard_map/gram/pallas_call | solution.py:283
  32.7 0.0 collective-permute-start.7
  32.7 1.2 %collective-permute-done.7 = f32[32,128]{1,0:T(8,128)S(1)} collective-permute-done((f32[32,128]{1,0:T(8,128)S(1)}, f32[32,128]{1,0:T(8,128)S(1)}, u32[]{:S(2)}, u32[]{:S(2)}) %collective-permute-start.7) | collective-permute-done | bytes 16416 | tf_op jit(solution)/shard_map/gram_sum/ppermute | solution.py:461
  33.9 2.8 %collective-permute-start.10 = (f32[32,128]{1,0:T(8,128)S(1)}, f32[32,128]{1,0:T(8,128)S(1)}, u32[]{:S(2)}, u32[]{:S(2)}) collective-permute-start(f32[32,128]{1,0:T(8,128)S(1)} %add.12), channel_id=1, source_target_pairs={{0,24},{4,28},{8,16},{12,20},{16,8},{20,12},{24,0},{28,4},{1,25},{... | collective-permute-start | bytes 49160 | tf_op jit(solution)/shard_map/gram_sum/ppermute | solution.py:461
  36.7 0.5 %collective-permute-start.9 = (f32[32,128]{1,0:T(8,128)S(1)}, f32[32,128]{1,0:T(8,128)S(1)}, u32[]{:S(2)}, u32[]{:S(2)}) collective-permute-start(f32[32,128]{1,0:T(8,128)S(1)} %add.12), channel_id=1, source_target_pairs={{0,16},{4,20},{8,24},{12,28},{16,0},{20,4},{24,8},{28,12},{1,17},{... | collective-permute-start | bytes 49160 | tf_op jit(solution)/shard_map/gram_sum/ppermute | solution.py:461
  37.2 0.2 collective-permute-start.8
  37.4 1.1 %collective-permute-done.10 = f32[32,128]{1,0:T(8,128)S(1)} collective-permute-done((f32[32,128]{1,0:T(8,128)S(1)}, f32[32,128]{1,0:T(8,128)S(1)}, u32[]{:S(2)}, u32[]{:S(2)}) %collective-permute-start.10) | collective-permute-done | bytes 16416 | tf_op jit(solution)/shard_map/gram_sum/ppermute | solution.py:461
  38.5 1.9 %collective-permute-done.9 = f32[32,128]{1,0:T(8,128)S(1)} collective-permute-done((f32[32,128]{1,0:T(8,128)S(1)}, f32[32,128]{1,0:T(8,128)S(1)}, u32[]{:S(2)}, u32[]{:S(2)}) %collective-permute-start.9) | collective-permute-done | bytes 16416 | tf_op jit(solution)/shard_map/gram_sum/ppermute | solution.py:461
  40.5 0.5 %collective-permute-done.8 = f32[32,128]{1,0:T(8,128)S(1)} collective-permute-done((f32[32,128]{1,0:T(8,128)S(1)}, f32[32,128]{1,0:T(8,128)S(1)}, u32[]{:S(2)}, u32[]{:S(2)}) %collective-permute-start.8) | collective-permute-done | bytes 16416 | tf_op jit(solution)/shard_map/gram_sum/ppermute | solution.py:461
  41.0 2.6 %orthonormal.1 = f32[16,4116]{1,0:T(8,128)} custom-call(f32[32,128]{1,0:T(8,128)S(1)} %add_add_fusion.gram_ref, bf16[80,4352]{1,0:T(8,128)(2,1)S(1)} %get-tuple-element.50.terms_ref), custom_call_target="tpu_custom_call" | custom-call | tf_op jit(solution)/shard_map/orthonormal/pallas_call | solution.py:283
  (2 shorter events, 0.0 us)
Async XLA Ops:
  0.0 6.4 %copy-start = (bf16[12,512,512]{2,1,0:T(8,128)(2,1)S(1)}, bf16[12,512,512]{2,1,0:T(8,128)(2,1)}, u32[]{:S(2)}) copy-start(bf16[12,512,512]{2,1,0:T(8,128)(2,1)} %ham_ref.7) | copy-start | bytes 18874372
  1.4 5.8 %collective-permute-start = (bf16[16,640]{1,0:T(8,128)(2,1)S(1)}, bf16[16,640]{1,0:T(8,128)(2,1)S(1)}, u32[]{:S(2)}, u32[]{:S(2)}) collective-permute-start(bf16[16,640]{1,0:T(8,128)(2,1)S(1)} %get-tuple-element.35), channel_id=1, source_target_pairs={{4,0},{8,4},{12,8},{16,12},{20,16},{24,20},{28,24},{0,28},{5,1},{9... | collective-permute-start | bytes 61448 | tf_op jit(solution)/shard_map/ppermute | solution.py:297
  9.0 3.8 %collective-permute-start.1 = (bf16[16,640]{1,0:T(8,128)(2,1)S(1)}, bf16[16,640]{1,0:T(8,128)(2,1)S(1)}, u32[]{:S(2)}, u32[]{:S(2)}) collective-permute-start(bf16[16,640]{1,0:T(8,128)(2,1)S(1)} %get-tuple-element.38), channel_id=1, source_target_pairs={{0,4},{4,0},{8,12},{12,8},{16,20},{20,16},{24,28},{28,24},{1,5},{5... | collective-permute-start | bytes 61448 | tf_op jit(solution)/shard_map/ppermute | solution.py:357
  9.1 4.2 %collective-permute-start.2 = (bf16[16,640]{1,0:T(8,128)(2,1)S(1)}, bf16[16,640]{1,0:T(8,128)(2,1)S(1)}, u32[]{:S(2)}, u32[]{:S(2)}) collective-permute-start(bf16[16,640]{1,0:T(8,128)(2,1)S(1)} %get-tuple-element.39), channel_id=1, source_target_pairs={{0,28},{4,8},{8,4},{12,16},{16,12},{20,24},{24,20},{28,0},{1,29},{... | collective-permute-start | bytes 61448 | tf_op jit(solution)/shard_map/ppermute | solution.py:356
  14.2 4.2 %collective-permute-start.3 = (bf16[16,640]{1,0:T(8,128)(2,1)S(1)}, bf16[16,640]{1,0:T(8,128)(2,1)S(1)}, u32[]{:S(2)}, u32[]{:S(2)}) collective-permute-start(bf16[16,640]{1,0:T(8,128)(2,1)S(1)} %get-tuple-element.46), channel_id=1, source_target_pairs={{28,0},{0,4},{4,8},{8,12},{12,16},{16,20},{20,24},{24,28},{29,1},{... | collective-permute-start | bytes 61448 | tf_op jit(solution)/shard_map/ppermute | solution.py:297
  18.7 7.9 %collective-permute-start.6 = (bf16[16,4224]{1,0:T(8,128)(2,1)S(1)}, bf16[16,4224]{1,0:T(8,128)(2,1)S(1)}, u32[]{:S(2)}, u32[]{:S(2)}) collective-permute-start(bf16[16,4224]{1,0:T(8,128)(2,1)S(1)} %get-tuple-element.48), channel_id=1, source_target_pairs={{0,3},{1,2},{2,1},{3,0},{4,7},{5,6},{6,5},{7,4},{8,11},{9,10},{10,... | collective-permute-start | bytes 405512 | tf_op jit(solution)/shard_map/ppermute | solution.py:307
  22.3 9.8 %collective-permute-start.5 = (bf16[16,4224]{1,0:T(8,128)(2,1)S(1)}, bf16[16,4224]{1,0:T(8,128)(2,1)S(1)}, u32[]{:S(2)}, u32[]{:S(2)}) collective-permute-start(bf16[16,4224]{1,0:T(8,128)(2,1)S(1)} %get-tuple-element.48), channel_id=1, source_target_pairs={{0,2},{1,3},{2,0},{3,1},{4,6},{5,7},{6,4},{7,5},{8,10},{9,11},{10,... | collective-permute-start | bytes 405512 | tf_op jit(solution)/shard_map/ppermute | solution.py:307
  22.3 9.8 %collective-permute-start.4 = (bf16[16,4224]{1,0:T(8,128)(2,1)S(1)}, bf16[16,4224]{1,0:T(8,128)(2,1)S(1)}, u32[]{:S(2)}, u32[]{:S(2)}) collective-permute-start(bf16[16,4224]{1,0:T(8,128)(2,1)S(1)} %get-tuple-element.48), channel_id=1, source_target_pairs={{0,1},{1,0},{2,3},{3,2},{4,5},{5,4},{6,7},{7,6},{8,9},{9,8},{10,11... | collective-permute-start | bytes 405512 | tf_op jit(solution)/shard_map/ppermute | solution.py:307
  32.7 1.2 %collective-permute-start.7 = (f32[32,128]{1,0:T(8,128)S(1)}, f32[32,128]{1,0:T(8,128)S(1)}, u32[]{:S(2)}, u32[]{:S(2)}) collective-permute-start(f32[32,128]{1,0:T(8,128)S(1)} %get-tuple-element.49), channel_id=1, source_target_pairs={{0,4},{4,0},{8,12},{12,8},{16,20},{20,16},{24,28},{28,24},{1,5},{5... | collective-permute-start | bytes 49160 | tf_op jit(solution)/shard_map/gram_sum/ppermute | solution.py:461
  33.9 4.6 %collective-permute-start.10 = (f32[32,128]{1,0:T(8,128)S(1)}, f32[32,128]{1,0:T(8,128)S(1)}, u32[]{:S(2)}, u32[]{:S(2)}) collective-permute-start(f32[32,128]{1,0:T(8,128)S(1)} %add.12), channel_id=1, source_target_pairs={{0,24},{4,28},{8,16},{12,20},{16,8},{20,12},{24,0},{28,4},{1,25},{... | collective-permute-start | bytes 49160 | tf_op jit(solution)/shard_map/gram_sum/ppermute | solution.py:461
  36.7 3.7 %collective-permute-start.9 = (f32[32,128]{1,0:T(8,128)S(1)}, f32[32,128]{1,0:T(8,128)S(1)}, u32[]{:S(2)}, u32[]{:S(2)}) collective-permute-start(f32[32,128]{1,0:T(8,128)S(1)} %add.12), channel_id=1, source_target_pairs={{0,16},{4,20},{8,24},{12,28},{16,0},{20,4},{24,8},{28,12},{1,17},{... | collective-permute-start | bytes 49160 | tf_op jit(solution)/shard_map/gram_sum/ppermute | solution.py:461
  37.2 3.7 %collective-permute-start.8 = (f32[32,128]{1,0:T(8,128)S(1)}, f32[32,128]{1,0:T(8,128)S(1)}, u32[]{:S(2)}, u32[]{:S(2)}) collective-permute-start(f32[32,128]{1,0:T(8,128)S(1)} %add.12), channel_id=1, source_target_pairs={{0,8},{4,12},{8,0},{12,4},{16,24},{20,28},{24,16},{28,20},{1,9},{5... | collective-permute-start | bytes 49160 | tf_op jit(solution)/shard_map/gram_sum/ppermute | solution.py:461

commit v11 on v10

--- a/solution.py
+++ b/solution.py
@@ -27,8 +27,11 @@
 
 
 def one_hot(low, lanes=LANES):
-    rows = lax.broadcasted_iota(jnp.int32, (lanes, low.shape[1]), 0)
-    return jnp.where(rows == low, 1.0, 0.0).astype(BF16)
+    shape = (lanes, low.shape[1])
+    rows = lax.broadcasted_iota(jnp.int32, shape, 0).astype(jnp.int16)
+    low = jnp.broadcast_to(low, (16, low.shape[1])).astype(jnp.int16)
+    low = jnp.concatenate([low] * (lanes // 16), axis=0)
+    return jnp.where(rows == low, jnp.ones(shape, BF16), jnp.zeros(shape, BF16))
 
 
 def stacked(field, lanes=LANES):

time: 43.7 us -> 43.3 us (level)
  Pallas kernels: 14 us -> 13.2 us
  starting transfers between devices: 13.2 us -> 13.8 us
    pallas_call x10, Pallas kernels: 14 us -> 13.2 us  [call(): pl.pallas_call(kernel, out_shape=out_shape, in_specs=[HBM if i in far els...]
    ppermute x1, starting transfers between devices: 1.71 us -> 2.27 us  [filter_field(): lax.ppermute(to_far, 'space', [(i, ((i + 1 ^ 1) - 1) % domains) for i in...]
    ppermute x3, waiting for transfers between devices: 8.96 us -> 9.48 us  [partner(): return lax.ppermute(block, axis, [(i, i ^ distance) for i in range(size)])]
  transfers between devices with their start and end apart: 11 -> 11, of which waited for: 8 -> 8; matrix products, arithmetic and copies ran while one was open for 0% -> 0% of each run, Pallas kernels for 15% -> 13%
where the time goes in v11:
time: 43.3 us; the launch traced here: 43.2 us
  waiting for transfers between devices  16.1 us (37%)
  starting transfers between devices  13.8 us (32%)
  Pallas kernels  13.2 us (30%)
    pallas_call x10, Pallas kernels, call(): pl.pallas_call(kernel, out_shape=out_shape, in_specs=[HBM if i in far els...  13.2 us
    ppermute x3, waiting for transfers between devices, partner(): return lax.ppermute(block, axis, [(i, i ^ distance) for i in range(size)])  9.48 us
    ppermute x3, starting transfers between devices, partner(): return lax.ppermute(block, axis, [(i, i ^ distance) for i in range(size)])  4.45 us
    ppermute x4, waiting for transfers between devices, space_sum(): lax.ppermute(block, 'space', [(i, i ^ step * k) for i in range(size)])  4.39 us
    ppermute x4, starting transfers between devices, space_sum(): lax.ppermute(block, 'space', [(i, i ^ step * k) for i in range(size)])  3.51 us
    ppermute x2, starting transfers between devices, from_behind(): return lax.ppermute(block, axis, route)  3.44 us
    ppermute x1, starting transfers between devices, filter_field(): lax.ppermute(to_far, 'space', [(i, ((i + 1 ^ 1) - 1) % domains) for i in...  2.27 us
    ppermute x2, waiting for transfers between devices, from_behind(): return lax.ppermute(block, axis, route)  2.08 us
  transfers between devices with their start and end apart: 11, of which 8 were waited for; matrix products, arithmetic and copies ran while one was open for 0% of the time, Pallas kernels for 13%

profile of v11, /device:TPU:0, one launch (start us, length us, event | category | flops | bytes accessed | tf_op | source)
XLA Modules:
  0.0 43.2 jit_solution(6785403710450591688)
XLA Ops:
  0.0 0.0 copy-start
  0.0 1.4 %face_values.1 = (bf16[16,640]{1,0:T(8,128)(2,1)S(1)}, f32[16,4352]{1,0:T(8,128)S(1)}, s32[12,512]{1,0:T(8,128)S(1)}, s32[1,640]{1,0:T(1,128)S(1)}) custom-call(f32[16,4116]{1,0:T(8,128)} %psi_hbm.1, s32[12,512]{1,0:T(8,128)} %conn_hbm.1, s32[588]{0:T(1024)} %face_hbm.1), custom_call_target="tpu_custom_call" | custom-call | flops 20000000000 | bytes 40000000 | tf_op jit(solution)/shard_map/face_values/pallas_call | solution.py:286
  1.4 3.4 %collective-permute-start = (bf16[16,640]{1,0:T(8,128)(2,1)S(1)}, bf16[16,640]{1,0:T(8,128)(2,1)S(1)}, u32[]{:S(2)}, u32[]{:S(2)}) collective-permute-start(bf16[16,640]{1,0:T(8,128)(2,1)S(1)} %get-tuple-element.35), channel_id=1, source_target_pairs={{4,0},{8,4},{12,8},{16,12},{20,16},{24,20},{28,24},{0,28},{5,1},{9... | collective-permute-start | bytes 61448 | tf_op jit(solution)/shard_map/ppermute | solution.py:300
  4.8 1.0 %near_values.1 = (bf16[16,5376]{1,0:T(8,128)(2,1)S(1)}, s32[1,5376]{1,0:T(1,128)S(1)}, s32[1,768]{1,0:T(1,128)S(1)}, bf16[256,5376]{1,0:T(8,128)(2,1)S(1)}, bf16[256,768]{1,0:T(8,128)(2,1)S(1)}) custom-call(f32[16,4352]{1,0:T(8,128)S(1)} %get-tuple-element.28.psi_ref, s32[12,512]{1,0:T(8,128)S(1)} %get-tuple-element.29.conn_ref), custom_call_target="tpu_custom_call" | custom-call | tf_op jit(solution)/shard_map/near_values/pallas_call | solution.py:286
  5.9 0.0 copy-done
  5.9 0.8 %interior.1.part_ref = f32[16,6144]{1,0:T(8,128)S(1)} custom-call(bf16[16,5376]{1,0:T(8,128)(2,1)S(1)} %get-tuple-element.36.inside_ref, bf16[12,512,512]{2,1,0:T(8,128)(2,1)S(1)} %copy-done), custom_call_target="tpu_custom_call" | custom-call | flops 4000000000 | bytes 8000000 | tf_op jit(solution)/shard_map/interior/pallas_call | solution.py:286
  6.7 0.0 collective-permute-done.ghost_ref
  6.7 1.8 %first_step.1 = (f32[16,4352]{1,0:T(8,128)S(1)}, f32[16,640]{1,0:T(8,128)S(1)}, bf16[16,640]{1,0:T(8,128)(2,1)S(1)}, bf16[16,640]{1,0:T(8,128)(2,1)S(1)}) custom-call(f32[16,4352]{1,0:T(8,128)S(1)} %get-tuple-element.28.psi_ref, s32[1,5376]{1,0:T(1,128)S(1)} %get-tuple-element.30.slots_ref, s32[1,768]{1,0:T(1,128)S(1)} %get-tuple-element.33.ghosts_ref, ...), custom_call_target="tpu_custom_call" | custom-call | flops 4000000000 | bytes 1000000 | tf_op jit(solution)/shard_map/first_step/pallas_call | solution.py:286
  8.5 0.1 collective-permute-start.1
  8.6 2.3 %collective-permute-start.2 = (bf16[16,640]{1,0:T(8,128)(2,1)S(1)}, bf16[16,640]{1,0:T(8,128)(2,1)S(1)}, u32[]{:S(2)}, u32[]{:S(2)}) collective-permute-start(bf16[16,640]{1,0:T(8,128)(2,1)S(1)} %get-tuple-element.39), channel_id=1, source_target_pairs={{0,28},{4,8},{8,4},{12,16},{16,12},{20,24},{24,20},{28,0},{1,29},{... | collective-permute-start | bytes 61448 | tf_op jit(solution)/shard_map/ppermute | solution.py:359
  10.9 1.8 %off_face.1 = (f32[16,640]{1,0:T(8,128)S(1)}, bf16[16,5376]{1,0:T(8,128)(2,1)S(1)}, s32[1,5376]{1,0:T(1,128)S(1)}, bf16[128,5376]{1,0:T(8,128)(2,1)S(1)}) custom-call(f32[16,4352]{1,0:T(8,128)S(1)} %get-tuple-element.37.own_in, s32[1,5376]{1,0:T(1,128)S(1)} %get-tuple-element.30.slots_ref, bf16[256,5376]{1,0:T(8,128)(2,1)S(1)} %get-tuple-element.31.hots_ref, ...), custom_call_target="tpu_custom_call" | custom-call | flops 4000000000 | bytes 1000000 | tf_op jit(solution)/shard_map/off_face/pallas_call | solution.py:286
  12.7 0.0 collective-permute-done.1.near_in
  12.7 0.1 collective-permute-done.2.far_in
  12.8 0.9 %second_step.1 = (bf16[16,6144]{1,0:T(8,128)(2,1)S(1)}, bf16[16,640]{1,0:T(8,128)(2,1)S(1)}) custom-call(bf16[16,5376]{1,0:T(8,128)(2,1)S(1)} %get-tuple-element.40.inside_ref, s32[1,5376]{1,0:T(1,128)S(1)} %get-tuple-element.41.high_ref, bf16[128,5376]{1,0:T(8,128)(2,1)S(1)} %get-tuple-element.42.faces_ref, s32[1,768]{1,0:T(1,128)S(1)} %get-tuple-element.33.ghosts_ref, ...), custom_call_target="tpu_custom_call" | custom-call | flops 4000000000 | bytes 1000000 | tf_op jit(solution)/shard_map/second_step/pallas_call | solution.py:286
  13.7 0.1 collective-permute-start.3
  13.7 2.0 %second_sums.1.own_in = f32[16,4352]{1,0:T(8,128)S(1)} custom-call(f32[16,4352]{1,0:T(8,128)S(1)} %get-tuple-element.28.psi_ref, s32[1,5376]{1,0:T(1,128)S(1)} %get-tuple-element.30.slots_ref, bf16[256,5376]{1,0:T(8,128)(2,1)S(1)} %get-tuple-element.31.hots_ref, bf16[12,512,512]{2,1,0:T(8,128)(2,1)S(1)} %copy-done, s32[1,640]{1,0:T(1,128)S(1)} %get-tuple-element.32.face_ref, ...), custom_call_target="tpu_custom_call" | custom-call | flops 4000000000 | bytes 8000000 | tf_op jit(solution)/shard_map/second_sums/pallas_call | solution.py:286
  15.7 2.1 %collective-permute-done.3.below_in = bf16[16,640]{1,0:T(8,128)(2,1)S(1)} collective-permute-done((bf16[16,640]{1,0:T(8,128)(2,1)S(1)}, bf16[16,640]{1,0:T(8,128)(2,1)S(1)}, u32[]{:S(2)}, u32[]{:S(2)}) %collective-permute-start.3) | collective-permute-done | bytes 20512 | tf_op jit(solution)/shard_map/ppermute | solution.py:300
  17.8 0.3 last_faces.1
  18.1 3.7 %collective-permute-start.6 = (bf16[16,4224]{1,0:T(8,128)(2,1)S(1)}, bf16[16,4224]{1,0:T(8,128)(2,1)S(1)}, u32[]{:S(2)}, u32[]{:S(2)}) collective-permute-start(bf16[16,4224]{1,0:T(8,128)(2,1)S(1)} %get-tuple-element.48), channel_id=1, source_target_pairs={{0,3},{1,2},{2,1},{3,0},{4,7},{5,6},{6,5},{7,4},{8,11},{9,10},{10,... | collective-permute-start | bytes 405512 | tf_op jit(solution)/shard_map/ppermute | solution.py:310
  21.8 0.0 collective-permute-start.5
  21.8 0.8 %collective-permute-start.4 = (bf16[16,4224]{1,0:T(8,128)(2,1)S(1)}, bf16[16,4224]{1,0:T(8,128)(2,1)S(1)}, u32[]{:S(2)}, u32[]{:S(2)}) collective-permute-start(bf16[16,4224]{1,0:T(8,128)(2,1)S(1)} %get-tuple-element.48), channel_id=1, source_target_pairs={{0,1},{1,0},{2,3},{3,2},{4,5},{5,4},{6,7},{7,6},{8,9},{9,8},{10,11... | collective-permute-start | bytes 405512 | tf_op jit(solution)/shard_map/ppermute | solution.py:310
  22.6 3.9 %collective-permute-done.6.refs_3_ = bf16[16,4224]{1,0:T(8,128)(2,1)S(1)} collective-permute-done((bf16[16,4224]{1,0:T(8,128)(2,1)S(1)}, bf16[16,4224]{1,0:T(8,128)(2,1)S(1)}, u32[]{:S(2)}, u32[]{:S(2)}) %collective-permute-start.6) | collective-permute-done | bytes 135200 | tf_op jit(solution)/shard_map/ppermute | solution.py:310
  26.5 5.5 %collective-permute-done.5.refs_2_ = bf16[16,4224]{1,0:T(8,128)(2,1)S(1)} collective-permute-done((bf16[16,4224]{1,0:T(8,128)(2,1)S(1)}, bf16[16,4224]{1,0:T(8,128)(2,1)S(1)}, u32[]{:S(2)}, u32[]{:S(2)}) %collective-permute-start.5) | collective-permute-done | bytes 135200 | tf_op jit(solution)/shard_map/ppermute | solution.py:310
  32.1 0.0 collective-permute-done.4.refs_1_
  32.1 0.6 %gram.1 = (bf16[80,4352]{1,0:T(8,128)(2,1)S(1)}, f32[32,128]{1,0:T(8,128)S(1)}) custom-call(f32[16,4352]{1,0:T(8,128)S(1)} %get-tuple-element.47.refs_0_, bf16[16,4224]{1,0:T(8,128)(2,1)S(1)} %collective-permute-done.4.refs_1_, bf16[16,4224]{1,0:T(8,128)(2,1)S(1)} %collective-permute-done.5.refs_2_, bf16[16,4224]{1,0:T(8,128)(2,1)S(1)} %collective-permute-done.6.refs_3_), custom_call_target="tpu_custom_call" | custom-call | tf_op jit(solution)/shard_map/gram/pallas_call | solution.py:286
  32.7 0.0 collective-permute-start.7
  32.7 1.2 %collective-permute-done.7 = f32[32,128]{1,0:T(8,128)S(1)} collective-permute-done((f32[32,128]{1,0:T(8,128)S(1)}, f32[32,128]{1,0:T(8,128)S(1)}, u32[]{:S(2)}, u32[]{:S(2)}) %collective-permute-start.7) | collective-permute-done | bytes 16416 | tf_op jit(solution)/shard_map/gram_sum/ppermute | solution.py:464
  33.9 2.3 %collective-permute-start.10 = (f32[32,128]{1,0:T(8,128)S(1)}, f32[32,128]{1,0:T(8,128)S(1)}, u32[]{:S(2)}, u32[]{:S(2)}) collective-permute-start(f32[32,128]{1,0:T(8,128)S(1)} %add.12), channel_id=1, source_target_pairs={{0,24},{4,28},{8,16},{12,20},{16,8},{20,12},{24,0},{28,4},{1,25},{... | collective-permute-start | bytes 49160 | tf_op jit(solution)/shard_map/gram_sum/ppermute | solution.py:464
  36.2 0.7 %collective-permute-start.9 = (f32[32,128]{1,0:T(8,128)S(1)}, f32[32,128]{1,0:T(8,128)S(1)}, u32[]{:S(2)}, u32[]{:S(2)}) collective-permute-start(f32[32,128]{1,0:T(8,128)S(1)} %add.12), channel_id=1, source_target_pairs={{0,16},{4,20},{8,24},{12,28},{16,0},{20,4},{24,8},{28,12},{1,17},{... | collective-permute-start | bytes 49160 | tf_op jit(solution)/shard_map/gram_sum/ppermute | solution.py:464
  36.8 0.5 %collective-permute-start.8 = (f32[32,128]{1,0:T(8,128)S(1)}, f32[32,128]{1,0:T(8,128)S(1)}, u32[]{:S(2)}, u32[]{:S(2)}) collective-permute-start(f32[32,128]{1,0:T(8,128)S(1)} %add.12), channel_id=1, source_target_pairs={{0,8},{4,12},{8,0},{12,4},{16,24},{20,28},{24,16},{28,20},{1,9},{5... | collective-permute-start | bytes 49160 | tf_op jit(solution)/shard_map/gram_sum/ppermute | solution.py:464
  37.4 1.1 %collective-permute-done.10 = f32[32,128]{1,0:T(8,128)S(1)} collective-permute-done((f32[32,128]{1,0:T(8,128)S(1)}, f32[32,128]{1,0:T(8,128)S(1)}, u32[]{:S(2)}, u32[]{:S(2)}) %collective-permute-start.10) | collective-permute-done | bytes 16416 | tf_op jit(solution)/shard_map/gram_sum/ppermute | solution.py:464
  38.5 1.4 %collective-permute-done.9 = f32[32,128]{1,0:T(8,128)S(1)} collective-permute-done((f32[32,128]{1,0:T(8,128)S(1)}, f32[32,128]{1,0:T(8,128)S(1)}, u32[]{:S(2)}, u32[]{:S(2)}) %collective-permute-start.9) | collective-permute-done | bytes 16416 | tf_op jit(solution)/shard_map/gram_sum/ppermute | solution.py:464
  39.9 0.7 %collective-permute-done.8 = f32[32,128]{1,0:T(8,128)S(1)} collective-permute-done((f32[32,128]{1,0:T(8,128)S(1)}, f32[32,128]{1,0:T(8,128)S(1)}, u32[]{:S(2)}, u32[]{:S(2)}) %collective-permute-start.8) | collective-permute-done | bytes 16416 | tf_op jit(solution)/shard_map/gram_sum/ppermute | solution.py:464
  40.6 2.6 %orthonormal.1 = f32[16,4116]{1,0:T(8,128)} custom-call(f32[32,128]{1,0:T(8,128)S(1)} %add_add_fusion.gram_ref, bf16[80,4352]{1,0:T(8,128)(2,1)S(1)} %get-tuple-element.50.terms_ref), custom_call_target="tpu_custom_call" | custom-call | tf_op jit(solution)/shard_map/orthonormal/pallas_call | solution.py:286
  (2 shorter events, 0.0 us)
Async XLA Ops:
  0.0 5.9 %copy-start = (bf16[12,512,512]{2,1,0:T(8,128)(2,1)S(1)}, bf16[12,512,512]{2,1,0:T(8,128)(2,1)}, u32[]{:S(2)}) copy-start(bf16[12,512,512]{2,1,0:T(8,128)(2,1)} %ham_ref.7) | copy-start | bytes 18874372
  1.4 5.3 %collective-permute-start = (bf16[16,640]{1,0:T(8,128)(2,1)S(1)}, bf16[16,640]{1,0:T(8,128)(2,1)S(1)}, u32[]{:S(2)}, u32[]{:S(2)}) collective-permute-start(bf16[16,640]{1,0:T(8,128)(2,1)S(1)} %get-tuple-element.35), channel_id=1, source_target_pairs={{4,0},{8,4},{12,8},{16,12},{20,16},{24,20},{28,24},{0,28},{5,1},{9... | collective-permute-start | bytes 61448 | tf_op jit(solution)/shard_map/ppermute | solution.py:300
  8.5 4.2 %collective-permute-start.1 = (bf16[16,640]{1,0:T(8,128)(2,1)S(1)}, bf16[16,640]{1,0:T(8,128)(2,1)S(1)}, u32[]{:S(2)}, u32[]{:S(2)}) collective-permute-start(bf16[16,640]{1,0:T(8,128)(2,1)S(1)} %get-tuple-element.38), channel_id=1, source_target_pairs={{0,4},{4,0},{8,12},{12,8},{16,20},{20,16},{24,28},{28,24},{1,5},{5... | collective-permute-start | bytes 61448 | tf_op jit(solution)/shard_map/ppermute | solution.py:360
  8.6 4.2 %collective-permute-start.2 = (bf16[16,640]{1,0:T(8,128)(2,1)S(1)}, bf16[16,640]{1,0:T(8,128)(2,1)S(1)}, u32[]{:S(2)}, u32[]{:S(2)}) collective-permute-start(bf16[16,640]{1,0:T(8,128)(2,1)S(1)} %get-tuple-element.39), channel_id=1, source_target_pairs={{0,28},{4,8},{8,4},{12,16},{16,12},{20,24},{24,20},{28,0},{1,29},{... | collective-permute-start | bytes 61448 | tf_op jit(solution)/shard_map/ppermute | solution.py:359
  13.7 4.2 %collective-permute-start.3 = (bf16[16,640]{1,0:T(8,128)(2,1)S(1)}, bf16[16,640]{1,0:T(8,128)(2,1)S(1)}, u32[]{:S(2)}, u32[]{:S(2)}) collective-permute-start(bf16[16,640]{1,0:T(8,128)(2,1)S(1)} %get-tuple-element.46), channel_id=1, source_target_pairs={{28,0},{0,4},{4,8},{8,12},{12,16},{16,20},{20,24},{24,28},{29,1},{... | collective-permute-start | bytes 61448 | tf_op jit(solution)/shard_map/ppermute | solution.py:300
  18.1 8.4 %collective-permute-start.6 = (bf16[16,4224]{1,0:T(8,128)(2,1)S(1)}, bf16[16,4224]{1,0:T(8,128)(2,1)S(1)}, u32[]{:S(2)}, u32[]{:S(2)}) collective-permute-start(bf16[16,4224]{1,0:T(8,128)(2,1)S(1)} %get-tuple-element.48), channel_id=1, source_target_pairs={{0,3},{1,2},{2,1},{3,0},{4,7},{5,6},{6,5},{7,4},{8,11},{9,10},{10,... | collective-permute-start | bytes 405512 | tf_op jit(solution)/shard_map/ppermute | solution.py:310
  21.8 10.2 %collective-permute-start.5 = (bf16[16,4224]{1,0:T(8,128)(2,1)S(1)}, bf16[16,4224]{1,0:T(8,128)(2,1)S(1)}, u32[]{:S(2)}, u32[]{:S(2)}) collective-permute-start(bf16[16,4224]{1,0:T(8,128)(2,1)S(1)} %get-tuple-element.48), channel_id=1, source_target_pairs={{0,2},{1,3},{2,0},{3,1},{4,6},{5,7},{6,4},{7,5},{8,10},{9,11},{10,... | collective-permute-start | bytes 405512 | tf_op jit(solution)/shard_map/ppermute | solution.py:310
  21.8 10.2 %collective-permute-start.4 = (bf16[16,4224]{1,0:T(8,128)(2,1)S(1)}, bf16[16,4224]{1,0:T(8,128)(2,1)S(1)}, u32[]{:S(2)}, u32[]{:S(2)}) collective-permute-start(bf16[16,4224]{1,0:T(8,128)(2,1)S(1)} %get-tuple-element.48), channel_id=1, source_target_pairs={{0,1},{1,0},{2,3},{3,2},{4,5},{5,4},{6,7},{7,6},{8,9},{9,8},{10,11... | collective-permute-start | bytes 405512 | tf_op jit(solution)/shard_map/ppermute | solution.py:310
  32.7 1.2 %collective-permute-start.7 = (f32[32,128]{1,0:T(8,128)S(1)}, f32[32,128]{1,0:T(8,128)S(1)}, u32[]{:S(2)}, u32[]{:S(2)}) collective-permute-start(f32[32,128]{1,0:T(8,128)S(1)} %get-tuple-element.49), channel_id=1, source_target_pairs={{0,4},{4,0},{8,12},{12,8},{16,20},{20,16},{24,28},{28,24},{1,5},{5... | collective-permute-start | bytes 49160 | tf_op jit(solution)/shard_map/gram_sum/ppermute | solution.py:464
  33.9 4.6 %collective-permute-start.10 = (f32[32,128]{1,0:T(8,128)S(1)}, f32[32,128]{1,0:T(8,128)S(1)}, u32[]{:S(2)}, u32[]{:S(2)}) collective-permute-start(f32[32,128]{1,0:T(8,128)S(1)} %add.12), channel_id=1, source_target_pairs={{0,24},{4,28},{8,16},{12,20},{16,8},{20,12},{24,0},{28,4},{1,25},{... | collective-permute-start | bytes 49160 | tf_op jit(solution)/shard_map/gram_sum/ppermute | solution.py:464
  36.2 3.7 %collective-permute-start.9 = (f32[32,128]{1,0:T(8,128)S(1)}, f32[32,128]{1,0:T(8,128)S(1)}, u32[]{:S(2)}, u32[]{:S(2)}) collective-permute-start(f32[32,128]{1,0:T(8,128)S(1)} %add.12), channel_id=1, source_target_pairs={{0,16},{4,20},{8,24},{12,28},{16,0},{20,4},{24,8},{28,12},{1,17},{... | collective-permute-start | bytes 49160 | tf_op jit(solution)/shard_map/gram_sum/ppermute | solution.py:464
  36.8 3.7 %collective-permute-start.8 = (f32[32,128]{1,0:T(8,128)S(1)}, f32[32,128]{1,0:T(8,128)S(1)}, u32[]{:S(2)}, u32[]{:S(2)}) collective-permute-start(f32[32,128]{1,0:T(8,128)S(1)} %add.12), channel_id=1, source_target_pairs={{0,8},{4,12},{8,0},{12,4},{16,24},{20,28},{24,16},{28,20},{1,9},{5... | collective-permute-start | bytes 49160 | tf_op jit(solution)/shard_map/gram_sum/ppermute | solution.py:464

commit v12 on v11

--- a/solution.py
+++ b/solution.py
@@ -85,7 +85,10 @@
 
 
 def spread_once(values, high, blocks):
-    return jnp.concatenate([jnp.where(high == i, values, 0.0).astype(BF16) for i in range(blocks)], axis=0)
+    values = values.astype(BF16)
+    high = jnp.broadcast_to(high, values.shape).astype(jnp.int16)
+    zero = jnp.zeros_like(values)
+    return jnp.concatenate([jnp.where(high == jnp.int16(i), values, zero) for i in range(blocks)], axis=0)
 
 
 def scatter_sum(values_ref, high, hots_ref, blocks, once=False):

time: 43.3 us -> 43.3 us (level)
  no operation moved by 1% of the time
where the time goes in v12:
time: 43.3 us; the launch traced here: 43.2 us
  waiting for transfers between devices  16.1 us (37%)
  starting transfers between devices  13.8 us (32%)
  Pallas kernels  13.2 us (30%)
    pallas_call x10, Pallas kernels, call(): pl.pallas_call(kernel, out_shape=out_shape, in_specs=[HBM if i in far els...  13.2 us
    ppermute x3, waiting for transfers between devices, partner(): return lax.ppermute(block, axis, [(i, i ^ distance) for i in range(size)])  9.47 us
    ppermute x3, starting transfers between devices, partner(): return lax.ppermute(block, axis, [(i, i ^ distance) for i in range(size)])  4.45 us
    ppermute x4, waiting for transfers between devices, space_sum(): lax.ppermute(block, 'space', [(i, i ^ step * k) for i in range(size)])  4.4 us
    ppermute x4, starting transfers between devices, space_sum(): lax.ppermute(block, 'space', [(i, i ^ step * k) for i in range(size)])  3.51 us
    ppermute x2, starting transfers between devices, from_behind(): return lax.ppermute(block, axis, route)  3.44 us
    ppermute x1, starting transfers between devices, filter_field(): lax.ppermute(to_far, 'space', [(i, ((i + 1 ^ 1) - 1) % domains) for i in...  2.27 us
    ppermute x2, waiting for transfers between devices, from_behind(): return lax.ppermute(block, axis, route)  2.07 us
  transfers between devices with their start and end apart: 11, of which 8 were waited for; matrix products, arithmetic and copies ran while one was open for 0% of the time, Pallas kernels for 13%

profile of v12, /device:TPU:0, one launch (start us, length us, event | category | flops | bytes accessed | tf_op | source)
XLA Modules:
  0.0 43.2 jit_solution(2455284643214810028)
XLA Ops:
  0.0 0.0 copy-start
  0.0 1.4 %face_values.1 = (bf16[16,640]{1,0:T(8,128)(2,1)S(1)}, f32[16,4352]{1,0:T(8,128)S(1)}, s32[12,512]{1,0:T(8,128)S(1)}, s32[1,640]{1,0:T(1,128)S(1)}) custom-call(f32[16,4116]{1,0:T(8,128)} %psi_hbm.1, s32[12,512]{1,0:T(8,128)} %conn_hbm.1, s32[588]{0:T(1024)} %face_hbm.1), custom_call_target="tpu_custom_call" | custom-call | flops 20000000000 | bytes 40000000 | tf_op jit(solution)/shard_map/face_values/pallas_call | solution.py:289
  1.4 3.4 %collective-permute-start = (bf16[16,640]{1,0:T(8,128)(2,1)S(1)}, bf16[16,640]{1,0:T(8,128)(2,1)S(1)}, u32[]{:S(2)}, u32[]{:S(2)}) collective-permute-start(bf16[16,640]{1,0:T(8,128)(2,1)S(1)} %get-tuple-element.35), channel_id=1, source_target_pairs={{4,0},{8,4},{12,8},{16,12},{20,16},{24,20},{28,24},{0,28},{5,1},{9... | collective-permute-start | bytes 61448 | tf_op jit(solution)/shard_map/ppermute | solution.py:303
  4.8 1.0 %near_values.1 = (bf16[16,5376]{1,0:T(8,128)(2,1)S(1)}, s32[1,5376]{1,0:T(1,128)S(1)}, s32[1,768]{1,0:T(1,128)S(1)}, bf16[256,5376]{1,0:T(8,128)(2,1)S(1)}, bf16[256,768]{1,0:T(8,128)(2,1)S(1)}) custom-call(f32[16,4352]{1,0:T(8,128)S(1)} %get-tuple-element.28.psi_ref, s32[12,512]{1,0:T(8,128)S(1)} %get-tuple-element.29.conn_ref), custom_call_target="tpu_custom_call" | custom-call | tf_op jit(solution)/shard_map/near_values/pallas_call | solution.py:289
  5.9 0.0 copy-done
  5.9 0.8 %interior.1.part_ref = f32[16,6144]{1,0:T(8,128)S(1)} custom-call(bf16[16,5376]{1,0:T(8,128)(2,1)S(1)} %get-tuple-element.36.inside_ref, bf16[12,512,512]{2,1,0:T(8,128)(2,1)S(1)} %copy-done), custom_call_target="tpu_custom_call" | custom-call | flops 4000000000 | bytes 8000000 | tf_op jit(solution)/shard_map/interior/pallas_call | solution.py:289
  6.7 0.0 collective-permute-done.ghost_ref
  6.7 1.8 %first_step.1 = (f32[16,4352]{1,0:T(8,128)S(1)}, f32[16,640]{1,0:T(8,128)S(1)}, bf16[16,640]{1,0:T(8,128)(2,1)S(1)}, bf16[16,640]{1,0:T(8,128)(2,1)S(1)}) custom-call(f32[16,4352]{1,0:T(8,128)S(1)} %get-tuple-element.28.psi_ref, s32[1,5376]{1,0:T(1,128)S(1)} %get-tuple-element.30.slots_ref, s32[1,768]{1,0:T(1,128)S(1)} %get-tuple-element.33.ghosts_ref, ...), custom_call_target="tpu_custom_call" | custom-call | flops 4000000000 | bytes 1000000 | tf_op jit(solution)/shard_map/first_step/pallas_call | solution.py:289
  8.5 0.1 collective-permute-start.1
  8.6 2.3 %collective-permute-start.2 = (bf16[16,640]{1,0:T(8,128)(2,1)S(1)}, bf16[16,640]{1,0:T(8,128)(2,1)S(1)}, u32[]{:S(2)}, u32[]{:S(2)}) collective-permute-start(bf16[16,640]{1,0:T(8,128)(2,1)S(1)} %get-tuple-element.39), channel_id=1, source_target_pairs={{0,28},{4,8},{8,4},{12,16},{16,12},{20,24},{24,20},{28,0},{1,29},{... | collective-permute-start | bytes 61448 | tf_op jit(solution)/shard_map/ppermute | solution.py:362
  10.8 1.8 %off_face.1 = (f32[16,640]{1,0:T(8,128)S(1)}, bf16[16,5376]{1,0:T(8,128)(2,1)S(1)}, s32[1,5376]{1,0:T(1,128)S(1)}, bf16[128,5376]{1,0:T(8,128)(2,1)S(1)}) custom-call(f32[16,4352]{1,0:T(8,128)S(1)} %get-tuple-element.37.own_in, s32[1,5376]{1,0:T(1,128)S(1)} %get-tuple-element.30.slots_ref, bf16[256,5376]{1,0:T(8,128)(2,1)S(1)} %get-tuple-element.31.hots_ref, ...), custom_call_target="tpu_custom_call" | custom-call | flops 4000000000 | bytes 1000000 | tf_op jit(solution)/shard_map/off_face/pallas_call | solution.py:289
  12.7 0.0 collective-permute-done.1.near_in
  12.7 0.1 collective-permute-done.2.far_in
  12.8 0.9 %second_step.1 = (bf16[16,6144]{1,0:T(8,128)(2,1)S(1)}, bf16[16,640]{1,0:T(8,128)(2,1)S(1)}) custom-call(bf16[16,5376]{1,0:T(8,128)(2,1)S(1)} %get-tuple-element.40.inside_ref, s32[1,5376]{1,0:T(1,128)S(1)} %get-tuple-element.41.high_ref, bf16[128,5376]{1,0:T(8,128)(2,1)S(1)} %get-tuple-element.42.faces_ref, s32[1,768]{1,0:T(1,128)S(1)} %get-tuple-element.33.ghosts_ref, ...), custom_call_target="tpu_custom_call" | custom-call | flops 4000000000 | bytes 1000000 | tf_op jit(solution)/shard_map/second_step/pallas_call | solution.py:289
  13.6 0.1 collective-permute-start.3
  13.7 2.0 %second_sums.1.own_in = f32[16,4352]{1,0:T(8,128)S(1)} custom-call(f32[16,4352]{1,0:T(8,128)S(1)} %get-tuple-element.28.psi_ref, s32[1,5376]{1,0:T(1,128)S(1)} %get-tuple-element.30.slots_ref, bf16[256,5376]{1,0:T(8,128)(2,1)S(1)} %get-tuple-element.31.hots_ref, bf16[12,512,512]{2,1,0:T(8,128)(2,1)S(1)} %copy-done, s32[1,640]{1,0:T(1,128)S(1)} %get-tuple-element.32.face_ref, ...), custom_call_target="tpu_custom_call" | custom-call | flops 4000000000 | bytes 8000000 | tf_op jit(solution)/shard_map/second_sums/pallas_call | solution.py:289
  15.7 2.1 %collective-permute-done.3.below_in = bf16[16,640]{1,0:T(8,128)(2,1)S(1)} collective-permute-done((bf16[16,640]{1,0:T(8,128)(2,1)S(1)}, bf16[16,640]{1,0:T(8,128)(2,1)S(1)}, u32[]{:S(2)}, u32[]{:S(2)}) %collective-permute-start.3) | collective-permute-done | bytes 20512 | tf_op jit(solution)/shard_map/ppermute | solution.py:303
  17.8 0.3 last_faces.1
  18.1 3.7 %collective-permute-start.6 = (bf16[16,4224]{1,0:T(8,128)(2,1)S(1)}, bf16[16,4224]{1,0:T(8,128)(2,1)S(1)}, u32[]{:S(2)}, u32[]{:S(2)}) collective-permute-start(bf16[16,4224]{1,0:T(8,128)(2,1)S(1)} %get-tuple-element.48), channel_id=1, source_target_pairs={{0,3},{1,2},{2,1},{3,0},{4,7},{5,6},{6,5},{7,4},{8,11},{9,10},{10,... | collective-permute-start | bytes 405512 | tf_op jit(solution)/shard_map/ppermute | solution.py:313
  21.8 0.0 collective-permute-start.5
  21.8 0.8 %collective-permute-start.4 = (bf16[16,4224]{1,0:T(8,128)(2,1)S(1)}, bf16[16,4224]{1,0:T(8,128)(2,1)S(1)}, u32[]{:S(2)}, u32[]{:S(2)}) collective-permute-start(bf16[16,4224]{1,0:T(8,128)(2,1)S(1)} %get-tuple-element.48), channel_id=1, source_target_pairs={{0,1},{1,0},{2,3},{3,2},{4,5},{5,4},{6,7},{7,6},{8,9},{9,8},{10,11... | collective-permute-start | bytes 405512 | tf_op jit(solution)/shard_map/ppermute | solution.py:313
  22.6 3.9 %collective-permute-done.6.refs_3_ = bf16[16,4224]{1,0:T(8,128)(2,1)S(1)} collective-permute-done((bf16[16,4224]{1,0:T(8,128)(2,1)S(1)}, bf16[16,4224]{1,0:T(8,128)(2,1)S(1)}, u32[]{:S(2)}, u32[]{:S(2)}) %collective-permute-start.6) | collective-permute-done | bytes 135200 | tf_op jit(solution)/shard_map/ppermute | solution.py:313
  26.5 5.5 %collective-permute-done.5.refs_2_ = bf16[16,4224]{1,0:T(8,128)(2,1)S(1)} collective-permute-done((bf16[16,4224]{1,0:T(8,128)(2,1)S(1)}, bf16[16,4224]{1,0:T(8,128)(2,1)S(1)}, u32[]{:S(2)}, u32[]{:S(2)}) %collective-permute-start.5) | collective-permute-done | bytes 135200 | tf_op jit(solution)/shard_map/ppermute | solution.py:313
  32.1 0.0 collective-permute-done.4.refs_1_
  32.1 0.6 %gram.1 = (bf16[80,4352]{1,0:T(8,128)(2,1)S(1)}, f32[32,128]{1,0:T(8,128)S(1)}) custom-call(f32[16,4352]{1,0:T(8,128)S(1)} %get-tuple-element.47.refs_0_, bf16[16,4224]{1,0:T(8,128)(2,1)S(1)} %collective-permute-done.4.refs_1_, bf16[16,4224]{1,0:T(8,128)(2,1)S(1)} %collective-permute-done.5.refs_2_, bf16[16,4224]{1,0:T(8,128)(2,1)S(1)} %collective-permute-done.6.refs_3_), custom_call_target="tpu_custom_call" | custom-call | tf_op jit(solution)/shard_map/gram/pallas_call | solution.py:289
  32.6 0.0 collective-permute-start.7
  32.7 1.2 %collective-permute-done.7 = f32[32,128]{1,0:T(8,128)S(1)} collective-permute-done((f32[32,128]{1,0:T(8,128)S(1)}, f32[32,128]{1,0:T(8,128)S(1)}, u32[]{:S(2)}, u32[]{:S(2)}) %collective-permute-start.7) | collective-permute-done | bytes 16416 | tf_op jit(solution)/shard_map/gram_sum/ppermute | solution.py:467
  33.8 2.3 %collective-permute-start.10 = (f32[32,128]{1,0:T(8,128)S(1)}, f32[32,128]{1,0:T(8,128)S(1)}, u32[]{:S(2)}, u32[]{:S(2)}) collective-permute-start(f32[32,128]{1,0:T(8,128)S(1)} %add.12), channel_id=1, source_target_pairs={{0,24},{4,28},{8,16},{12,20},{16,8},{20,12},{24,0},{28,4},{1,25},{... | collective-permute-start | bytes 49160 | tf_op jit(solution)/shard_map/gram_sum/ppermute | solution.py:467
  36.2 0.7 %collective-permute-start.9 = (f32[32,128]{1,0:T(8,128)S(1)}, f32[32,128]{1,0:T(8,128)S(1)}, u32[]{:S(2)}, u32[]{:S(2)}) collective-permute-start(f32[32,128]{1,0:T(8,128)S(1)} %add.12), channel_id=1, source_target_pairs={{0,16},{4,20},{8,24},{12,28},{16,0},{20,4},{24,8},{28,12},{1,17},{... | collective-permute-start | bytes 49160 | tf_op jit(solution)/shard_map/gram_sum/ppermute | solution.py:467
  36.8 0.5 %collective-permute-start.8 = (f32[32,128]{1,0:T(8,128)S(1)}, f32[32,128]{1,0:T(8,128)S(1)}, u32[]{:S(2)}, u32[]{:S(2)}) collective-permute-start(f32[32,128]{1,0:T(8,128)S(1)} %add.12), channel_id=1, source_target_pairs={{0,8},{4,12},{8,0},{12,4},{16,24},{20,28},{24,16},{28,20},{1,9},{5... | collective-permute-start | bytes 49160 | tf_op jit(solution)/shard_map/gram_sum/ppermute | solution.py:467
  37.3 1.1 %collective-permute-done.10 = f32[32,128]{1,0:T(8,128)S(1)} collective-permute-done((f32[32,128]{1,0:T(8,128)S(1)}, f32[32,128]{1,0:T(8,128)S(1)}, u32[]{:S(2)}, u32[]{:S(2)}) %collective-permute-start.10) | collective-permute-done | bytes 16416 | tf_op jit(solution)/shard_map/gram_sum/ppermute | solution.py:467
  38.5 1.4 %collective-permute-done.9 = f32[32,128]{1,0:T(8,128)S(1)} collective-permute-done((f32[32,128]{1,0:T(8,128)S(1)}, f32[32,128]{1,0:T(8,128)S(1)}, u32[]{:S(2)}, u32[]{:S(2)}) %collective-permute-start.9) | collective-permute-done | bytes 16416 | tf_op jit(solution)/shard_map/gram_sum/ppermute | solution.py:467
  39.9 0.7 %collective-permute-done.8 = f32[32,128]{1,0:T(8,128)S(1)} collective-permute-done((f32[32,128]{1,0:T(8,128)S(1)}, f32[32,128]{1,0:T(8,128)S(1)}, u32[]{:S(2)}, u32[]{:S(2)}) %collective-permute-start.8) | collective-permute-done | bytes 16416 | tf_op jit(solution)/shard_map/gram_sum/ppermute | solution.py:467
  40.6 2.6 %orthonormal.1 = f32[16,4116]{1,0:T(8,128)} custom-call(f32[32,128]{1,0:T(8,128)S(1)} %add_add_fusion.gram_ref, bf16[80,4352]{1,0:T(8,128)(2,1)S(1)} %get-tuple-element.50.terms_ref), custom_call_target="tpu_custom_call" | custom-call | tf_op jit(solution)/shard_map/orthonormal/pallas_call | solution.py:289
  (2 shorter events, 0.0 us)
Async XLA Ops:
  0.0 5.9 %copy-start = (bf16[12,512,512]{2,1,0:T(8,128)(2,1)S(1)}, bf16[12,512,512]{2,1,0:T(8,128)(2,1)}, u32[]{:S(2)}) copy-start(bf16[12,512,512]{2,1,0:T(8,128)(2,1)} %ham_ref.7) | copy-start | bytes 18874372
  1.4 5.3 %collective-permute-start = (bf16[16,640]{1,0:T(8,128)(2,1)S(1)}, bf16[16,640]{1,0:T(8,128)(2,1)S(1)}, u32[]{:S(2)}, u32[]{:S(2)}) collective-permute-start(bf16[16,640]{1,0:T(8,128)(2,1)S(1)} %get-tuple-element.35), channel_id=1, source_target_pairs={{4,0},{8,4},{12,8},{16,12},{20,16},{24,20},{28,24},{0,28},{5,1},{9... | collective-permute-start | bytes 61448 | tf_op jit(solution)/shard_map/ppermute | solution.py:303
  8.5 4.2 %collective-permute-start.1 = (bf16[16,640]{1,0:T(8,128)(2,1)S(1)}, bf16[16,640]{1,0:T(8,128)(2,1)S(1)}, u32[]{:S(2)}, u32[]{:S(2)}) collective-permute-start(bf16[16,640]{1,0:T(8,128)(2,1)S(1)} %get-tuple-element.38), channel_id=1, source_target_pairs={{0,4},{4,0},{8,12},{12,8},{16,20},{20,16},{24,28},{28,24},{1,5},{5... | collective-permute-start | bytes 61448 | tf_op jit(solution)/shard_map/ppermute | solution.py:363
  8.6 4.2 %collective-permute-start.2 = (bf16[16,640]{1,0:T(8,128)(2,1)S(1)}, bf16[16,640]{1,0:T(8,128)(2,1)S(1)}, u32[]{:S(2)}, u32[]{:S(2)}) collective-permute-start(bf16[16,640]{1,0:T(8,128)(2,1)S(1)} %get-tuple-element.39), channel_id=1, source_target_pairs={{0,28},{4,8},{8,4},{12,16},{16,12},{20,24},{24,20},{28,0},{1,29},{... | collective-permute-start | bytes 61448 | tf_op jit(solution)/shard_map/ppermute | solution.py:362
  13.6 4.2 %collective-permute-start.3 = (bf16[16,640]{1,0:T(8,128)(2,1)S(1)}, bf16[16,640]{1,0:T(8,128)(2,1)S(1)}, u32[]{:S(2)}, u32[]{:S(2)}) collective-permute-start(bf16[16,640]{1,0:T(8,128)(2,1)S(1)} %get-tuple-element.46), channel_id=1, source_target_pairs={{28,0},{0,4},{4,8},{8,12},{12,16},{16,20},{20,24},{24,28},{29,1},{... | collective-permute-start | bytes 61448 | tf_op jit(solution)/shard_map/ppermute | solution.py:303
  18.1 8.4 %collective-permute-start.6 = (bf16[16,4224]{1,0:T(8,128)(2,1)S(1)}, bf16[16,4224]{1,0:T(8,128)(2,1)S(1)}, u32[]{:S(2)}, u32[]{:S(2)}) collective-permute-start(bf16[16,4224]{1,0:T(8,128)(2,1)S(1)} %get-tuple-element.48), channel_id=1, source_target_pairs={{0,3},{1,2},{2,1},{3,0},{4,7},{5,6},{6,5},{7,4},{8,11},{9,10},{10,... | collective-permute-start | bytes 405512 | tf_op jit(solution)/shard_map/ppermute | solution.py:313
  21.8 10.2 %collective-permute-start.5 = (bf16[16,4224]{1,0:T(8,128)(2,1)S(1)}, bf16[16,4224]{1,0:T(8,128)(2,1)S(1)}, u32[]{:S(2)}, u32[]{:S(2)}) collective-permute-start(bf16[16,4224]{1,0:T(8,128)(2,1)S(1)} %get-tuple-element.48), channel_id=1, source_target_pairs={{0,2},{1,3},{2,0},{3,1},{4,6},{5,7},{6,4},{7,5},{8,10},{9,11},{10,... | collective-permute-start | bytes 405512 | tf_op jit(solution)/shard_map/ppermute | solution.py:313
  21.8 10.2 %collective-permute-start.4 = (bf16[16,4224]{1,0:T(8,128)(2,1)S(1)}, bf16[16,4224]{1,0:T(8,128)(2,1)S(1)}, u32[]{:S(2)}, u32[]{:S(2)}) collective-permute-start(bf16[16,4224]{1,0:T(8,128)(2,1)S(1)} %get-tuple-element.48), channel_id=1, source_target_pairs={{0,1},{1,0},{2,3},{3,2},{4,5},{5,4},{6,7},{7,6},{8,9},{9,8},{10,11... | collective-permute-start | bytes 405512 | tf_op jit(solution)/shard_map/ppermute | solution.py:313
  32.6 1.2 %collective-permute-start.7 = (f32[32,128]{1,0:T(8,128)S(1)}, f32[32,128]{1,0:T(8,128)S(1)}, u32[]{:S(2)}, u32[]{:S(2)}) collective-permute-start(f32[32,128]{1,0:T(8,128)S(1)} %get-tuple-element.49), channel_id=1, source_target_pairs={{0,4},{4,0},{8,12},{12,8},{16,20},{20,16},{24,28},{28,24},{1,5},{5... | collective-permute-start | bytes 49160 | tf_op jit(solution)/shard_map/gram_sum/ppermute | solution.py:467
  33.8 4.6 %collective-permute-start.10 = (f32[32,128]{1,0:T(8,128)S(1)}, f32[32,128]{1,0:T(8,128)S(1)}, u32[]{:S(2)}, u32[]{:S(2)}) collective-permute-start(f32[32,128]{1,0:T(8,128)S(1)} %add.12), channel_id=1, source_target_pairs={{0,24},{4,28},{8,16},{12,20},{16,8},{20,12},{24,0},{28,4},{1,25},{... | collective-permute-start | bytes 49160 | tf_op jit(solution)/shard_map/gram_sum/ppermute | solution.py:467
  36.2 3.7 %collective-permute-start.9 = (f32[32,128]{1,0:T(8,128)S(1)}, f32[32,128]{1,0:T(8,128)S(1)}, u32[]{:S(2)}, u32[]{:S(2)}) collective-permute-start(f32[32,128]{1,0:T(8,128)S(1)} %add.12), channel_id=1, source_target_pairs={{0,16},{4,20},{8,24},{12,28},{16,0},{20,4},{24,8},{28,12},{1,17},{... | collective-permute-start | bytes 49160 | tf_op jit(solution)/shard_map/gram_sum/ppermute | solution.py:467
  36.8 3.7 %collective-permute-start.8 = (f32[32,128]{1,0:T(8,128)S(1)}, f32[32,128]{1,0:T(8,128)S(1)}, u32[]{:S(2)}, u32[]{:S(2)}) collective-permute-start(f32[32,128]{1,0:T(8,128)S(1)} %add.12), channel_id=1, source_target_pairs={{0,8},{4,12},{8,0},{12,4},{16,24},{20,28},{24,16},{28,20},{1,9},{5... | collective-permute-start | bytes 49160 | tf_op jit(solution)/shard_map/gram_sum/ppermute | solution.py:467
